TPU v7x, 32 devices: a whole 2x2x4 slice. The times are simulated.
32 devices in a mesh: aux: 4 (over y, x), occ: 8 (over z, core).
Axes of the slice: x: 2, y: 2, z: 4, core: 2. Of those that a mesh axis runs over, the one named last changes fastest.
Arguments:
- integrals: bfloat16 [8, 192, 128, 128], P('aux', 'occ'), may hold values from -2 to 2
- coefficients: bfloat16 [4096, 384], P('occ'), may hold values from -0.3125 to 0.3125
- pair_rows: int32 [4, 192], P('aux', 'occ'), may hold values from 0 to 3
- pair_cols: int32 [4, 192], P('aux', 'occ'), may hold values from 0 to 31
- pair_count: int32 [4, 8], P('aux', 'occ'), may hold values from 1 to 24, as said below
- row_blocks: int32 [32], replicated, may hold values from 0 to 31, each once
Outputs:
- exchange_matrix: float32 [4096, 4096], P('aux', 'occ')
Inputs may be any that keep to these rules, and one draw needn't show every extreme that they name: `pair_count`: at most 24 live slots for each auxiliary block and row owner, and some auxiliary block and owner has exactly 24.
All inputs are finite; a program needn't handle non-finite values.
Results may differ from a plain program's by a relative error of at most 0.0022.
Values may be sent and summed in bfloat16 or wider, within the bound.
No kernel may reach another device: no remote copies, remote signals or barrier semaphores. Data moves between devices by JAX's collectives and lax.ppermute only.
A program may use at most 64 MiB of HBM per device.

v0:
```python
import jax
import jax.numpy as jnp
from jax import lax
from jax.sharding import PartitionSpec as P


def contract_rows(first, second):
    return jnp.einsum("pni,pmi->nm", first, second, preferred_element_type=jnp.float32)


def local(integrals, coefficients, pair_rows, pair_cols, pair_count, row_blocks):
    aux_count = integrals.shape[0]
    block_size = integrals.shape[2]
    block_total = row_blocks.shape[0]
    occ_size = lax.axis_size("occ")
    own_blocks = block_total // occ_size
    strip_width = own_blocks * block_size
    full_coeff = lax.all_gather(coefficients, "occ", axis=0, tiled=True)
    orbitals = full_coeff.shape[1]
    coeff_blocks = full_coeff.reshape(block_total, block_size, orbitals)

    def add_pair(slot_index, partial_half):
        row_slot = pair_rows[0, slot_index]
        basis_block = row_blocks[pair_cols[0, slot_index]]
        coeff_piece = lax.dynamic_index_in_dim(coeff_blocks, basis_block, 0, keepdims=False)
        integral_piece = lax.dynamic_index_in_dim(integrals, slot_index, 1, keepdims=False)
        product = jnp.einsum(
            "pmn,ni->pmi", integral_piece, coeff_piece, preferred_element_type=jnp.float32
        )
        current = lax.dynamic_index_in_dim(partial_half, row_slot, 1, keepdims=False)
        return lax.dynamic_update_index_in_dim(partial_half, current + product, row_slot, 1)

    start_half = jnp.zeros((aux_count, own_blocks, block_size, orbitals), jnp.float32)
    summed_half = lax.fori_loop(0, pair_count[0, 0], add_pair, start_half)
    half = summed_half.reshape(aux_count, strip_width, orbitals).astype(jnp.bfloat16)
    strip = contract_rows(lax.all_gather(half, "occ", axis=1, tiled=True), half)
    summed = lax.psum(strip, "aux")
    share_rows = summed.shape[0] // lax.axis_size("aux")
    mine = lax.dynamic_slice_in_dim(summed, lax.axis_index("aux") * share_rows, share_rows, 0)
    return mine


def solution(mesh):
    return jax.shard_map(
        local,
        mesh=mesh,
        in_specs=(
            P("aux", "occ", None, None),
            P("occ", None),
            P("aux", "occ"),
            P("aux", "occ"),
            P("aux", "occ"),
            P(),
        ),
        out_specs=P("aux", "occ"),
        check_vma=False,
    )
```

profile of v0, /device:TPU:5, one launch (start us, length us, event | category | flops | bytes accessed | tf_op | source)
XLA Modules:
  0.0 545.6 jit_solution(660592965672363096)
XLA Ops:
  7.3 41.6 %all-gather.3.cloned.1.call-done = bf16[4096,384]{1,0:T(8,128)(2,1)} async-done(((bf16[512,384]{1,0:T(8,128)(2,1)}), bf16[4096,384]{1,0:T(8,128)(2,1)}) %all-gather.3.cloned.1.call-update) | async-done | bytes 3145744 | tf_op jit(solution)/shard_map/all_gather | solution.py:18
  49.0 173.0 %while.10 = (s32[]{:T(128)}, f32[2,4,128,384]{3,2,0,1:T(8,128)S(1)}, s32[]{:T(128)}, s32[1,24]{1,0:T(1,128)}, bf16[2,24,128,128]{3,2,1,0:T(8,128)(2,1)}, /*index...) while((s32[]{:T(128)}, ...), condition=%wide.region_1.2_spmd, body=%wide.region_0.1_spmd.sunk | while | flops 25264140 | bytes 1737021 | solution.py:34
  49.7 1.3 constant_dynamic-slice_fusion.6
  54.9 1.3 dynamic_slice.46
  59.8 1.3 constant_dynamic-slice_fusion.6
  70.0 1.3 constant_dynamic-slice_fusion.6
  80.1 1.3 constant_dynamic-slice_fusion.6
  90.3 1.3 constant_dynamic-slice_fusion.6
  100.4 1.3 constant_dynamic-slice_fusion.6
  110.5 1.3 constant_dynamic-slice_fusion.6
  120.7 1.3 constant_dynamic-slice_fusion.6
  130.8 1.3 constant_dynamic-slice_fusion.6
  141.0 1.3 constant_dynamic-slice_fusion.6
  151.1 1.3 constant_dynamic-slice_fusion.6
  161.2 1.3 constant_dynamic-slice_fusion.6
  171.4 1.3 constant_dynamic-slice_fusion.6
  181.5 1.3 constant_dynamic-slice_fusion.6
  191.7 1.3 constant_dynamic-slice_fusion.6
  201.8 1.3 constant_dynamic-slice_fusion.6
  211.9 1.3 constant_dynamic-slice_fusion.6
  223.2 132.8 %all-gather.5.cloned.1.call-done = bf16[2,4096,384]{2,1,0:T(8,128)(2,1)} async-done(((bf16[2,512,384]{2,1,0:T(8,128)(2,1)}), bf16[2,4096,384]{2,1,0:T(8,128)(2,1)}) %all-gather.5.cloned.1.call-update) | async-done | bytes 6291472 | tf_op jit(solution)/shard_map/all_gather | solution.py:36
  356.0 9.7 %convolution_bitcast_fusion = f32[4096,512]{1,0:T(8,128)} fusion(bf16[2,4096,384]{2,1,0:T(8,128)(2,1)} %all-gather.5.cloned.1.call-done, bf16[2,512,384]{2,1,0:T(8,128)(2,1)} %bitcast.40), kind=kOutput, calls=%fused_computation.11 | convolution fusion | flops 3221225472 | bytes 15466496 | tf_op jit(solution)/shard_map/pni,pmi->nm/dot_general | solution.py:8
  365.7 170.3 %all-reduce.2.cloned.1.call-done = f32[4096,512]{1,0:T(8,128)} async-done(((f32[4096,512]{1,0:T(8,128)}), f32[4096,512]{1,0:T(8,128)}) %all-reduce.2.cloned.1.call-update) | async-done | bytes 8388624 | tf_op jit(solution)/shard_map/psum | solution.py:37
  536.0 3.1 constant_dynamic-slice_fusion.3
  (59 shorter events, 42.1 us)
Async XLA Ops:
  6.5 42.4 %all-gather.3.cloned.1.call-start = ((), (), s32[]{:S(2)}) async-start(), calls=%async_computation | async-start | bytes 3538944 | tf_op jit(solution)/shard_map/all_gather | solution.py:18
  7.3 348.8 %all-gather.5.cloned.1.call-start = ((), (), s32[]{:S(2)}) async-start(), calls=%async_computation.1 | async-start | bytes 7077888 | tf_op jit(solution)/shard_map/all_gather | solution.py:36
  223.2 312.8 %all-reduce.2.cloned.1.call-start = ((), (), s32[]{:S(2)}) async-start(), calls=%async_computation.2 | async-start | bytes 16777216 | tf_op jit(solution)/shard_map/psum | solution.py:37
Sparse Core Ops, SparseCore 0:
  9.0 39.8 all-gather.2
  223.3 132.6 all-gather.4
  365.8 170.1 all-reduce.1
where the time goes:
time: 551 us; the launch traced here: 546 us
  waiting for transfers between devices  345 us (63%)
  loops' own time  109 us (20%)
  local copies, waits for them, and re-layouts  48.6 us (9%)
  matrix products  29 us (5%)
  between operations  13.1 us (2%)
    psum x1, waiting for transfers between devices, local(): summed = lax.psum(strip, 'aux')  170 us
    all_gather x1, waiting for transfers between devices, local(): strip = contract_rows(lax.all_gather(half, 'occ', axis=1, tiled=True), half)  133 us
    another operation x1, loops' own time, local(): summed_half = lax.fori_loop(0, pair_count[0, 0], add_pair, start_half)  109 us
    dynamic_slice x34, local copies, waits for them, and re-layouts, add_pair(): basis_block = row_blocks[pair_cols[0, slot_index]]  43.9 us
    all_gather x1, waiting for transfers between devices, local(): full_coeff = lax.all_gather(coefficients, 'occ', axis=0, tiled=True)  41.6 us
    dot_general x17, matrix products, add_pair(): jnp.einsum('pmn,ni->pmi', integral_piece, coeff_piece, preferred_element_...  19.3 us
  transfers between devices with their start and end apart: 3, of which 3 were waited for; matrix products, arithmetic and copies ran while one was open for 0% of the time, Pallas kernels for 0%

commit v1 on v0

v1 whole, which is shorter than its diff:
```python
import functools
import math

import jax
import jax.numpy as jnp
from jax import lax
from jax.experimental import pallas as pl
from jax.experimental.pallas import tpu as pltpu
from jax.sharding import PartitionSpec as P

AXES = ("aux", "occ")
CORES = 2
ANY = pl.BlockSpec(memory_space=pl.ANY)
IN_SMEM = pl.BlockSpec(memory_space=pltpu.SMEM)
IN_VMEM = pl.BlockSpec(memory_space=pltpu.VMEM)


class Layout:
    def __init__(self, aux, occ):
        self.aux, self.occ, self.planes = aux, occ, occ // CORES
        self.bits = int(math.log2(aux))

    def send(self, value, where):
        pairs = []
        for a in range(self.aux):
            for z in range(self.planes):
                for c in range(CORES):
                    to = where(a, z, c)
                    if to is not None:
                        pairs.append((a * self.occ + z * CORES + c, to[0] * self.occ + to[1] * CORES + to[2]))
        return lax.ppermute(value, AXES, pairs)


def half_kernel(lay, share, sources, count_ref, cols_ref, rows_ref, natural_ref, integrals_ref, *refs):
    pieces, (out_ref, coeff, total, sems) = refs[:sources], refs[sources:]
    own_blocks = total.shape[0]
    part = own_blocks // share
    copies = []
    start = 0
    for n, piece in enumerate(pieces):
        size = piece.shape[0]
        copies.append(pltpu.make_async_copy(piece, coeff.at[pl.ds(start, size)], sems.at[n]))
        start += size
    for copy in copies:
        copy.start()
    total[...] = jnp.zeros_like(total)
    for copy in copies:
        copy.wait()
    aux_count, slots, block, _ = integrals_ref.shape
    orbitals = coeff.shape[2]
    occ_index = lax.axis_index("occ")
    z, c = occ_index // CORES, occ_index % CORES
    k = lax.axis_index("aux") % share
    per_piece = (lay.planes - 1) * part

    def add_slot(slot, carry):
        natural = natural_ref[cols_ref[0, slot]]
        source, inner = natural // own_blocks, natural % own_blocks
        z_off, c_off = (source // CORES) ^ z, (source % CORES) ^ c
        k_off, in_part = (inner // part) ^ k, inner % part
        near = c_off * own_blocks + inner
        away = CORES * own_blocks + (k_off * CORES + c_off) * per_piece + (z_off - 1) * part + in_part
        piece = coeff[jnp.where(z_off == 0, near, away)]
        left = jnp.concatenate([integrals_ref[p, slot] for p in range(aux_count)], axis=0)
        total[rows_ref[0, slot]] += jnp.dot(left, piece, preferred_element_type=jnp.float32)
        return carry

    lax.fori_loop(0, count_ref[0, 0], add_slot, 0)
    for row in range(own_blocks):
        for p in range(aux_count):
            out_ref[pl.ds(row * block, block), pl.ds(p * orbitals, orbitals)] = total[
                row, pl.ds(p * block, block), :
            ].astype(jnp.bfloat16)


def half_transform(lay, share, own_blocks, integrals, pieces, cols, rows, count, natural):
    aux_count, slots, block, _ = integrals.shape
    orbitals = pieces[0].shape[2]
    blocks = sum(piece.shape[0] for piece in pieces)
    return pl.pallas_call(
        functools.partial(half_kernel, lay, share, len(pieces)),
        out_shape=jax.ShapeDtypeStruct((own_blocks * block, aux_count * orbitals), jnp.bfloat16),
        in_specs=[IN_SMEM] * 4 + [IN_VMEM] + [ANY] * len(pieces),
        out_specs=IN_VMEM,
        scratch_shapes=[
            pltpu.VMEM((blocks, block, orbitals), jnp.bfloat16),
            pltpu.VMEM((own_blocks, aux_count * block, orbitals), jnp.float32),
            pltpu.SemaphoreType.DMA((len(pieces),)),
        ],
        compiler_params=pltpu.CompilerParams(vmem_limit_bytes=32 * 1024 * 1024),
        name="half_transform",
    )(count, cols, rows, natural, integrals, *pieces)


def product(first, second):
    return lax.dot_general(first, second, (((1,), (1,)), ((), ())), preferred_element_type=jnp.float32)


def reduce_to_owner(lay, partial, owner, order):
    terms = [partial]
    done = 0
    for step, bit in enumerate(order):
        total = functools.reduce(lambda x, y: x + y.astype(jnp.float32), terms)

        def where(a, z, c, bit=bit, done=done):
            own = owner(z, c)
            if own is None or (a ^ own) & done or not (a ^ own) >> bit & 1:
                return None
            return (a ^ (1 << bit), z, c)

        terms.append(lay.send(total.astype(jnp.bfloat16), where))
        done |= 1 << bit
    return terms


def local(lay, integrals, coefficients, pair_rows, pair_cols, pair_count, row_blocks):
    aux_count, slots, block, _ = integrals.shape
    block_total = row_blocks.shape[0]
    own_blocks = block_total // lay.occ
    width = own_blocks * block
    orbitals = coefficients.shape[1]
    planes = lay.planes
    a = lax.axis_index("aux")
    occ_index = lax.axis_index("occ")
    z, c = occ_index // CORES, occ_index % CORES

    share = min(lay.aux, own_blocks)
    part = own_blocks // share
    blocks = coefficients.reshape(own_blocks, block, orbitals)
    mine = lax.dynamic_slice_in_dim(blocks, (a % share) * part, part, 0)
    far = [lay.send(mine, lambda a_, z_, c_, d=d: (a_, z_ ^ d, c_)) for d in range(1, planes)]
    far = jnp.concatenate(far, axis=0)
    spread = [far] + [lay.send(far, lambda a_, z_, c_, k=k: (a_ ^ k, z_, c_)) for k in range(1, share)]
    other = lambda v: lay.send(v, lambda a_, z_, c_: (a_, z_, 1 - c_))
    pieces = [blocks, other(blocks)]
    for piece in spread:
        pieces += [piece, other(piece)]
    half = half_transform(lay, share, own_blocks, integrals, pieces, pair_cols, pair_rows, pair_count, row_blocks)

    out_blocks = block_total * block // lay.aux // width
    x_first, y_first = tuple(range(lay.bits)), tuple(reversed(range(lay.bits)))
    entries = []

    def arrived(held, plane_of):
        def owner(z_, c_):
            plane = plane_of(z_)
            return None if plane is None else (plane * CORES + c_) // out_blocks

        same = reduce_to_owner(lay, product(held, half), owner, x_first)
        cross = reduce_to_owner(lay, product(other(held), half), lambda z_, c_: owner(z_, 1 - c_), y_first)
        entries.append((plane_of, same, cross))

    arrived(half, lambda z_: z_)
    up = down = half
    for s in range(1, planes):
        up = lay.send(up, lambda a_, z_, c_: (a_, z_ + 1, c_) if z_ + 1 < planes else None)
        down = lay.send(down, lambda a_, z_, c_: (a_, z_ - 1, c_) if z_ > 0 else None)
        below = lambda z_, s=s: z_ - s if z_ >= s else None
        above = lambda z_, s=s: z_ + s if z_ + s < planes else None
        if 2 * s < planes:
            arrived(up, below)
            arrived(down, above)
        else:
            both = jnp.where(z >= s, up, down)
            arrived(both, lambda z_, below=below, above=above: below(z_) if above(z_) is None else above(z_))

    results = []
    for t in range(out_blocks):
        row = a * out_blocks + t
        index = jnp.int32(0)
        branches = []
        for plane_of, same, cross in entries:
            plane = jnp.int32(-1)
            for z_ in range(planes):
                if plane_of(z_) is not None:
                    plane = jnp.where(z == z_, plane_of(z_), plane)
            for terms, core in ((same, c), (cross, 1 - c)):
                index = jnp.where(plane * CORES + core == row, len(branches), index)
                branches.append(lambda terms=terms: functools.reduce(lambda x, y: x + y.astype(jnp.float32), terms))
        results.append(lax.switch(index, branches))
    return jnp.concatenate(results, axis=0) if out_blocks > 1 else results[0]


def solution(mesh):
    lay = Layout(mesh.shape["aux"], mesh.shape["occ"])
    return jax.shard_map(
        functools.partial(local, lay),
        mesh=mesh,
        in_specs=(
            P("aux", "occ", None, None),
            P("occ", None),
            P("aux", "occ"),
            P("aux", "occ"),
            P("aux", "occ"),
            P(),
        ),
        out_specs=P("aux", "occ"),
        check_vma=False,
    )
```

time: 551 us -> 210 us (0.38)
  waiting for transfers between devices: 345 us -> 78.6 us
  loops' own time: 109 us -> 0.01 us
  starting transfers between devices: 0.08 us -> 90.3 us
  local copies, waits for them, and re-layouts: 48.6 us -> 15 us
  matrix products: 29 us -> 8.29 us
  between operations: 13.1 us -> 1.29 us
  other arithmetic: 0.09 us -> 9.79 us
    all_gather x2 -> x0, waiting for transfers between devices: 174 us -> none  [the longest x1 133 us: local(): strip = contract_rows(lax.all_gather(half, 'occ', axis=1, tiled=True), half)]
    psum x1 -> x0, waiting for transfers between devices: 170 us -> none  [local(): summed = lax.psum(strip, 'aux')]
    another operation x1 -> x2, loops' own time: 109 us -> 0.01 us  [local(): results.append(lax.switch(index, branches))]
    ppermute x0 -> x42, starting transfers between devices: none -> 90.3 us  [send(): return lax.ppermute(value, AXES, pairs)]
    ppermute x0 -> x42, waiting for transfers between devices: none -> 78.6 us  [send(): return lax.ppermute(value, AXES, pairs)]
    dynamic_slice x52 -> x1, local copies, waits for them, and re-layouts: 47.5 us -> 0.9 us  [local(): mine = lax.dynamic_slice_in_dim(blocks, a % share * part, part, 0)]
    dot_general x18 -> x10, matrix products: 29 us -> 8.29 us  [product(): lax.dot_general(first, second, (((1,), (1,)), ((), ())), preferred_elemen...]
    cond x0 -> x10, local copies, waits for them, and re-layouts: none -> 7.43 us
  transfers between devices with their start and end apart: 3 -> 42, of which waited for: 3 -> 17; matrix products, arithmetic and copies ran while one was open for 0% -> 7% of each run, Pallas kernels for 0% -> 0%
where the time goes in v1:
time: 210 us; the launch traced here: 207 us
  starting transfers between devices  90.3 us (43%)
  waiting for transfers between devices  78.6 us (37%)
  local copies, waits for them, and re-layouts  15 us (7%)
  other arithmetic  9.79 us (5%)
  matrix products  8.29 us (4%)
  Pallas kernels  3.43 us (2%)
    ppermute x42, starting transfers between devices, send(): return lax.ppermute(value, AXES, pairs)  90.3 us
    ppermute x42, waiting for transfers between devices, send(): return lax.ppermute(value, AXES, pairs)  78.6 us
    dot_general x10, matrix products, product(): lax.dot_general(first, second, (((1,), (1,)), ((), ())), preferred_elemen...  8.29 us
    cond x10, local copies, waits for them, and re-layouts  7.43 us
    unnamed x58, local copies, waits for them, and re-layouts  6.62 us
    convert_element_type x10, other arithmetic, reduce_to_owner(): terms.append(lay.send(total.astype(jnp.bfloat16), where))  5.59 us
  transfers between devices with their start and end apart: 42, of which 17 were waited for; matrix products, arithmetic and copies ran while one was open for 7% of the time, Pallas kernels for 0%

profile of v1, /device:TPU:5, one launch (start us, length us, event | category | flops | bytes accessed | tf_op | source)
XLA Modules:
  0.0 206.6 jit_solution(4213631879902174326)
XLA Ops:
  6.9 4.2 %collective-permute-done.3 = bf16[1,128,384]{2,1,0:T(8,128)(2,1)S(1)} collective-permute-done((bf16[1,128,384]{2,1,0:T(8,128)(2,1)S(1)}, bf16[1,128,384]{2,1,0:T(8,128)(2,1)S(1)}, u32[]{:S(2)}, u32[]{:S(2)}) %collective-permute-start.3) | collective-permute-done | bytes 98336 | tf_op jit(solution)/shard_map/ppermute | solution.py:31
  13.8 3.4 %collective-permute-start = (bf16[4,128,384]{2,1,0:T(8,128)(2,1)}, bf16[4,128,384]{2,1,0:T(8,128)(2,1)S(1)}, u32[]{:S(2)}, u32[]{:S(2)}) collective-permute-start(bf16[4,128,384]{2,1,0:T(8,128)(2,1)} %bitcast.22), channel_id=1, source_target_pairs={{0,1},{1,0},{2,3},{3,2},{4,5},{5,4},{6,7},{7,6},{8,9},{9,8},{10,11... | collective-permute-start | bytes 1179656 | tf_op jit(solution)/shard_map/ppermute | solution.py:31
  18.1 6.5 %collective-permute-start.10 = (bf16[3,128,384]{2,1,0:T(8,128)(2,1)S(1)}, bf16[3,128,384]{2,1,0:T(8,128)(2,1)S(1)}, u32[]{:S(2)}, u32[]{:S(2)}) collective-permute-start(bf16[3,128,384]{2,1,0:T(8,128)(2,1)S(1)} %collective-permute-done.9.refs_8_), channel_id=1, source_target_pairs={{0,1},{1,0},{2,3},{3,2},{4,5},{5,4},{6,7},{7,6},{8,9},{9,8},{10,11... | collective-permute-start | bytes 884744 | tf_op jit(solution)/shard_map/ppermute | solution.py:31
  33.4 3.4 %half_transform.1 = bf16[512,768]{1,0:T(8,128)(2,1)S(1)} custom-call(s32[1,1]{1,0:T(1,128)S(6)} %copy.69.count_ref, s32[1,24]{1,0:T(1,128)S(1)} %copy-done.2, s32[1,24]{1,0:T(1,128)S(1)} %copy-done.3, s32[32]{0:T(128)S(1)} %copy-done.4, bf16[2,24,128,128]{3,2,1,0:T(8,128)(2,1)S(1)} %copy-done, bf16[4,128,384]{2,1,0:T(8,128)(2,1)S(1)} %bitcast.23, ...), custom_call_target="tpu_custom_call" | custom-call | tf_op jit(solution)/shard_map/half_transform/pallas_call | solution.py:80
  40.1 9.5 %collective-permute-start.16 = (bf16[512,768]{1,0:T(8,128)(2,1)S(1)}, bf16[512,768]{1,0:T(8,128)(2,1)}, u32[]{:S(2)}, u32[]{:S(2)}) collective-permute-start(bf16[512,768]{1,0:T(8,128)(2,1)S(1)} %half_transform.1), channel_id=1, source_target_pairs={{0,2},{1,3},{2,4},{3,5},{4,6},{5,7},{8,10},{9,11},{10,12},{11,13},... | collective-permute-start | bytes 2359304 | tf_op jit(solution)/shard_map/ppermute | solution.py:31
  49.5 3.5 %collective-permute-done.11 = bf16[512,512]{1,0:T(8,128)(2,1)S(1)} collective-permute-done((bf16[512,512]{1,0:T(8,128)(2,1)S(1)}, bf16[512,512]{1,0:T(8,128)(2,1)S(1)}, u32[]{:S(2)}, u32[]{:S(2)}) %collective-permute-start.11) | collective-permute-done | bytes 524320 | tf_op jit(solution)/shard_map/ppermute | solution.py:31
  53.2 2.6 %collective-permute-start.12 = (bf16[512,512]{1,0:T(8,128)(2,1)S(1)}, bf16[512,512]{1,0:T(8,128)(2,1)S(1)}, u32[]{:S(2)}, u32[]{:S(2)}) collective-permute-start(bf16[512,512]{1,0:T(8,128)(2,1)S(1)} %add_convert_fusion.9), channel_id=1, source_target_pairs={{4,20},{5,21},{14,30},{15,31},{16,0},{17,1},{26,10},{27,11}} | collective-permute-start | bytes 1572872 | tf_op jit(solution)/shard_map/ppermute | solution.py:31
  55.8 8.4 %collective-permute-done.22 = bf16[512,768]{1,0:T(8,128)(2,1)} collective-permute-done((bf16[512,768]{1,0:T(8,128)(2,1)S(1)}, bf16[512,768]{1,0:T(8,128)(2,1)}, u32[]{:S(2)}, u32[]{:S(2)}) %collective-permute-start.22) | collective-permute-done | bytes 786464 | tf_op jit(solution)/shard_map/ppermute | solution.py:31
  72.0 4.3 %collective-permute-start.28 = (bf16[512,768]{1,0:T(8,128)(2,1)}, bf16[512,768]{1,0:T(8,128)(2,1)S(1)}, u32[]{:S(2)}, u32[]{:S(2)}) collective-permute-start(bf16[512,768]{1,0:T(8,128)(2,1)} %collective-permute-done.16), channel_id=1, source_target_pairs={{0,2},{1,3},{2,4},{3,5},{4,6},{5,7},{8,10},{9,11},{10,12},{11,13},... | collective-permute-start | bytes 2359304 | tf_op jit(solution)/shard_map/ppermute | solution.py:31
  81.4 2.7 %collective-permute-start.19 = (bf16[512,768]{1,0:T(8,128)(2,1)}, bf16[512,768]{1,0:T(8,128)(2,1)S(1)}, u32[]{:S(2)}, u32[]{:S(2)}) collective-permute-start(bf16[512,768]{1,0:T(8,128)(2,1)} %collective-permute-done.16), channel_id=1, source_target_pairs={{0,1},{1,0},{2,3},{3,2},{4,5},{5,4},{6,7},{7,6},{8,9},{9,8},{10,11... | collective-permute-start | bytes 2359304 | tf_op jit(solution)/shard_map/ppermute | solution.py:31
  84.2 7.7 %collective-permute-done.28 = bf16[512,768]{1,0:T(8,128)(2,1)S(1)} collective-permute-done((bf16[512,768]{1,0:T(8,128)(2,1)}, bf16[512,768]{1,0:T(8,128)(2,1)S(1)}, u32[]{:S(2)}, u32[]{:S(2)}) %collective-permute-start.28) | collective-permute-done | bytes 786464 | tf_op jit(solution)/shard_map/ppermute | solution.py:31
  91.9 9.5 %collective-permute-done.29 = bf16[512,768]{1,0:T(8,128)(2,1)S(1)} collective-permute-done((bf16[512,768]{1,0:T(8,128)(2,1)}, bf16[512,768]{1,0:T(8,128)(2,1)S(1)}, u32[]{:S(2)}, u32[]{:S(2)}) %collective-permute-start.29) | collective-permute-done | bytes 786464 | tf_op jit(solution)/shard_map/ppermute | solution.py:31
  103.4 4.7 %collective-permute-start.35 = (bf16[512,768]{1,0:T(8,128)(2,1)S(1)}, bf16[512,768]{1,0:T(8,128)(2,1)S(1)}, u32[]{:S(2)}, u32[]{:S(2)}) collective-permute-start(bf16[512,768]{1,0:T(8,128)(2,1)S(1)} %collective-permute-done.28), channel_id=1, source_target_pairs={{0,2},{1,3},{2,4},{3,5},{4,6},{5,7},{8,10},{9,11},{10,12},{11,13},... | collective-permute-start | bytes 2359304 | tf_op jit(solution)/shard_map/ppermute | solution.py:31
  112.2 2.8 %collective-permute-done.30 = bf16[512,512]{1,0:T(8,128)(2,1)S(1)} collective-permute-done((bf16[512,512]{1,0:T(8,128)(2,1)S(1)}, bf16[512,512]{1,0:T(8,128)(2,1)S(1)}, u32[]{:S(2)}, u32[]{:S(2)}) %collective-permute-start.30) | collective-permute-done | bytes 524320 | tf_op jit(solution)/shard_map/ppermute | solution.py:31
  117.0 4.9 %collective-permute-done.35 = bf16[512,768]{1,0:T(8,128)(2,1)S(1)} collective-permute-done((bf16[512,768]{1,0:T(8,128)(2,1)S(1)}, bf16[512,768]{1,0:T(8,128)(2,1)S(1)}, u32[]{:S(2)}, u32[]{:S(2)}) %collective-permute-start.35) | collective-permute-done | bytes 786464 | tf_op jit(solution)/shard_map/ppermute | solution.py:31
  121.9 4.0 %collective-permute-start.32 = (bf16[512,768]{1,0:T(8,128)(2,1)S(1)}, bf16[512,768]{1,0:T(8,128)(2,1)S(1)}, u32[]{:S(2)}, u32[]{:S(2)}) collective-permute-start(bf16[512,768]{1,0:T(8,128)(2,1)S(1)} %broadcast_select_fusion.1), channel_id=1, source_target_pairs={{0,1},{1,0},{2,3},{3,2},{4,5},{5,4},{6,7},{7,6},{8,9},{9,8},{10,11... | collective-permute-start | bytes 2359304 | tf_op jit(solution)/shard_map/ppermute | solution.py:31
  126.6 4.2 %collective-permute-start.39 = (bf16[512,768]{1,0:T(8,128)(2,1)S(1)}, bf16[512,768]{1,0:T(8,128)(2,1)S(1)}, u32[]{:S(2)}, u32[]{:S(2)}) collective-permute-start(bf16[512,768]{1,0:T(8,128)(2,1)S(1)} %broadcast_select_fusion), channel_id=1, source_target_pairs={{0,1},{1,0},{2,3},{3,2},{4,5},{5,4},{6,7},{7,6},{8,9},{9,8},{10,11... | collective-permute-start | bytes 2359304 | tf_op jit(solution)/shard_map/ppermute | solution.py:31
  132.5 8.4 %collective-permute-start.37 = (bf16[512,512]{1,0:T(8,128)(2,1)S(1)}, bf16[512,512]{1,0:T(8,128)(2,1)S(1)}, u32[]{:S(2)}, u32[]{:S(2)}) collective-permute-start(bf16[512,512]{1,0:T(8,128)(2,1)S(1)} %get-tuple-element.231), channel_id=1, source_target_pairs={{0,8},{1,9},{14,6},{15,7},{16,24},{17,25},{30,22},{31,23}} | collective-permute-start | bytes 1572872 | tf_op jit(solution)/shard_map/ppermute | solution.py:31
  145.8 6.4 %collective-permute-done.37 = bf16[512,512]{1,0:T(8,128)(2,1)S(1)} collective-permute-done((bf16[512,512]{1,0:T(8,128)(2,1)S(1)}, bf16[512,512]{1,0:T(8,128)(2,1)S(1)}, u32[]{:S(2)}, u32[]{:S(2)}) %collective-permute-start.37) | collective-permute-done | bytes 524320 | tf_op jit(solution)/shard_map/ppermute | solution.py:31
  158.4 9.8 %collective-permute-done.40 = bf16[512,512]{1,0:T(8,128)(2,1)S(1)} collective-permute-done((bf16[512,512]{1,0:T(8,128)(2,1)S(1)}, bf16[512,512]{1,0:T(8,128)(2,1)S(1)}, u32[]{:S(2)}, u32[]{:S(2)}) %collective-permute-start.40) | collective-permute-done | bytes 524320 | tf_op jit(solution)/shard_map/ppermute | solution.py:31
  177.9 4.7 %collective-permute-done.31 = bf16[512,512]{1,0:T(8,128)(2,1)} collective-permute-done((bf16[512,512]{1,0:T(8,128)(2,1)S(1)}, bf16[512,512]{1,0:T(8,128)(2,1)}, u32[]{:S(2)}, u32[]{:S(2)}) %collective-permute-start.31) | collective-permute-done | bytes 524320 | tf_op jit(solution)/shard_map/ppermute | solution.py:31
  184.7 6.5 %collective-permute-done.34 = bf16[512,512]{1,0:T(8,128)(2,1)} collective-permute-done((bf16[512,512]{1,0:T(8,128)(2,1)}, bf16[512,512]{1,0:T(8,128)(2,1)}, u32[]{:S(2)}, u32[]{:S(2)}) %collective-permute-start.34) | collective-permute-done | bytes 524320 | tf_op jit(solution)/shard_map/ppermute | solution.py:31
  197.6 5.0 %conditional.3 = (f32[512,512]{1,0:T(8,128)}, bf16[512,512]{1,0:T(8,128)(2,1)}, bf16[512,512]{1,0:T(8,128)(2,1)}) conditional(s32[]{:T(128)} %clamp.7, (f32[512,512]{1,0:T(8,128)}, bf16[512,512]{1,0:T(8,128)(2,1)}, bf16[512,512]{1,0:T(8,128)(2,1)}) %tuple.227, (f32[512,512]{1,0:T(8,128)S(1)}, ...), branch_computations={%region_10.11_spmd, %region_11.12_spmd, %region_12.13_spmd, %regio... | conditional | bytes 6291508 | solution.py:180
  202.6 2.5 %fusion = (f32[512,512]{1,0:T(8,128)S(1)}, f32[512,512]{1,0:T(8,128)S(1)}) fusion(f32[512,512]{1,0:T(8,128)} %get-tuple-element.212, bf16[512,512]{1,0:T(8,128)(2,1)} %get-tuple-element.213, bf16[512,512]{1,0:T(8,128)(2,1)} %get-tuple-element.214, bf16[512,512]{1,0:T(8,128)(2,1)} %copy-done.47, f32[512,512]{1,0:T(8,128)} %copy-done.43, ...), kind=kLoop, calls=%fused_computation.2 | loop fusion | flops 2097152 | bytes 6291456 | tf_op jit(solution)/shard_map/cond/branch_0_fun/add | solution.py:179
  (157 shorter events, 83.1 us)
Async XLA Ops:
  12.6 14.3 %collective-permute-start.7 = (bf16[3,128,384]{2,1,0:T(8,128)(2,1)S(1)}, bf16[3,128,384]{2,1,0:T(8,128)(2,1)S(1)}, u32[]{:S(2)}, u32[]{:S(2)}) collective-permute-start(bf16[3,128,384]{2,1,0:T(8,128)(2,1)S(1)} %constant_dynamic-update-slice_fusion.refs_2_), channel_id=1, source_target_pairs={{0,16},{1,17},{2,18},{3,19},{4,20},{5,21},{6,22},{7,23},{8,24},{9,... | collective-permute-start | bytes 884744 | tf_op jit(solution)/shard_map/ppermute | solution.py:31
  13.8 14.7 %collective-permute-start = (bf16[4,128,384]{2,1,0:T(8,128)(2,1)}, bf16[4,128,384]{2,1,0:T(8,128)(2,1)S(1)}, u32[]{:S(2)}, u32[]{:S(2)}) collective-permute-start(bf16[4,128,384]{2,1,0:T(8,128)(2,1)} %bitcast.22), channel_id=1, source_target_pairs={{0,1},{1,0},{2,3},{3,2},{4,5},{5,4},{6,7},{7,6},{8,9},{9,8},{10,11... | collective-permute-start | bytes 1179656 | tf_op jit(solution)/shard_map/ppermute | solution.py:31
  37.5 15.6 %collective-permute-start.11 = (bf16[512,512]{1,0:T(8,128)(2,1)S(1)}, bf16[512,512]{1,0:T(8,128)(2,1)S(1)}, u32[]{:S(2)}, u32[]{:S(2)}) collective-permute-start(bf16[512,512]{1,0:T(8,128)(2,1)S(1)} %get-tuple-element.215), channel_id=1, source_target_pairs={{2,10},{3,11},{6,14},{7,15},{8,0},{9,1},{12,4},{13,5},{18,26},{19,... | collective-permute-start | bytes 1572872 | tf_op jit(solution)/shard_map/ppermute | solution.py:31
  38.8 25.4 %collective-permute-start.22 = (bf16[512,768]{1,0:T(8,128)(2,1)S(1)}, bf16[512,768]{1,0:T(8,128)(2,1)}, u32[]{:S(2)}, u32[]{:S(2)}) collective-permute-start(bf16[512,768]{1,0:T(8,128)(2,1)S(1)} %half_transform.1), channel_id=1, source_target_pairs={{2,0},{3,1},{4,2},{5,3},{6,4},{7,5},{10,8},{11,9},{12,10},{13,11},... | collective-permute-start | bytes 2359304 | tf_op jit(solution)/shard_map/ppermute | solution.py:31
  40.1 27.5 %collective-permute-start.16 = (bf16[512,768]{1,0:T(8,128)(2,1)S(1)}, bf16[512,768]{1,0:T(8,128)(2,1)}, u32[]{:S(2)}, u32[]{:S(2)}) collective-permute-start(bf16[512,768]{1,0:T(8,128)(2,1)S(1)} %half_transform.1), channel_id=1, source_target_pairs={{0,2},{1,3},{2,4},{3,5},{4,6},{5,7},{8,10},{9,11},{10,12},{11,13},... | collective-permute-start | bytes 2359304 | tf_op jit(solution)/shard_map/ppermute | solution.py:31
  49.5 20.5 %collective-permute-start.13 = (bf16[512,768]{1,0:T(8,128)(2,1)S(1)}, bf16[512,768]{1,0:T(8,128)(2,1)S(1)}, u32[]{:S(2)}, u32[]{:S(2)}) collective-permute-start(bf16[512,768]{1,0:T(8,128)(2,1)S(1)} %half_transform.1), channel_id=1, source_target_pairs={{0,1},{1,0},{2,3},{3,2},{4,5},{5,4},{6,7},{7,6},{8,9},{9,8},{10,11... | collective-permute-start | bytes 2359304 | tf_op jit(solution)/shard_map/ppermute | solution.py:31
  53.2 118.2 %collective-permute-start.12 = (bf16[512,512]{1,0:T(8,128)(2,1)S(1)}, bf16[512,512]{1,0:T(8,128)(2,1)S(1)}, u32[]{:S(2)}, u32[]{:S(2)}) collective-permute-start(bf16[512,512]{1,0:T(8,128)(2,1)S(1)} %add_convert_fusion.9), channel_id=1, source_target_pairs={{4,20},{5,21},{14,30},{15,31},{16,0},{17,1},{26,10},{27,11}} | collective-permute-start | bytes 1572872 | tf_op jit(solution)/shard_map/ppermute | solution.py:31
  72.0 20.0 %collective-permute-start.28 = (bf16[512,768]{1,0:T(8,128)(2,1)}, bf16[512,768]{1,0:T(8,128)(2,1)S(1)}, u32[]{:S(2)}, u32[]{:S(2)}) collective-permute-start(bf16[512,768]{1,0:T(8,128)(2,1)} %collective-permute-done.16), channel_id=1, source_target_pairs={{0,2},{1,3},{2,4},{3,5},{4,6},{5,7},{8,10},{9,11},{10,12},{11,13},... | collective-permute-start | bytes 2359304 | tf_op jit(solution)/shard_map/ppermute | solution.py:31
  77.9 23.5 %collective-permute-start.29 = (bf16[512,768]{1,0:T(8,128)(2,1)}, bf16[512,768]{1,0:T(8,128)(2,1)S(1)}, u32[]{:S(2)}, u32[]{:S(2)}) collective-permute-start(bf16[512,768]{1,0:T(8,128)(2,1)} %collective-permute-done.22), channel_id=1, source_target_pairs={{2,0},{3,1},{4,2},{5,3},{6,4},{7,5},{10,8},{11,9},{12,10},{13,11},... | collective-permute-start | bytes 2359304 | tf_op jit(solution)/shard_map/ppermute | solution.py:31
  79.4 28.7 %collective-permute-start.25 = (bf16[512,768]{1,0:T(8,128)(2,1)}, bf16[512,768]{1,0:T(8,128)(2,1)S(1)}, u32[]{:S(2)}, u32[]{:S(2)}) collective-permute-start(bf16[512,768]{1,0:T(8,128)(2,1)} %collective-permute-done.22), channel_id=1, source_target_pairs={{0,1},{1,0},{2,3},{3,2},{4,5},{5,4},{6,7},{7,6},{8,9},{9,8},{10,11... | collective-permute-start | bytes 2359304 | tf_op jit(solution)/shard_map/ppermute | solution.py:31
  81.4 28.7 %collective-permute-start.19 = (bf16[512,768]{1,0:T(8,128)(2,1)}, bf16[512,768]{1,0:T(8,128)(2,1)S(1)}, u32[]{:S(2)}, u32[]{:S(2)}) collective-permute-start(bf16[512,768]{1,0:T(8,128)(2,1)} %collective-permute-done.16), channel_id=1, source_target_pairs={{0,1},{1,0},{2,3},{3,2},{4,5},{5,4},{6,7},{7,6},{8,9},{9,8},{10,11... | collective-permute-start | bytes 2359304 | tf_op jit(solution)/shard_map/ppermute | solution.py:31
  102.1 12.9 %collective-permute-start.30 = (bf16[512,512]{1,0:T(8,128)(2,1)S(1)}, bf16[512,512]{1,0:T(8,128)(2,1)S(1)}, u32[]{:S(2)}, u32[]{:S(2)}) collective-permute-start(bf16[512,512]{1,0:T(8,128)(2,1)S(1)} %get-tuple-element.227), channel_id=1, source_target_pairs={{2,10},{3,11},{6,14},{7,15},{8,0},{9,1},{12,4},{13,5},{18,26},{19,... | collective-permute-start | bytes 1572872 | tf_op jit(solution)/shard_map/ppermute | solution.py:31
  103.4 18.5 %collective-permute-start.35 = (bf16[512,768]{1,0:T(8,128)(2,1)S(1)}, bf16[512,768]{1,0:T(8,128)(2,1)S(1)}, u32[]{:S(2)}, u32[]{:S(2)}) collective-permute-start(bf16[512,768]{1,0:T(8,128)(2,1)S(1)} %collective-permute-done.28), channel_id=1, source_target_pairs={{0,2},{1,3},{2,4},{3,5},{4,6},{5,7},{8,10},{9,11},{10,12},{11,13},... | collective-permute-start | bytes 2359304 | tf_op jit(solution)/shard_map/ppermute | solution.py:31
  108.2 17.7 %collective-permute-start.36 = (bf16[512,768]{1,0:T(8,128)(2,1)S(1)}, bf16[512,768]{1,0:T(8,128)(2,1)S(1)}, u32[]{:S(2)}, u32[]{:S(2)}) collective-permute-start(bf16[512,768]{1,0:T(8,128)(2,1)S(1)} %collective-permute-done.29), channel_id=1, source_target_pairs={{2,0},{3,1},{4,2},{5,3},{6,4},{7,5},{10,8},{11,9},{12,10},{13,11},... | collective-permute-start | bytes 2359304 | tf_op jit(solution)/shard_map/ppermute | solution.py:31
  110.1 63.6 %collective-permute-start.24 = (bf16[512,512]{1,0:T(8,128)(2,1)S(1)}, bf16[512,512]{1,0:T(8,128)(2,1)}, u32[]{:S(2)}, u32[]{:S(2)}) collective-permute-start(bf16[512,512]{1,0:T(8,128)(2,1)S(1)} %add_convert_fusion.5), channel_id=1, source_target_pairs={{2,18},{3,19},{12,28},{13,29},{24,8},{25,9}} | collective-permute-start | bytes 1572872 | tf_op jit(solution)/shard_map/ppermute | solution.py:31
  125.8 17.6 %collective-permute-start.20 = (bf16[512,512]{1,0:T(8,128)(2,1)S(1)}, bf16[512,512]{1,0:T(8,128)(2,1)S(1)}, u32[]{:S(2)}, u32[]{:S(2)}) collective-permute-start(bf16[512,512]{1,0:T(8,128)(2,1)S(1)} %get-tuple-element.221), channel_id=1, source_target_pairs={{6,22},{7,23},{14,30},{15,31},{18,2},{19,3},{20,4},{21,5},{26,10},... | collective-permute-start | bytes 1572872 | tf_op jit(solution)/shard_map/ppermute | solution.py:31
  126.6 14.9 %collective-permute-start.39 = (bf16[512,768]{1,0:T(8,128)(2,1)S(1)}, bf16[512,768]{1,0:T(8,128)(2,1)S(1)}, u32[]{:S(2)}, u32[]{:S(2)}) collective-permute-start(bf16[512,768]{1,0:T(8,128)(2,1)S(1)} %broadcast_select_fusion), channel_id=1, source_target_pairs={{0,1},{1,0},{2,3},{3,2},{4,5},{5,4},{6,7},{7,6},{8,9},{9,8},{10,11... | collective-permute-start | bytes 2359304 | tf_op jit(solution)/shard_map/ppermute | solution.py:31
  132.5 19.7 %collective-permute-start.37 = (bf16[512,512]{1,0:T(8,128)(2,1)S(1)}, bf16[512,512]{1,0:T(8,128)(2,1)S(1)}, u32[]{:S(2)}, u32[]{:S(2)}) collective-permute-start(bf16[512,512]{1,0:T(8,128)(2,1)S(1)} %get-tuple-element.231), channel_id=1, source_target_pairs={{0,8},{1,9},{14,6},{15,7},{16,24},{17,25},{30,22},{31,23}} | collective-permute-start | bytes 1572872 | tf_op jit(solution)/shard_map/ppermute | solution.py:31
  141.5 15.4 %collective-permute-start.33 = (bf16[512,512]{1,0:T(8,128)(2,1)S(1)}, bf16[512,512]{1,0:T(8,128)(2,1)S(1)}, u32[]{:S(2)}, u32[]{:S(2)}) collective-permute-start(bf16[512,512]{1,0:T(8,128)(2,1)S(1)} %get-tuple-element.229), channel_id=1, source_target_pairs={{0,16},{1,17},{2,18},{3,19},{8,24},{9,25},{10,26},{11,27},{20,4},{... | collective-permute-start | bytes 1572872 | tf_op jit(solution)/shard_map/ppermute | solution.py:31
  143.5 24.7 %collective-permute-start.40 = (bf16[512,512]{1,0:T(8,128)(2,1)S(1)}, bf16[512,512]{1,0:T(8,128)(2,1)S(1)}, u32[]{:S(2)}, u32[]{:S(2)}) collective-permute-start(bf16[512,512]{1,0:T(8,128)(2,1)S(1)} %get-tuple-element.233), channel_id=1, source_target_pairs={{0,16},{1,17},{8,24},{9,25},{22,6},{23,7},{30,14},{31,15}} | collective-permute-start | bytes 1572872 | tf_op jit(solution)/shard_map/ppermute | solution.py:31
  152.2 22.9 %collective-permute-start.18 = (bf16[512,512]{1,0:T(8,128)(2,1)S(1)}, bf16[512,512]{1,0:T(8,128)(2,1)}, u32[]{:S(2)}, u32[]{:S(2)}) collective-permute-start(bf16[512,512]{1,0:T(8,128)(2,1)S(1)} %add_convert_fusion.7), channel_id=1, source_target_pairs={{6,22},{7,23},{18,2},{19,3},{28,12},{29,13}} | collective-permute-start | bytes 1572872 | tf_op jit(solution)/shard_map/ppermute | solution.py:31
  156.9 19.7 %collective-permute-start.15 = (bf16[512,512]{1,0:T(8,128)(2,1)S(1)}, bf16[512,512]{1,0:T(8,128)(2,1)}, u32[]{:S(2)}, u32[]{:S(2)}) collective-permute-start(bf16[512,512]{1,0:T(8,128)(2,1)S(1)} %add_convert_fusion.8), channel_id=1, source_target_pairs={{2,10},{3,11},{8,0},{9,1},{22,30},{23,31},{28,20},{29,21}} | collective-permute-start | bytes 1572872 | tf_op jit(solution)/shard_map/ppermute | solution.py:31
  168.2 14.4 %collective-permute-start.31 = (bf16[512,512]{1,0:T(8,128)(2,1)S(1)}, bf16[512,512]{1,0:T(8,128)(2,1)}, u32[]{:S(2)}, u32[]{:S(2)}) collective-permute-start(bf16[512,512]{1,0:T(8,128)(2,1)S(1)} %add_convert_fusion.3), channel_id=1, source_target_pairs={{0,16},{1,17},{10,26},{11,27},{20,4},{21,5},{30,14},{31,15}} | collective-permute-start | bytes 1572872 | tf_op jit(solution)/shard_map/ppermute | solution.py:31
  176.6 14.7 %collective-permute-start.34 = (bf16[512,512]{1,0:T(8,128)(2,1)}, bf16[512,512]{1,0:T(8,128)(2,1)}, u32[]{:S(2)}, u32[]{:S(2)}) collective-permute-start(bf16[512,512]{1,0:T(8,128)(2,1)} %add_convert_fusion.2), channel_id=1, source_target_pairs={{6,14},{7,15},{12,4},{13,5},{18,26},{19,27},{24,16},{25,17}} | collective-permute-start | bytes 1572872 | tf_op jit(solution)/shard_map/ppermute | solution.py:31
  (48 other events, 479.7 us)

commit v2 on v1

--- a/solution.py
+++ b/solution.py
@@ -10,8 +10,9 @@
 
 AXES = ("aux", "occ")
 CORES = 2
+VMEM_LIMIT = 24 * 1024 * 1024
 ANY = pl.BlockSpec(memory_space=pl.ANY)
-IN_SMEM = pl.BlockSpec(memory_space=pltpu.SMEM)
+IN_HBM = pl.BlockSpec(memory_space=pltpu.HBM)
 IN_VMEM = pl.BlockSpec(memory_space=pltpu.VMEM)
 
 
@@ -31,41 +32,83 @@
         return lax.ppermute(value, AXES, pairs)
 
 
-def half_kernel(lay, share, sources, count_ref, cols_ref, rows_ref, natural_ref, integrals_ref, *refs):
-    pieces, (out_ref, coeff, total, sems) = refs[:sources], refs[sources:]
+def half_kernel(lay, share, sources, mirrored, count_ref, cols_ref, rows_ref, natural_ref, integrals_ref, *refs):
+    pieces, (out_ref, coeff, ints, total, count, cols, rows, natural, found, listed, *sems) = (
+        refs[:sources],
+        refs[sources:],
+    )
+    sems, piece_sems = sems
     own_blocks = total.shape[0]
     part = own_blocks // share
+    small = [
+        pltpu.make_async_copy(source, target, sems.at[n])
+        for n, (source, target) in enumerate(
+            ((count_ref, count), (cols_ref, cols), (rows_ref, rows), (natural_ref, natural), (integrals_ref, ints))
+        )
+    ]
     copies = []
     start = 0
     for n, piece in enumerate(pieces):
         size = piece.shape[0]
-        copies.append(pltpu.make_async_copy(piece, coeff.at[pl.ds(start, size)], sems.at[n]))
+        copies.append(pltpu.make_async_copy(piece, coeff.at[pl.ds(start, size)], piece_sems.at[n]))
         start += size
-    for copy in copies:
+    for copy in small + copies:
         copy.start()
     total[...] = jnp.zeros_like(total)
-    for copy in copies:
+    for copy in small + copies:
         copy.wait()
-    aux_count, slots, block, _ = integrals_ref.shape
+    aux_count, slots, block, _ = ints.shape
     orbitals = coeff.shape[2]
     occ_index = lax.axis_index("occ")
     z, c = occ_index // CORES, occ_index % CORES
-    k = lax.axis_index("aux") % share
-    per_piece = (lay.planes - 1) * part
-
-    def add_slot(slot, carry):
-        natural = natural_ref[cols_ref[0, slot]]
-        source, inner = natural // own_blocks, natural % own_blocks
-        z_off, c_off = (source // CORES) ^ z, (source % CORES) ^ c
+    a = lax.axis_index("aux")
+    k = a % share
+
+    for row in range(own_blocks):
+        found[row] = 0
+
+    def enter(slot, carry):
+        row = rows[0, slot]
+        at = found[row]
+        listed[row, at] = slot
+        found[row] = at + 1
+        return carry
+
+    lax.fori_loop(0, count[0, 0], enter, 0)
+
+    def coeff_block(slot):
+        source = natural[cols[0, slot]]
+        owner, inner = source // own_blocks, source % own_blocks
+        z_off, c_off = (owner // CORES) ^ z, (owner % CORES) ^ c
         k_off, in_part = (inner // part) ^ k, inner % part
         near = c_off * own_blocks + inner
-        away = CORES * own_blocks + (k_off * CORES + c_off) * per_piece + (z_off - 1) * part + in_part
-        piece = coeff[jnp.where(z_off == 0, near, away)]
-        left = jnp.concatenate([integrals_ref[p, slot] for p in range(aux_count)], axis=0)
-        total[rows_ref[0, slot]] += jnp.dot(left, piece, preferred_element_type=jnp.float32)
-        return carry
-
-    lax.fori_loop(0, count_ref[0, 0], add_slot, 0)
+        base = jnp.int32(0)
+        start = CORES * own_blocks
+        for group in plane_groups(lay.planes):
+            inside = (z_off >= group[0]) & (z_off <= group[-1])
+            at = start + ((k_off * CORES + c_off) * len(group) + z_off - group[0]) * part + in_part
+            base = jnp.where(inside, at, base)
+            start += share * CORES * len(group) * part
+        return coeff[jnp.where(z_off == 0, near, base)]
+
+    def ints_block(slot):
+        return jnp.concatenate([ints[p, slot] for p in range(aux_count)], axis=0)
+
+    for row in range(own_blocks):
+        number = found[row]
+        place = row ^ a if mirrored else row
+
+        def add_two(step, carry, row=row, number=number, place=place):
+            one = listed[row, 2 * step]
+            paired = 2 * step + 1 < number
+            two = jnp.where(paired, listed[row, jnp.where(paired, 2 * step + 1, 2 * step)], one)
+            second = ints_block(two)
+            left = jnp.concatenate([ints_block(one), jnp.where(paired, second, jnp.zeros_like(second))], axis=1)
+            right = jnp.concatenate([coeff_block(one), coeff_block(two)], axis=0)
+            total[place] += jnp.dot(left, right, preferred_element_type=jnp.float32)
+            return carry
+
+        lax.fori_loop(0, (number + 1) // 2, add_two, 0)
     for row in range(own_blocks):
         for p in range(aux_count):
             out_ref[pl.ds(row * block, block), pl.ds(p * orbitals, orbitals)] = total[
@@ -73,21 +116,33 @@
             ].astype(jnp.bfloat16)
 
 
-def half_transform(lay, share, own_blocks, integrals, pieces, cols, rows, count, natural):
+def plane_groups(planes):
+    return [list(range(1, 2)), list(range(2, planes))] if planes > 2 else [list(range(1, planes))]
+
+
+def half_transform(lay, share, mirrored, own_blocks, integrals, pieces, cols, rows, count, natural):
     aux_count, slots, block, _ = integrals.shape
     orbitals = pieces[0].shape[2]
     blocks = sum(piece.shape[0] for piece in pieces)
     return pl.pallas_call(
-        functools.partial(half_kernel, lay, share, len(pieces)),
+        functools.partial(half_kernel, lay, share, len(pieces), mirrored),
         out_shape=jax.ShapeDtypeStruct((own_blocks * block, aux_count * orbitals), jnp.bfloat16),
-        in_specs=[IN_SMEM] * 4 + [IN_VMEM] + [ANY] * len(pieces),
+        in_specs=[IN_HBM] * 5 + [ANY] * len(pieces),
         out_specs=IN_VMEM,
         scratch_shapes=[
             pltpu.VMEM((blocks, block, orbitals), jnp.bfloat16),
+            pltpu.VMEM(integrals.shape, integrals.dtype),
             pltpu.VMEM((own_blocks, aux_count * block, orbitals), jnp.float32),
+            pltpu.SMEM(count.shape, count.dtype),
+            pltpu.SMEM(cols.shape, cols.dtype),
+            pltpu.SMEM(rows.shape, rows.dtype),
+            pltpu.SMEM(natural.shape, natural.dtype),
+            pltpu.SMEM((own_blocks,), jnp.int32),
+            pltpu.SMEM((own_blocks, slots), jnp.int32),
+            pltpu.SemaphoreType.DMA((5,)),
             pltpu.SemaphoreType.DMA((len(pieces),)),
         ],
-        compiler_params=pltpu.CompilerParams(vmem_limit_bytes=32 * 1024 * 1024),
+        compiler_params=pltpu.CompilerParams(vmem_limit_bytes=VMEM_LIMIT),
         name="half_transform",
     )(count, cols, rows, natural, integrals, *pieces)
 
@@ -111,6 +166,180 @@
         terms.append(lay.send(total.astype(jnp.bfloat16), where))
         done |= 1 << bit
     return terms
+
+
+ROWS = (((1,), (1,)), ((), ()))
+
+
+def dot_rows(first, second):
+    return lax.dot_general(first, second, ROWS, preferred_element_type=jnp.float32)
+
+
+def plane_rows(held, s, k):
+    per_core = len(held) // CORES
+    whole, near, *rest = held[s * per_core : (s + 1) * per_core]
+    if k == 0:
+        return [whole[...].reshape(-1, whole.shape[2])]
+    return [near[k - 1], rest[k - 1][...].reshape(-1, near.shape[2])]
+
+
+def pair_kernel(distances, *refs):
+    firsts, laters = refs[:distances], refs[distances : 2 * distances]
+    held, outs = refs[2 * distances : -distances], refs[-distances:]
+    n = firsts[0].shape[0]
+    count = laters[0].shape[0] + 1
+    quarters = [jnp.concatenate([first[...] for first in firsts], axis=0)]
+    quarters += [jnp.concatenate([later[k] for later in laters], axis=0) for k in range(count - 1)]
+    for s in range(CORES):
+        start = s * count * n
+        lower = upper = None
+        for k in range(count):
+            parts = [dot_rows(part, quarters[k]) for part in plane_rows(held, s, k)]
+            if k == 0:
+                lower, upper = parts[0][:n], parts[0][n:]
+            else:
+                lower, upper = lower + parts[0], upper + parts[1]
+        for d, out in enumerate(outs):
+            out[pl.ds(start, n), :] = lower[:, d * n : (d + 1) * n].astype(jnp.bfloat16)
+            out[pl.ds(start + n, (count - 1) * n), :] = upper[:, d * n : (d + 1) * n].astype(jnp.bfloat16)
+
+
+def pair_blocks(firsts, laters, held):
+    count, n, _ = held[0].shape
+    distances = len(firsts)
+    shape = jax.ShapeDtypeStruct((CORES * count * n, n), jnp.bfloat16)
+    return pl.pallas_call(
+        functools.partial(pair_kernel, distances),
+        out_shape=[shape] * distances,
+        in_specs=[IN_VMEM] * (2 * distances + len(held)),
+        out_specs=[IN_VMEM] * distances,
+        compiler_params=pltpu.CompilerParams(vmem_limit_bytes=VMEM_LIMIT),
+        name="pair_blocks",
+    )(*firsts, *laters, *held)
+
+
+def own_kernel(*refs):
+    *held, _, out_ref = refs
+    count, n, _ = held[0].shape
+    a = lax.axis_index("aux")
+    occ_index = lax.axis_index("occ")
+    z, c = occ_index // CORES, occ_index % CORES
+
+    @pl.when(a == z)
+    def _():
+        for s in range(CORES):
+            core = c if s == 0 else 1 - c
+            total = None
+            for k in range(count):
+                own = jnp.concatenate(plane_rows(held, 0, k), axis=0)
+                value = jnp.concatenate([dot_rows(part, own) for part in plane_rows(held, s, k)], axis=0)
+                total = value if total is None else total + value
+            for m in range(count):
+                row = pl.multiple_of(core * count * n + (a ^ m) * n, n)
+                for col in range(count):
+                    out_ref[pl.ds(row, n), pl.ds(pl.multiple_of((a ^ col) * n, n), n)] = total[
+                        m * n : (m + 1) * n, col * n : (col + 1) * n
+                    ]
+
+
+def own_block(held, earlier):
+    count, n, _ = held[0].shape
+    return pl.pallas_call(
+        own_kernel,
+        out_shape=jax.ShapeDtypeStruct((CORES * count * n, count * n), jnp.float32),
+        in_specs=[IN_VMEM] * len(held) + [ANY],
+        out_specs=IN_VMEM,
+        compiler_params=pltpu.CompilerParams(vmem_limit_bytes=VMEM_LIMIT),
+        name="own_block",
+    )(*held, earlier)
+
+
+def place_kernel(*refs):
+    *quarters, crossed_ref, own_ref, out_ref = refs
+    count = len(quarters)
+    n = quarters[0].shape[1]
+    width = count * n
+    a = lax.axis_index("aux")
+    occ_index = lax.axis_index("occ")
+    z, c = occ_index // CORES, occ_index % CORES
+    apart = lax.rem(a - z + count, count)
+
+    def tile(row, col, value):
+        out_ref[pl.ds(pl.multiple_of(row, n), n), pl.ds(pl.multiple_of(col, n), n)] = value
+
+    @pl.when(apart == 0)
+    def _():
+        out_ref[...] = own_ref[...]
+
+    @pl.when((apart > 0) & (apart <= count // 2))
+    def _():
+        for k, quarter in enumerate(quarters):
+            for m in range(count):
+                col, rows = (a ^ k ^ m) * n, pl.ds(m * n, n)
+                tile(c * width + (a ^ k) * n, col, quarter[rows, :].astype(jnp.float32).T)
+                tile((1 - c) * width + (a ^ k) * n, col, crossed_ref[k, rows, :].astype(jnp.float32).T)
+
+    @pl.when(apart > count // 2)
+    def _():
+        for k, quarter in enumerate(quarters):
+            for s in range(CORES):
+                core = c if s == 0 else 1 - c
+                for m in range(count):
+                    value = quarter[pl.ds((s * count + m) * n, n), :].astype(jnp.float32)
+                    tile(core * width + (a ^ k ^ m) * n, (a ^ k) * n, value)
+
+
+def place_blocks(quarters, crossed, out):
+    return pl.pallas_call(
+        place_kernel,
+        out_shape=jax.ShapeDtypeStruct(out.shape, out.dtype),
+        in_specs=[IN_VMEM] * (len(quarters) + 2),
+        out_specs=IN_VMEM,
+        compiler_params=pltpu.CompilerParams(vmem_limit_bytes=VMEM_LIMIT),
+        name="place_blocks",
+    )(*quarters, crossed, out)
+
+
+def after(value, *done):
+    return lax.optimization_barrier((value, *done))[0]
+
+
+def mirrored_exchange(lay, half):
+    count, n, _ = half.shape
+    a = lax.axis_index("aux")
+    z = lax.axis_index("occ") // CORES
+    others = range(1, count)
+    other = lambda v: lay.send(v, lambda a_, z_, c_: (a_, z_, 1 - c_))
+    toward = lambda v, k: lay.send(v, lambda a_, z_, c_: (a_ ^ k, z_, c_))
+    below = lambda v: lay.send(v, lambda a_, z_, c_: (a_, (z_ - 1) % count, c_))
+
+    first, later = [half[0]], []
+    near = jnp.stack([toward(half[k], k) for k in others])
+    for d in range(1, count // 2 + 1):
+        first.append(below(first[-1]))
+        later.append(below(after(later[-1] if later else near, first[-1])))
+    rest = [toward(after(jnp.stack([half[k ^ m] for m in others]), near, first[1]), k) for k in others]
+    own = [half, near] + rest
+    held = own + [other(v) for v in own[:-1]] + [other(after(own[-1], later[-1]))]
+
+    blocks = pair_blocks(first[1:], later, held)
+    apart = dict(enumerate(blocks, 1))
+    for d in range(1, (count + 1) // 2):
+        apart[count - d] = lay.send(apart[d], lambda a_, z_, c_: (a_, (z_ + d) % count, c_))
+    out = own_block(held, blocks[0])
+    apart[count - 1] = after(apart[count - 1], out)
+
+    quarters = []
+    for k in range(count):
+        distance = lax.rem((a ^ k) - z + count, count)
+        value = apart[1]
+        for d in range(2, count):
+            value = jnp.where(distance == d, apart[d], value)
+        if k:
+            value = lay.send(value, lambda a_, z_, c_: (a_ ^ k, z_, c_) if a_ ^ k != z_ else None)
+        quarters.append(value)
+    crossed = other(jnp.stack([q[count * n :] for q in quarters]))
+    return place_blocks(quarters, crossed, out)
 
 
 def local(lay, integrals, coefficients, pair_rows, pair_cols, pair_count, row_blocks):
@@ -128,14 +357,19 @@
     part = own_blocks // share
     blocks = coefficients.reshape(own_blocks, block, orbitals)
     mine = lax.dynamic_slice_in_dim(blocks, (a % share) * part, part, 0)
-    far = [lay.send(mine, lambda a_, z_, c_, d=d: (a_, z_ ^ d, c_)) for d in range(1, planes)]
-    far = jnp.concatenate(far, axis=0)
-    spread = [far] + [lay.send(far, lambda a_, z_, c_, k=k: (a_ ^ k, z_, c_)) for k in range(1, share)]
     other = lambda v: lay.send(v, lambda a_, z_, c_: (a_, z_, 1 - c_))
     pieces = [blocks, other(blocks)]
-    for piece in spread:
-        pieces += [piece, other(piece)]
-    half = half_transform(lay, share, own_blocks, integrals, pieces, pair_cols, pair_rows, pair_count, row_blocks)
+    for group in plane_groups(planes):
+        far = [lay.send(mine, lambda a_, z_, c_, d=d: (a_, z_ ^ d, c_)) for d in group]
+        far = jnp.concatenate(far, axis=0) if len(far) > 1 else far[0]
+        for k in range(share):
+            piece = lay.send(far, lambda a_, z_, c_, k=k: (a_ ^ k, z_, c_)) if k else far
+            pieces += [piece, other(piece)]
+    mirrored = lay.aux == planes == own_blocks and planes % 2 == 0
+    half = half_transform(lay, share, mirrored, own_blocks, integrals, pieces, pair_cols, pair_rows, pair_count, row_blocks)
+
+    if mirrored:
+        return mirrored_exchange(lay, half.reshape(own_blocks, block, -1))
 
     out_blocks = block_total * block // lay.aux // width
     x_first, y_first = tuple(range(lay.bits)), tuple(reversed(range(lay.bits)))

time: 210 us -> 127 us (0.60); the launches traced: 207 us -> 126 us
  starting transfers between devices: 90.3 us -> 49.7 us
  waiting for transfers between devices: 78.6 us -> 51.4 us
  other arithmetic: 9.79 us -> 1.45 us
  matrix products: 8.29 us -> 0 us
  Pallas kernels: 3.43 us -> 10.9 us
  local copies, waits for them, and re-layouts: 15 us -> 11.5 us
    ppermute x42 -> x38, starting transfers between devices: 90.3 us -> 49.7 us  [send(): return lax.ppermute(value, AXES, pairs)]
    ppermute x42 -> x38, waiting for transfers between devices: 78.6 us -> 51.4 us  [send(): return lax.ppermute(value, AXES, pairs)]
    dot_general x10 -> x0, matrix products: 8.29 us -> none  [product(): lax.dot_general(first, second, (((1,), (1,)), ((), ())), preferred_elemen...]
    pallas_call x1 -> x4, Pallas kernels: 3.43 us -> 10.9 us  [the longest x1 6.19 us: half_transform(): pl.pallas_call(functools.partial(half_kernel, lay, share, len(pieces), mi...]
    cond x10 -> x0, local copies, waits for them, and re-layouts: 7.43 us -> none
    convert_element_type x10 -> x0, other arithmetic: 5.59 us -> none  [reduce_to_owner(): terms.append(lay.send(total.astype(jnp.bfloat16), where))]
    unnamed x58 -> x35, local copies, waits for them, and re-layouts: 6.62 us -> 10.4 us
    add x1 -> x0, other arithmetic: 2.54 us -> none  [local(): x + y.astype(jnp.float32)]
  transfers between devices with their start and end apart: 42 -> 38, of which waited for: 17 -> 13; matrix products, arithmetic and copies ran while one was open for 7% -> 0% of each run, Pallas kernels for 0% -> 0%
where the time goes in v2:
time: 127 us; the launch traced here: 126 us
  waiting for transfers between devices  51.4 us (40%)
  starting transfers between devices  49.7 us (39%)
  local copies, waits for them, and re-layouts  11.5 us (9%)
  Pallas kernels  10.9 us (9%)
  other arithmetic  1.45 us (1%)
    ppermute x38, waiting for transfers between devices, send(): return lax.ppermute(value, AXES, pairs)  51.4 us
    ppermute x38, starting transfers between devices, send(): return lax.ppermute(value, AXES, pairs)  49.7 us
    unnamed x35, local copies, waits for them, and re-layouts  10.4 us
    pallas_call x1, Pallas kernels, half_transform(): pl.pallas_call(functools.partial(half_kernel, lay, share, len(pieces), mi...  6.19 us
    pallas_call x1, Pallas kernels, pair_blocks(): pl.pallas_call(functools.partial(pair_kernel, distances), out_shape=[shap...  2.96 us
  transfers between devices with their start and end apart: 38, of which 13 were waited for; matrix products, arithmetic and copies ran while one was open for 0% of the time, Pallas kernels for 0%

profile of v2, /device:TPU:5, one launch (start us, length us, event | category | flops | bytes accessed | tf_op | source)
XLA Modules:
  0.0 125.8 jit_solution(17394546274194390401)
XLA Ops:
  2.3 2.3 %collective-permute-start.9 = (bf16[1,128,384]{2,1,0:T(8,128)(2,1)S(1)}, bf16[1,128,384]{2,1,0:T(8,128)(2,1)S(1)}, u32[]{:S(2)}, u32[]{:S(2)}) collective-permute-start(bf16[1,128,384]{2,1,0:T(8,128)(2,1)S(1)} %constant_dynamic-slice_fusion), channel_id=1, source_target_pairs={{0,4},{1,5},{2,6},{3,7},{4,0},{5,1},{6,2},{7,3},{8,12},{9,13},{10,... | collective-permute-start | bytes 294920 | tf_op jit(solution)/shard_map/ppermute | solution.py:32
  7.2 6.4 %collective-permute-start.2 = (bf16[1,128,384]{2,1,0:T(8,128)(2,1)S(1)}, bf16[1,128,384]{2,1,0:T(8,128)(2,1)S(1)}, u32[]{:S(2)}, u32[]{:S(2)}) collective-permute-start(bf16[1,128,384]{2,1,0:T(8,128)(2,1)S(1)} %collective-permute-done.1.refs_2_), channel_id=1, source_target_pairs={{0,1},{1,0},{2,3},{3,2},{4,5},{5,4},{6,7},{7,6},{8,9},{9,8},{10,11... | collective-permute-start | bytes 294920 | tf_op jit(solution)/shard_map/ppermute | solution.py:32
  17.5 2.8 %collective-permute-done.12.refs_12_ = bf16[2,128,384]{2,1,0:T(8,128)(2,1)S(1)} collective-permute-done((bf16[2,128,384]{2,1,0:T(8,128)(2,1)S(1)}, bf16[2,128,384]{2,1,0:T(8,128)(2,1)S(1)}, u32[]{:S(2)}, u32[]{:S(2)}) %collective-permute-start.12) | collective-permute-done | bytes 196640 | tf_op jit(solution)/shard_map/ppermute | solution.py:32
  21.5 4.3 %collective-permute-done.14.refs_14_ = bf16[2,128,384]{2,1,0:T(8,128)(2,1)S(1)} collective-permute-done((bf16[2,128,384]{2,1,0:T(8,128)(2,1)S(1)}, bf16[2,128,384]{2,1,0:T(8,128)(2,1)S(1)}, u32[]{:S(2)}, u32[]{:S(2)}) %collective-permute-start.14) | collective-permute-done | bytes 196640 | tf_op jit(solution)/shard_map/ppermute | solution.py:32
  29.1 1.4 %copy-done.10 = bf16[2,24,128,128]{3,2,1,0:T(8,128)(2,1)S(1)} copy-done((bf16[2,24,128,128]{3,2,1,0:T(8,128)(2,1)S(1)}, bf16[2,24,128,128]{3,2,1,0:T(8,128)(2,1)}, u32[]{:S(2)}) %copy-start.10) | copy-done | bytes 1572888
  33.4 6.2 %half_transform.1 = bf16[512,768]{1,0:T(8,128)(2,1)S(1)} custom-call(s32[1,1]{1,0:T(1,128)S(6)} %copy.8.count_ref, s32[1,24]{1,0:T(1,128)S(1)} %copy-done.14, s32[1,24]{1,0:T(1,128)S(1)} %copy-done.15, s32[32]{0:T(128)S(1)} %copy-done.16, bf16[2,24,128,128]{3,2,1,0:T(8,128)(2,1)S(1)} %copy-done.10, bf16[4,128,384]{2,1,0:T(8,128)(2,1)S(1)} %bitcast.26, ...), custom_call_target="tpu_custom_call" | custom-call | tf_op jit(solution)/shard_map/half_transform/pallas_call | solution.py:127
  40.6 1.8 %collective-permute-start.22 = (bf16[128,768]{1,0:T(8,128)(2,1)S(1)}, bf16[128,768]{1,0:T(8,128)(2,1)S(1)}, u32[]{:S(2)}, u32[]{:S(2)}) collective-permute-start(bf16[128,768]{1,0:T(8,128)(2,1)S(1)} %get-tuple-element.31), channel_id=1, source_target_pairs={{0,24},{1,25},{2,26},{3,27},{4,28},{5,29},{6,30},{7,31},{8,16},{9,... | collective-permute-start | bytes 589832 | tf_op jit(solution)/shard_map/ppermute | solution.py:32
  42.5 2.8 %collective-permute-start.18 = (bf16[128,768]{1,0:T(8,128)(2,1)S(1)}, bf16[128,768]{1,0:T(8,128)(2,1)S(1)}, u32[]{:S(2)}, u32[]{:S(2)}) collective-permute-start(bf16[128,768]{1,0:T(8,128)(2,1)S(1)} %get-tuple-element.34), channel_id=1, source_target_pairs={{0,6},{1,7},{2,0},{3,1},{4,2},{5,3},{6,4},{7,5},{8,14},{9,15},{10,... | collective-permute-start | bytes 589832 | tf_op jit(solution)/shard_map/ppermute | solution.py:32
  45.3 4.9 %collective-permute-done.22 = bf16[128,768]{1,0:T(8,128)(2,1)S(1)} collective-permute-done((bf16[128,768]{1,0:T(8,128)(2,1)S(1)}, bf16[128,768]{1,0:T(8,128)(2,1)S(1)}, u32[]{:S(2)}, u32[]{:S(2)}) %collective-permute-start.22) | collective-permute-done | bytes 196640 | tf_op jit(solution)/shard_map/ppermute | solution.py:32
  50.2 3.7 %collective-permute-start.23 = (bf16[3,128,768]{2,1,0:T(8,128)(2,1)S(1)}, bf16[3,128,768]{2,1,0:T(8,128)(2,1)S(1)}, u32[]{:S(2)}, u32[]{:S(2)}) collective-permute-start(bf16[3,128,768]{2,1,0:T(8,128)(2,1)S(1)} %pad_maximum_fusion.refs_5_.refs_1_), channel_id=1, source_target_pairs={{0,6},{1,7},{2,0},{3,1},{4,2},{5,3},{6,4},{7,5},{8,14},{9,15},{10,... | collective-permute-start | bytes 1769480 | tf_op jit(solution)/shard_map/ppermute | solution.py:32
  55.1 1.5 %collective-permute-start.27 = (bf16[3,128,768]{2,1,0:T(8,128)(2,1)S(1)}, bf16[3,128,768]{2,1,0:T(8,128)(2,1)S(1)}, u32[]{:S(2)}, u32[]{:S(2)}) collective-permute-start(bf16[3,128,768]{2,1,0:T(8,128)(2,1)S(1)} %get-tuple-element.18), channel_id=1, source_target_pairs={{0,24},{1,25},{2,26},{3,27},{4,28},{5,29},{6,30},{7,31},{8,16},{9,... | collective-permute-start | bytes 1769480 | tf_op jit(solution)/shard_map/ppermute | solution.py:32
  57.8 12.7 %collective-permute-done.19.refs_1_ = bf16[128,768]{1,0:T(8,128)(2,1)S(1)} collective-permute-done((bf16[128,768]{1,0:T(8,128)(2,1)S(1)}, bf16[128,768]{1,0:T(8,128)(2,1)S(1)}, u32[]{:S(2)}, u32[]{:S(2)}) %collective-permute-start.19) | collective-permute-done | bytes 196640 | tf_op jit(solution)/shard_map/ppermute | solution.py:32
  70.5 4.0 %collective-permute-start.24 = (bf16[3,128,768]{2,1,0:T(8,128)(2,1)S(1)}, bf16[3,128,768]{2,1,0:T(8,128)(2,1)S(1)}, u32[]{:S(2)}, u32[]{:S(2)}) collective-permute-start(bf16[3,128,768]{2,1,0:T(8,128)(2,1)S(1)} %collective-permute-done.23.refs_2_), channel_id=1, source_target_pairs={{0,6},{1,7},{2,0},{3,1},{4,2},{5,3},{6,4},{7,5},{8,14},{9,15},{10,... | collective-permute-start | bytes 1769480 | tf_op jit(solution)/shard_map/ppermute | solution.py:32
  74.5 1.5 %collective-permute-start.28 = (bf16[4,128,768]{2,1,0:T(8,128)(2,1)S(1)}, bf16[4,128,768]{2,1,0:T(8,128)(2,1)S(1)}, u32[]{:S(2)}, u32[]{:S(2)}) collective-permute-start(bf16[4,128,768]{2,1,0:T(8,128)(2,1)S(1)} %bitcast.21), channel_id=1, source_target_pairs={{0,1},{1,0},{2,3},{3,2},{4,5},{5,4},{6,7},{7,6},{8,9},{9,8},{10,11... | collective-permute-start | bytes 2359304 | tf_op jit(solution)/shard_map/ppermute | solution.py:32
  76.0 7.9 %collective-permute-done.26.refs_7_.refs_3_ = bf16[3,128,768]{2,1,0:T(8,128)(2,1)S(1)} collective-permute-done((bf16[3,128,768]{2,1,0:T(8,128)(2,1)S(1)}, bf16[3,128,768]{2,1,0:T(8,128)(2,1)S(1)}, u32[]{:S(2)}, u32[]{:S(2)}) %collective-permute-start.26) | collective-permute-done | bytes 589856 | tf_op jit(solution)/shard_map/ppermute | solution.py:32
  85.9 2.2 %collective-permute-start.32 = (bf16[3,128,768]{2,1,0:T(8,128)(2,1)S(1)}, bf16[3,128,768]{2,1,0:T(8,128)(2,1)S(1)}, u32[]{:S(2)}, u32[]{:S(2)}) collective-permute-start(bf16[3,128,768]{2,1,0:T(8,128)(2,1)S(1)} %collective-permute-done.27.refs_8_.refs_4_), channel_id=1, source_target_pairs={{0,1},{1,0},{2,3},{3,2},{4,5},{5,4},{6,7},{7,6},{8,9},{9,8},{10,11... | collective-permute-start | bytes 1769480 | tf_op jit(solution)/shard_map/ppermute | solution.py:32
  88.1 1.6 %collective-permute-done.32.refs_13_.refs_9_ = bf16[3,128,768]{2,1,0:T(8,128)(2,1)S(1)} collective-permute-done((bf16[3,128,768]{2,1,0:T(8,128)(2,1)S(1)}, bf16[3,128,768]{2,1,0:T(8,128)(2,1)S(1)}, u32[]{:S(2)}, u32[]{:S(2)}) %collective-permute-start.32) | collective-permute-done | bytes 589856 | tf_op jit(solution)/shard_map/ppermute | solution.py:32
  89.7 3.0 %pair_blocks.1 = (bf16[1024,128]{1,0:T(8,128)(2,1)}, bf16[1024,128]{1,0:T(8,128)(2,1)S(1)}) custom-call(bf16[128,768]{1,0:T(8,128)(2,1)S(1)} %collective-permute-done.18.refs_0_, bf16[128,768]{1,0:T(8,128)(2,1)S(1)} %collective-permute-done.19.refs_1_, bf16[3,128,768]{2,1,0:T(8,128)(2,1)S(1)} %collective-permute-done.23.refs_2_, ...), custom_call_target="tpu_custom_call" | custom-call | tf_op jit(solution)/shard_map/pair_blocks/pallas_call | solution.py:211
  98.7 5.4 %collective-permute-done.33 = bf16[1024,128]{1,0:T(8,128)(2,1)} collective-permute-done((bf16[1024,128]{1,0:T(8,128)(2,1)}, bf16[1024,128]{1,0:T(8,128)(2,1)}, u32[]{:S(2)}, u32[]{:S(2)}) %collective-permute-start.33) | collective-permute-done | bytes 262176 | tf_op jit(solution)/shard_map/ppermute | solution.py:32
  105.2 1.9 %collective-permute-start.36 = (bf16[1024,128]{1,0:T(8,128)(2,1)S(1)}, bf16[1024,128]{1,0:T(8,128)(2,1)S(1)}, u32[]{:S(2)}, u32[]{:S(2)}) collective-permute-start(bf16[1024,128]{1,0:T(8,128)(2,1)S(1)} %get-tuple-element.23), channel_id=1, source_target_pairs={{0,24},{1,25},{2,26},{3,27},{4,28},{5,29},{8,16},{9,17},{10,18},{1... | collective-permute-start | bytes 786440 | tf_op jit(solution)/shard_map/ppermute | solution.py:32
  108.4 5.2 %collective-permute-start.34 = (bf16[1024,128]{1,0:T(8,128)(2,1)S(1)}, bf16[1024,128]{1,0:T(8,128)(2,1)S(1)}, u32[]{:S(2)}, u32[]{:S(2)}) collective-permute-start(bf16[1024,128]{1,0:T(8,128)(2,1)S(1)} %get-tuple-element.25), channel_id=1, source_target_pairs={{0,8},{1,9},{4,12},{5,13},{6,14},{7,15},{10,2},{11,3},{12,4},{13,5... | collective-permute-start | bytes 786440 | tf_op jit(solution)/shard_map/ppermute | solution.py:32
  114.9 6.9 %collective-permute-done.35.refs_2_ = bf16[1024,128]{1,0:T(8,128)(2,1)S(1)} collective-permute-done((bf16[1024,128]{1,0:T(8,128)(2,1)S(1)}, bf16[1024,128]{1,0:T(8,128)(2,1)S(1)}, u32[]{:S(2)}, u32[]{:S(2)}) %collective-permute-start.35) | collective-permute-done | bytes 262176 | tf_op jit(solution)/shard_map/ppermute | solution.py:32
  122.5 1.5 %collective-permute-done.37.refs_4_ = bf16[4,512,128]{2,1,0:T(8,128)(2,1)S(1)} collective-permute-done((bf16[4,512,128]{2,1,0:T(8,128)(2,1)S(1)}, bf16[4,512,128]{2,1,0:T(8,128)(2,1)S(1)}, u32[]{:S(2)}, u32[]{:S(2)}) %collective-permute-start.37) | collective-permute-done | bytes 524320 | tf_op jit(solution)/shard_map/ppermute | solution.py:32
  124.0 1.8 %place_blocks.1 = f32[1024,512]{1,0:T(8,128)} custom-call(bf16[1024,128]{1,0:T(8,128)(2,1)S(1)} %get-tuple-element.26.refs_0_, bf16[1024,128]{1,0:T(8,128)(2,1)S(1)} %collective-permute-done.34.refs_1_, bf16[1024,128]{1,0:T(8,128)(2,1)S(1)} %collective-permute-done.35.refs_2_, bf16[1024,128]{1,0:T(8,128)(2,1)S(1)} %collective-permute-done.36.refs_3_, ...), custom_call_target="tpu_custom_call" | custom-call | tf_op jit(solution)/shard_map/place_blocks/pallas_call | solution.py:293
  (102 shorter events, 31.3 us)
Async XLA Ops:
  4.6 9.1 %collective-permute-start.10 = (bf16[1,128,384]{2,1,0:T(8,128)(2,1)S(1)}, bf16[1,128,384]{2,1,0:T(8,128)(2,1)S(1)}, u32[]{:S(2)}, u32[]{:S(2)}) collective-permute-start(bf16[1,128,384]{2,1,0:T(8,128)(2,1)S(1)} %constant_dynamic-slice_fusion), channel_id=1, source_target_pairs={{0,6},{1,7},{2,4},{3,5},{4,2},{5,3},{6,0},{7,1},{8,14},{9,15},{10,... | collective-permute-start | bytes 294920 | tf_op jit(solution)/shard_map/ppermute | solution.py:32
  4.6 10.4 %collective-permute-start.3 = (bf16[1,128,384]{2,1,0:T(8,128)(2,1)S(1)}, bf16[1,128,384]{2,1,0:T(8,128)(2,1)S(1)}, u32[]{:S(2)}, u32[]{:S(2)}) collective-permute-start(bf16[1,128,384]{2,1,0:T(8,128)(2,1)S(1)} %collective-permute-done.1.refs_2_), channel_id=1, source_target_pairs={{0,8},{1,9},{2,10},{3,11},{4,12},{5,13},{6,14},{7,15},{8,0},{9,1},... | collective-permute-start | bytes 294920 | tf_op jit(solution)/shard_map/ppermute | solution.py:32
  5.8 9.5 %collective-permute-start.5 = (bf16[1,128,384]{2,1,0:T(8,128)(2,1)S(1)}, bf16[1,128,384]{2,1,0:T(8,128)(2,1)S(1)}, u32[]{:S(2)}, u32[]{:S(2)}) collective-permute-start(bf16[1,128,384]{2,1,0:T(8,128)(2,1)S(1)} %collective-permute-done.1.refs_2_), channel_id=1, source_target_pairs={{0,16},{1,17},{2,18},{3,19},{4,20},{5,21},{6,22},{7,23},{8,24},{9,... | collective-permute-start | bytes 294920 | tf_op jit(solution)/shard_map/ppermute | solution.py:32
  6.0 9.5 %collective-permute-start.7 = (bf16[1,128,384]{2,1,0:T(8,128)(2,1)S(1)}, bf16[1,128,384]{2,1,0:T(8,128)(2,1)S(1)}, u32[]{:S(2)}, u32[]{:S(2)}) collective-permute-start(bf16[1,128,384]{2,1,0:T(8,128)(2,1)S(1)} %collective-permute-done.1.refs_2_), channel_id=1, source_target_pairs={{0,24},{1,25},{2,26},{3,27},{4,28},{5,29},{6,30},{7,31},{8,16},{9,... | collective-permute-start | bytes 294920 | tf_op jit(solution)/shard_map/ppermute | solution.py:32
  7.2 9.5 %collective-permute-start.2 = (bf16[1,128,384]{2,1,0:T(8,128)(2,1)S(1)}, bf16[1,128,384]{2,1,0:T(8,128)(2,1)S(1)}, u32[]{:S(2)}, u32[]{:S(2)}) collective-permute-start(bf16[1,128,384]{2,1,0:T(8,128)(2,1)S(1)} %collective-permute-done.1.refs_2_), channel_id=1, source_target_pairs={{0,1},{1,0},{2,3},{3,2},{4,5},{5,4},{6,7},{7,6},{8,9},{9,8},{10,11... | collective-permute-start | bytes 294920 | tf_op jit(solution)/shard_map/ppermute | solution.py:32
  15.0 14.1 %collective-permute-start = (bf16[4,128,384]{2,1,0:T(8,128)(2,1)}, bf16[4,128,384]{2,1,0:T(8,128)(2,1)S(1)}, u32[]{:S(2)}, u32[]{:S(2)}) collective-permute-start(bf16[4,128,384]{2,1,0:T(8,128)(2,1)} %bitcast.25), channel_id=1, source_target_pairs={{0,1},{1,0},{2,3},{3,2},{4,5},{5,4},{6,7},{7,6},{8,9},{9,8},{10,11... | collective-permute-start | bytes 1179656 | tf_op jit(solution)/shard_map/ppermute | solution.py:32
  15.3 10.5 %collective-permute-start.14 = (bf16[2,128,384]{2,1,0:T(8,128)(2,1)S(1)}, bf16[2,128,384]{2,1,0:T(8,128)(2,1)S(1)}, u32[]{:S(2)}, u32[]{:S(2)}) collective-permute-start(bf16[2,128,384]{2,1,0:T(8,128)(2,1)S(1)} %constant_dynamic-update-slice_fusion.refs_10_), channel_id=1, source_target_pairs={{0,16},{1,17},{2,18},{3,19},{4,20},{5,21},{6,22},{7,23},{8,24},{9,... | collective-permute-start | bytes 589832 | tf_op jit(solution)/shard_map/ppermute | solution.py:32
  15.5 11.3 %collective-permute-start.16 = (bf16[2,128,384]{2,1,0:T(8,128)(2,1)S(1)}, bf16[2,128,384]{2,1,0:T(8,128)(2,1)S(1)}, u32[]{:S(2)}, u32[]{:S(2)}) collective-permute-start(bf16[2,128,384]{2,1,0:T(8,128)(2,1)S(1)} %constant_dynamic-update-slice_fusion.refs_10_), channel_id=1, source_target_pairs={{0,24},{1,25},{2,26},{3,27},{4,28},{5,29},{6,30},{7,31},{8,16},{9,... | collective-permute-start | bytes 589832 | tf_op jit(solution)/shard_map/ppermute | solution.py:32
  16.7 10.1 %collective-permute-start.11 = (bf16[2,128,384]{2,1,0:T(8,128)(2,1)S(1)}, bf16[2,128,384]{2,1,0:T(8,128)(2,1)S(1)}, u32[]{:S(2)}, u32[]{:S(2)}) collective-permute-start(bf16[2,128,384]{2,1,0:T(8,128)(2,1)S(1)} %constant_dynamic-update-slice_fusion.refs_10_), channel_id=1, source_target_pairs={{0,1},{1,0},{2,3},{3,2},{4,5},{5,4},{6,7},{7,6},{8,9},{9,8},{10,11... | collective-permute-start | bytes 589832 | tf_op jit(solution)/shard_map/ppermute | solution.py:32
  20.3 7.0 %collective-permute-start.4 = (bf16[1,128,384]{2,1,0:T(8,128)(2,1)S(1)}, bf16[1,128,384]{2,1,0:T(8,128)(2,1)S(1)}, u32[]{:S(2)}, u32[]{:S(2)}) collective-permute-start(bf16[1,128,384]{2,1,0:T(8,128)(2,1)S(1)} %collective-permute-done.3.refs_4_), channel_id=1, source_target_pairs={{0,1},{1,0},{2,3},{3,2},{4,5},{5,4},{6,7},{7,6},{8,9},{9,8},{10,11... | collective-permute-start | bytes 294920 | tf_op jit(solution)/shard_map/ppermute | solution.py:32
  40.6 9.5 %collective-permute-start.22 = (bf16[128,768]{1,0:T(8,128)(2,1)S(1)}, bf16[128,768]{1,0:T(8,128)(2,1)S(1)}, u32[]{:S(2)}, u32[]{:S(2)}) collective-permute-start(bf16[128,768]{1,0:T(8,128)(2,1)S(1)} %get-tuple-element.31), channel_id=1, source_target_pairs={{0,24},{1,25},{2,26},{3,27},{4,28},{5,29},{6,30},{7,31},{8,16},{9,... | collective-permute-start | bytes 589832 | tf_op jit(solution)/shard_map/ppermute | solution.py:32
  42.5 7.7 %collective-permute-start.18 = (bf16[128,768]{1,0:T(8,128)(2,1)S(1)}, bf16[128,768]{1,0:T(8,128)(2,1)S(1)}, u32[]{:S(2)}, u32[]{:S(2)}) collective-permute-start(bf16[128,768]{1,0:T(8,128)(2,1)S(1)} %get-tuple-element.34), channel_id=1, source_target_pairs={{0,6},{1,7},{2,0},{3,1},{4,2},{5,3},{6,4},{7,5},{8,14},{9,15},{10,... | collective-permute-start | bytes 589832 | tf_op jit(solution)/shard_map/ppermute | solution.py:32
  50.2 20.3 %collective-permute-start.23 = (bf16[3,128,768]{2,1,0:T(8,128)(2,1)S(1)}, bf16[3,128,768]{2,1,0:T(8,128)(2,1)S(1)}, u32[]{:S(2)}, u32[]{:S(2)}) collective-permute-start(bf16[3,128,768]{2,1,0:T(8,128)(2,1)S(1)} %pad_maximum_fusion.refs_5_.refs_1_), channel_id=1, source_target_pairs={{0,6},{1,7},{2,0},{3,1},{4,2},{5,3},{6,4},{7,5},{8,14},{9,15},{10,... | collective-permute-start | bytes 1769480 | tf_op jit(solution)/shard_map/ppermute | solution.py:32
  54.0 16.5 %collective-permute-start.19 = (bf16[128,768]{1,0:T(8,128)(2,1)S(1)}, bf16[128,768]{1,0:T(8,128)(2,1)S(1)}, u32[]{:S(2)}, u32[]{:S(2)}) collective-permute-start(bf16[128,768]{1,0:T(8,128)(2,1)S(1)} %collective-permute-done.18.refs_0_), channel_id=1, source_target_pairs={{0,6},{1,7},{2,0},{3,1},{4,2},{5,3},{6,4},{7,5},{8,14},{9,15},{10,... | collective-permute-start | bytes 589832 | tf_op jit(solution)/shard_map/ppermute | solution.py:32
  55.1 20.9 %collective-permute-start.27 = (bf16[3,128,768]{2,1,0:T(8,128)(2,1)S(1)}, bf16[3,128,768]{2,1,0:T(8,128)(2,1)S(1)}, u32[]{:S(2)}, u32[]{:S(2)}) collective-permute-start(bf16[3,128,768]{2,1,0:T(8,128)(2,1)S(1)} %get-tuple-element.18), channel_id=1, source_target_pairs={{0,24},{1,25},{2,26},{3,27},{4,28},{5,29},{6,30},{7,31},{8,16},{9,... | collective-permute-start | bytes 1769480 | tf_op jit(solution)/shard_map/ppermute | solution.py:32
  56.6 27.3 %collective-permute-start.26 = (bf16[3,128,768]{2,1,0:T(8,128)(2,1)S(1)}, bf16[3,128,768]{2,1,0:T(8,128)(2,1)S(1)}, u32[]{:S(2)}, u32[]{:S(2)}) collective-permute-start(bf16[3,128,768]{2,1,0:T(8,128)(2,1)S(1)} %get-tuple-element.17), channel_id=1, source_target_pairs={{0,16},{1,17},{2,18},{3,19},{4,20},{5,21},{6,22},{7,23},{8,24},{9,... | collective-permute-start | bytes 1769480 | tf_op jit(solution)/shard_map/ppermute | solution.py:32
  57.5 26.9 %collective-permute-start.25 = (bf16[3,128,768]{2,1,0:T(8,128)(2,1)S(1)}, bf16[3,128,768]{2,1,0:T(8,128)(2,1)S(1)}, u32[]{:S(2)}, u32[]{:S(2)}) collective-permute-start(bf16[3,128,768]{2,1,0:T(8,128)(2,1)S(1)} %get-tuple-element.16), channel_id=1, source_target_pairs={{0,8},{1,9},{2,10},{3,11},{4,12},{5,13},{6,14},{7,15},{8,0},{9,1},... | collective-permute-start | bytes 1769480 | tf_op jit(solution)/shard_map/ppermute | solution.py:32
  70.5 15.4 %collective-permute-start.24 = (bf16[3,128,768]{2,1,0:T(8,128)(2,1)S(1)}, bf16[3,128,768]{2,1,0:T(8,128)(2,1)S(1)}, u32[]{:S(2)}, u32[]{:S(2)}) collective-permute-start(bf16[3,128,768]{2,1,0:T(8,128)(2,1)S(1)} %collective-permute-done.23.refs_2_), channel_id=1, source_target_pairs={{0,6},{1,7},{2,0},{3,1},{4,2},{5,3},{6,4},{7,5},{8,14},{9,15},{10,... | collective-permute-start | bytes 1769480 | tf_op jit(solution)/shard_map/ppermute | solution.py:32
  74.5 13.6 %collective-permute-start.28 = (bf16[4,128,768]{2,1,0:T(8,128)(2,1)S(1)}, bf16[4,128,768]{2,1,0:T(8,128)(2,1)S(1)}, u32[]{:S(2)}, u32[]{:S(2)}) collective-permute-start(bf16[4,128,768]{2,1,0:T(8,128)(2,1)S(1)} %bitcast.21), channel_id=1, source_target_pairs={{0,1},{1,0},{2,3},{3,2},{4,5},{5,4},{6,7},{7,6},{8,9},{9,8},{10,11... | collective-permute-start | bytes 2359304 | tf_op jit(solution)/shard_map/ppermute | solution.py:32
  76.0 12.0 %collective-permute-start.29 = (bf16[3,128,768]{2,1,0:T(8,128)(2,1)S(1)}, bf16[3,128,768]{2,1,0:T(8,128)(2,1)S(1)}, u32[]{:S(2)}, u32[]{:S(2)}) collective-permute-start(bf16[3,128,768]{2,1,0:T(8,128)(2,1)S(1)} %pad_maximum_fusion.refs_5_.refs_1_), channel_id=1, source_target_pairs={{0,1},{1,0},{2,3},{3,2},{4,5},{5,4},{6,7},{7,6},{8,9},{9,8},{10,11... | collective-permute-start | bytes 1769480 | tf_op jit(solution)/shard_map/ppermute | solution.py:32
  93.3 10.7 %collective-permute-start.33 = (bf16[1024,128]{1,0:T(8,128)(2,1)}, bf16[1024,128]{1,0:T(8,128)(2,1)}, u32[]{:S(2)}, u32[]{:S(2)}) collective-permute-start(bf16[1024,128]{1,0:T(8,128)(2,1)} %get-tuple-element.20.refs_10_), channel_id=1, source_target_pairs={{0,2},{1,3},{2,4},{3,5},{4,6},{5,7},{6,0},{7,1},{8,10},{9,11},{10,... | collective-permute-start | bytes 786440 | tf_op jit(solution)/shard_map/ppermute | solution.py:32
  105.2 9.8 %collective-permute-start.36 = (bf16[1024,128]{1,0:T(8,128)(2,1)S(1)}, bf16[1024,128]{1,0:T(8,128)(2,1)S(1)}, u32[]{:S(2)}, u32[]{:S(2)}) collective-permute-start(bf16[1024,128]{1,0:T(8,128)(2,1)S(1)} %get-tuple-element.23), channel_id=1, source_target_pairs={{0,24},{1,25},{2,26},{3,27},{4,28},{5,29},{8,16},{9,17},{10,18},{1... | collective-permute-start | bytes 786440 | tf_op jit(solution)/shard_map/ppermute | solution.py:32
  107.1 14.7 %collective-permute-start.35 = (bf16[1024,128]{1,0:T(8,128)(2,1)S(1)}, bf16[1024,128]{1,0:T(8,128)(2,1)S(1)}, u32[]{:S(2)}, u32[]{:S(2)}) collective-permute-start(bf16[1024,128]{1,0:T(8,128)(2,1)S(1)} %get-tuple-element.24), channel_id=1, source_target_pairs={{0,16},{1,17},{2,18},{3,19},{6,22},{7,23},{8,24},{9,25},{10,26},{1... | collective-permute-start | bytes 786440 | tf_op jit(solution)/shard_map/ppermute | solution.py:32
  108.4 13.4 %collective-permute-start.34 = (bf16[1024,128]{1,0:T(8,128)(2,1)S(1)}, bf16[1024,128]{1,0:T(8,128)(2,1)S(1)}, u32[]{:S(2)}, u32[]{:S(2)}) collective-permute-start(bf16[1024,128]{1,0:T(8,128)(2,1)S(1)} %get-tuple-element.25), channel_id=1, source_target_pairs={{0,8},{1,9},{4,12},{5,13},{6,14},{7,15},{10,2},{11,3},{12,4},{13,5... | collective-permute-start | bytes 786440 | tf_op jit(solution)/shard_map/ppermute | solution.py:32
  (31 other events, 90.0 us)

commit v3 on v1

--- a/solution.py
+++ b/solution.py
@@ -10,6 +10,8 @@
 
 AXES = ("aux", "occ")
 CORES = 2
+VMEM_LIMIT = 12 * 1024 * 1024
+VMEM_MOST = 60 * 1024 * 1024
 ANY = pl.BlockSpec(memory_space=pl.ANY)
 IN_SMEM = pl.BlockSpec(memory_space=pltpu.SMEM)
 IN_VMEM = pl.BlockSpec(memory_space=pltpu.VMEM)
@@ -31,65 +33,305 @@
         return lax.ppermute(value, AXES, pairs)
 
 
-def half_kernel(lay, share, sources, count_ref, cols_ref, rows_ref, natural_ref, integrals_ref, *refs):
-    pieces, (out_ref, coeff, total, sems) = refs[:sources], refs[sources:]
+def half_kernel(lay, share, sources, mirrored, meta, ints, *refs):
+    pieces, (*outs, coeff, total, found, listed) = refs[:sources], refs[sources:]
     own_blocks = total.shape[0]
     part = own_blocks // share
-    copies = []
     start = 0
-    for n, piece in enumerate(pieces):
-        size = piece.shape[0]
-        copies.append(pltpu.make_async_copy(piece, coeff.at[pl.ds(start, size)], sems.at[n]))
-        start += size
-    for copy in copies:
-        copy.start()
+    for piece in pieces:
+        coeff[pl.ds(start, piece.shape[0])] = piece[...]
+        start += piece.shape[0]
+    aux_count, slots, block, _ = ints.shape
+    cols_at, rows_at, natural_at = 1, 1 + slots, 1 + 2 * slots
     total[...] = jnp.zeros_like(total)
-    for copy in copies:
-        copy.wait()
-    aux_count, slots, block, _ = integrals_ref.shape
     orbitals = coeff.shape[2]
     occ_index = lax.axis_index("occ")
     z, c = occ_index // CORES, occ_index % CORES
-    k = lax.axis_index("aux") % share
-    per_piece = (lay.planes - 1) * part
-
-    def add_slot(slot, carry):
-        natural = natural_ref[cols_ref[0, slot]]
-        source, inner = natural // own_blocks, natural % own_blocks
-        z_off, c_off = (source // CORES) ^ z, (source % CORES) ^ c
+    a = lax.axis_index("aux")
+    k = a % share
+
+    for row in range(own_blocks):
+        found[row] = 0
+
+    def enter(slot, carry):
+        row = meta[0, rows_at + slot]
+        at = found[row]
+        listed[row, at] = slot
+        found[row] = at + 1
+        return carry
+
+    lax.fori_loop(0, meta[0, 0], enter, 0)
+
+    def coeff_block(slot):
+        source = meta[0, natural_at + meta[0, cols_at + slot]]
+        owner, inner = source // own_blocks, source % own_blocks
+        z_off, c_off = (owner // CORES) ^ z, (owner % CORES) ^ c
         k_off, in_part = (inner // part) ^ k, inner % part
         near = c_off * own_blocks + inner
-        away = CORES * own_blocks + (k_off * CORES + c_off) * per_piece + (z_off - 1) * part + in_part
-        piece = coeff[jnp.where(z_off == 0, near, away)]
-        left = jnp.concatenate([integrals_ref[p, slot] for p in range(aux_count)], axis=0)
-        total[rows_ref[0, slot]] += jnp.dot(left, piece, preferred_element_type=jnp.float32)
-        return carry
-
-    lax.fori_loop(0, count_ref[0, 0], add_slot, 0)
+        base = jnp.int32(0)
+        start = CORES * own_blocks
+        for group in plane_groups(lay.planes):
+            inside = (z_off >= group[0]) & (z_off <= group[-1])
+            at = start + ((k_off * CORES + c_off) * len(group) + z_off - group[0]) * part + in_part
+            base = jnp.where(inside, at, base)
+            start += share * CORES * len(group) * part
+        return coeff[jnp.where(z_off == 0, near, base)]
+
+    def ints_block(slot):
+        return jnp.concatenate([ints[p, slot] for p in range(aux_count)], axis=0)
+
+    for row in range(own_blocks):
+        number = found[row]
+        place = row ^ a if mirrored else row
+
+        def add_two(step, carry, row=row, number=number, place=place):
+            one = listed[row, 2 * step]
+            paired = 2 * step + 1 < number
+            two = jnp.where(paired, listed[row, jnp.where(paired, 2 * step + 1, 2 * step)], one)
+            second = ints_block(two)
+            left = jnp.concatenate([ints_block(one), jnp.where(paired, second, jnp.zeros_like(second))], axis=1)
+            right = jnp.concatenate([coeff_block(one), coeff_block(two)], axis=0)
+            total[place] += jnp.dot(left, right, preferred_element_type=jnp.float32)
+            return carry
+
+        lax.fori_loop(0, (number + 1) // 2, add_two, 0)
     for row in range(own_blocks):
         for p in range(aux_count):
-            out_ref[pl.ds(row * block, block), pl.ds(p * orbitals, orbitals)] = total[
-                row, pl.ds(p * block, block), :
-            ].astype(jnp.bfloat16)
-
-
-def half_transform(lay, share, own_blocks, integrals, pieces, cols, rows, count, natural):
+            value = total[row, pl.ds(p * block, block), :].astype(jnp.bfloat16)
+            columns = pl.ds(p * orbitals, orbitals)
+            outs[0][row, :, columns] = value
+            if mirrored:
+                outs[1 + row][0, :, columns] = value
+                for place in range(1, own_blocks):
+                    if place != row:
+                        outs[own_blocks + place][(place ^ row) - 1, :, columns] = value
+
+
+def plane_groups(planes):
+    return [list(range(1, 2)), list(range(2, planes))] if planes > 2 else [list(range(1, planes))]
+
+
+def half_transform(lay, share, mirrored, own_blocks, integrals, pieces, meta):
     aux_count, slots, block, _ = integrals.shape
     orbitals = pieces[0].shape[2]
     blocks = sum(piece.shape[0] for piece in pieces)
+    sizes = [own_blocks]
+    if mirrored:
+        sizes += [1] * own_blocks + [own_blocks - 1] * (own_blocks - 1)
     return pl.pallas_call(
-        functools.partial(half_kernel, lay, share, len(pieces)),
-        out_shape=jax.ShapeDtypeStruct((own_blocks * block, aux_count * orbitals), jnp.bfloat16),
-        in_specs=[IN_SMEM] * 4 + [IN_VMEM] + [ANY] * len(pieces),
-        out_specs=IN_VMEM,
+        functools.partial(half_kernel, lay, share, len(pieces), mirrored),
+        out_shape=[jax.ShapeDtypeStruct((size, block, aux_count * orbitals), jnp.bfloat16) for size in sizes],
+        in_specs=[IN_SMEM] + [IN_VMEM] * (1 + len(pieces)),
+        out_specs=[IN_VMEM] * len(sizes),
         scratch_shapes=[
             pltpu.VMEM((blocks, block, orbitals), jnp.bfloat16),
             pltpu.VMEM((own_blocks, aux_count * block, orbitals), jnp.float32),
-            pltpu.SemaphoreType.DMA((len(pieces),)),
+            pltpu.SMEM((own_blocks,), jnp.int32),
+            pltpu.SMEM((own_blocks, slots), jnp.int32),
         ],
-        compiler_params=pltpu.CompilerParams(vmem_limit_bytes=32 * 1024 * 1024),
+        compiler_params=pltpu.CompilerParams(vmem_limit_bytes=VMEM_LIMIT),
         name="half_transform",
-    )(count, cols, rows, natural, integrals, *pieces)
+    )(meta, integrals, *pieces)
+
+
+ROWS = (((1,), (1,)), ((), ()))
+
+
+def dot_rows(first, second):
+    return lax.dot_general(first, second, ROWS, preferred_element_type=jnp.float32)
+
+
+STEPS = ([[0], [1, 2, 3]], [[0], [1, 2, 3]])
+HELD = 5
+
+
+def core_parts(held, s, k):
+    whole, near, *rest = held[s * HELD : (s + 1) * HELD]
+    depth = whole.shape[2]
+    if k == 0:
+        return [whole[...].reshape(-1, depth)]
+    return [near[k - 1], rest[k - 1][...].reshape(-1, depth)]
+
+
+def pair_kernel(*refs):
+    held, outs = refs[-len(STEPS) - CORES * HELD : -len(STEPS)], refs[-len(STEPS) :]
+    count, n, _ = held[0].shape
+    quarters = [[] for _ in range(count)]
+    at = 0
+    for step in STEPS:
+        for group in step:
+            for place, k in enumerate(group):
+                quarters[k].append(refs[at][place])
+            at += 1
+    quarters = [jnp.concatenate(parts, axis=0) for parts in quarters]
+    for s in range(CORES):
+        start = s * count * n
+        lower = upper = None
+        for k in range(count):
+            parts = [dot_rows(part, quarters[k]) for part in core_parts(held, s, k)]
+            if k == 0:
+                lower, upper = parts[0][:n], parts[0][n:]
+            else:
+                lower, upper = lower + parts[0], upper + parts[1]
+        for d, out in enumerate(outs):
+            out[pl.ds(start, n), :] = lower[:, d * n : (d + 1) * n].astype(jnp.bfloat16)
+            out[pl.ds(start + n, (count - 1) * n), :] = upper[:, d * n : (d + 1) * n].astype(jnp.bfloat16)
+
+
+def pair_blocks(rows, held):
+    count, n, _ = held[0].shape
+    flat = [part for parts in rows for part in parts]
+    shape = jax.ShapeDtypeStruct((CORES * count * n, n), jnp.bfloat16)
+    return pl.pallas_call(
+        pair_kernel,
+        out_shape=[shape] * len(STEPS),
+        in_specs=[IN_VMEM] * (len(flat) + len(held)),
+        out_specs=[IN_VMEM] * len(STEPS),
+        compiler_params=pltpu.CompilerParams(vmem_limit_bytes=VMEM_LIMIT),
+        name="pair_blocks",
+    )(*flat, *held)
+
+
+def own_kernel(*refs):
+    *held, _, out_ref, plane, sems = refs
+    _, count, rows, depth = plane.shape
+    n = rows // count
+    a = lax.axis_index("aux")
+    occ_index = lax.axis_index("occ")
+    z, c = occ_index // CORES, occ_index % CORES
+
+    def moves(s, k):
+        whole, near, *rest = held[s * HELD : (s + 1) * HELD]
+        parts = [(whole if k == 0 else rest[k - 1]).at[m] for m in range(count if k == 0 else count - 1)]
+        if k:
+            parts = [near.at[k - 1]] + parts
+        return [pltpu.make_async_copy(x, plane.at[s, k, pl.ds(m * n, n)], sems.at[s, k, m]) for m, x in enumerate(parts)]
+
+    @pl.when(a == z)
+    def _():
+        copies = {(s, k): moves(s, k) for s in range(CORES) for k in range(count)}
+        for parts in copies.values():
+            for copy in parts:
+                copy.start()
+        for s in range(CORES):
+            core = c if s == 0 else 1 - c
+            total = None
+            for k in range(count):
+                for copy in copies[s, k]:
+                    copy.wait()
+                value = dot_rows(plane[s, k], plane[0, k])
+                total = value if total is None else total + value
+            for m in range(count):
+                row = pl.multiple_of(core * rows + (a ^ m) * n, n)
+                for col in range(count):
+                    out_ref[pl.ds(row, n), pl.ds(pl.multiple_of((a ^ col) * n, n), n)] = total[
+                        m * n : (m + 1) * n, col * n : (col + 1) * n
+                    ]
+
+
+def own_block(held, earlier):
+    count, n, depth = held[0].shape
+    return pl.pallas_call(
+        own_kernel,
+        out_shape=jax.ShapeDtypeStruct((CORES * count * n, count * n), jnp.float32),
+        in_specs=[ANY] * (len(held) + 1),
+        out_specs=IN_VMEM,
+        scratch_shapes=[
+            pltpu.VMEM((CORES, count, count * n, depth), jnp.bfloat16),
+            pltpu.SemaphoreType.DMA((CORES, count, count)),
+        ],
+        compiler_params=pltpu.CompilerParams(vmem_limit_bytes=VMEM_MOST),
+        name="own_block",
+    )(*held, earlier)
+
+
+def place_kernel(*refs):
+    *quarters, own_ref, out_ref = refs
+    count = len(quarters)
+    n = quarters[0].shape[1]
+    width = count * n
+    a = lax.axis_index("aux")
+    occ_index = lax.axis_index("occ")
+    z, c = occ_index // CORES, occ_index % CORES
+    apart = lax.rem(a - z + count, count)
+
+    def tile(row, col, value):
+        out_ref[pl.ds(pl.multiple_of(row, n), n), pl.ds(pl.multiple_of(col, n), n)] = value
+
+    @pl.when(apart == 0)
+    def _():
+        out_ref[...] = own_ref[...]
+
+    @pl.when((apart > 0) & (apart <= count // 2))
+    def _():
+        for k, quarter in enumerate(quarters):
+            for s in range(CORES):
+                row = (c if s == 0 else 1 - c) * width + (a ^ k) * n
+                for m in range(count):
+                    value = quarter[pl.ds((s * count + m) * n, n), :].astype(jnp.float32)
+                    tile(row, (a ^ k ^ m) * n, value.T)
+
+    @pl.when(apart > count // 2)
+    def _():
+        for k, quarter in enumerate(quarters):
+            for s in range(CORES):
+                core = c if s == 0 else 1 - c
+                for m in range(count):
+                    value = quarter[pl.ds((s * count + m) * n, n), :].astype(jnp.float32)
+                    tile(core * width + (a ^ k ^ m) * n, (a ^ k) * n, value)
+
+
+def place_blocks(quarters, out):
+    return pl.pallas_call(
+        place_kernel,
+        out_shape=jax.ShapeDtypeStruct(out.shape, out.dtype),
+        in_specs=[IN_VMEM] * (len(quarters) + 1),
+        out_specs=IN_VMEM,
+        compiler_params=pltpu.CompilerParams(vmem_limit_bytes=VMEM_LIMIT),
+        name="place_blocks",
+    )(*quarters, out)
+
+
+def after(value, *done):
+    return lax.optimization_barrier((value, *done))[0]
+
+
+def mirrored_exchange(lay, half, *sent):
+    count, n, _ = half.shape
+    a = lax.axis_index("aux")
+    z = lax.axis_index("occ") // CORES
+    others = range(1, count)
+    other = lambda v: lay.send(v, lambda a_, z_, c_: (a_, z_, 1 - c_))
+    toward = lambda v, k: lay.send(v, lambda a_, z_, c_: (a_ ^ k, z_, c_))
+    below = lambda v: lay.send(v, lambda a_, z_, c_: (a_, (z_ - 1) % count, c_))
+
+    near = jnp.concatenate([toward(sent[k], k) for k in others])
+    first, later = [sent[0]], [near]
+    for _ in STEPS:
+        first.append(below(first[-1]))
+    for d in range(len(STEPS)):
+        later.append(below(after(later[-1], first[-1]) if d == 0 else later[-1]))
+    rest = [toward(after(sent[count - 1 + k], near), k) for k in others]
+    own = [half, near] + rest
+    held = own + [other(v) for v in own[:-1]] + [other(after(own[-1], later[-1]))]
+
+    ahead = pair_blocks(list(zip(first[1:], later[1:])), held)
+    mirror = lay.send(ahead[0], lambda a_, z_, c_: (a_, (z_ + 1) % count, c_))
+    out = own_block(held, ahead[1])
+    width = count * n
+    ahead = [jnp.concatenate([v[:width], other(v[width:])]) for v in ahead]
+    apart = {1: ahead[0], 2: ahead[1], 3: after(mirror, out)}
+
+    quarters = []
+    for k in range(count):
+        distance = lax.rem((a ^ k) - z + count, count)
+        value = apart[1]
+        for d in range(2, count):
+            value = jnp.where(distance == d, apart[d], value)
+        if k:
+            value = lay.send(value, lambda a_, z_, c_: (a_ ^ k, z_, c_) if a_ ^ k != z_ else None)
+        quarters.append(value)
+    return place_blocks(quarters, out)
 
 
 def product(first, second):
@@ -128,14 +370,22 @@
     part = own_blocks // share
     blocks = coefficients.reshape(own_blocks, block, orbitals)
     mine = lax.dynamic_slice_in_dim(blocks, (a % share) * part, part, 0)
-    far = [lay.send(mine, lambda a_, z_, c_, d=d: (a_, z_ ^ d, c_)) for d in range(1, planes)]
-    far = jnp.concatenate(far, axis=0)
-    spread = [far] + [lay.send(far, lambda a_, z_, c_, k=k: (a_ ^ k, z_, c_)) for k in range(1, share)]
     other = lambda v: lay.send(v, lambda a_, z_, c_: (a_, z_, 1 - c_))
     pieces = [blocks, other(blocks)]
-    for piece in spread:
-        pieces += [piece, other(piece)]
-    half = half_transform(lay, share, own_blocks, integrals, pieces, pair_cols, pair_rows, pair_count, row_blocks)
+    meta = jnp.concatenate([v.reshape(1, -1) for v in (pair_count, pair_cols, pair_rows, row_blocks)], axis=1)
+    for group in plane_groups(planes):
+        far = [lay.send(mine, lambda a_, z_, c_, d=d: (a_, z_ ^ d, c_)) for d in group]
+        far = jnp.concatenate(far, axis=0) if len(far) > 1 else far[0]
+        for k in range(share):
+            piece = lay.send(far, lambda a_, z_, c_, k=k: (a_ ^ k, z_, c_)) if k else far
+            pieces += [piece, other(piece)]
+    mirrored = lay.aux == planes == own_blocks == 4
+    half = half_transform(lay, share, mirrored, own_blocks, integrals, pieces, meta)
+
+    if mirrored:
+        return mirrored_exchange(lay, *half)
+
+    half = half[0].reshape(width, -1)
 
     out_blocks = block_total * block // lay.aux // width
     x_first, y_first = tuple(range(lay.bits)), tuple(reversed(range(lay.bits)))

time: 210 us -> 119 us (0.57); the launches traced: 207 us -> 118 us
  starting transfers between devices: 90.3 us -> 53.3 us
  waiting for transfers between devices: 78.6 us -> 46.9 us
  local copies, waits for them, and re-layouts: 15 us -> 5.04 us
  matrix products: 8.29 us -> 0 us
  other arithmetic: 9.79 us -> 2.84 us
  Pallas kernels: 3.43 us -> 9.27 us
    ppermute x42 -> x39, starting transfers between devices: 90.3 us -> 53.3 us  [send(): return lax.ppermute(value, AXES, pairs)]
    ppermute x42 -> x39, waiting for transfers between devices: 78.6 us -> 46.9 us  [send(): return lax.ppermute(value, AXES, pairs)]
    dot_general x10 -> x0, matrix products: 8.29 us -> none  [product(): lax.dot_general(first, second, (((1,), (1,)), ((), ())), preferred_elemen...]
    cond x10 -> x0, local copies, waits for them, and re-layouts: 7.43 us -> none
    pallas_call x1 -> x4, Pallas kernels: 3.43 us -> 9.27 us  [the longest x1 2.97 us: pair_blocks(): pl.pallas_call(pair_kernel, out_shape=[shape] * len(STEPS), in_specs=[IN_...]
    convert_element_type x10 -> x0, other arithmetic: 5.59 us -> none  [reduce_to_owner(): terms.append(lay.send(total.astype(jnp.bfloat16), where))]
    unnamed x58 -> x33, local copies, waits for them, and re-layouts: 6.62 us -> 3.1 us
    add x1 -> x0, other arithmetic: 2.54 us -> none  [local(): x + y.astype(jnp.float32)]
  transfers between devices with their start and end apart: 42 -> 39, of which waited for: 17 -> 13; matrix products, arithmetic and copies ran while one was open for 7% -> 2% of each run, Pallas kernels for 0% -> 1%
where the time goes in v3:
time: 119 us; the launch traced here: 118 us
  starting transfers between devices  53.3 us (45%)
  waiting for transfers between devices  46.9 us (39%)
  Pallas kernels  9.27 us (8%)
  local copies, waits for them, and re-layouts  5.04 us (4%)
  other arithmetic  2.84 us (2%)
    ppermute x39, starting transfers between devices, send(): return lax.ppermute(value, AXES, pairs)  53.3 us
    ppermute x39, waiting for transfers between devices, send(): return lax.ppermute(value, AXES, pairs)  46.9 us
    unnamed x33, local copies, waits for them, and re-layouts  3.1 us
    pallas_call x1, Pallas kernels, pair_blocks(): pl.pallas_call(pair_kernel, out_shape=[shape] * len(STEPS), in_specs=[IN_...  2.97 us
    pallas_call x1, Pallas kernels, half_transform(): pl.pallas_call(functools.partial(half_kernel, lay, share, len(pieces), mi...  2.95 us
  transfers between devices with their start and end apart: 39, of which 13 were waited for; matrix products, arithmetic and copies ran while one was open for 2% of the time, Pallas kernels for 1%

profile of v3, /device:TPU:5, one launch (start us, length us, event | category | flops | bytes accessed | tf_op | source)
XLA Modules:
  0.0 118.3 jit_solution(17342570553857169465)
XLA Ops:
  0.9 1.4 %collective-permute-start.1 = (bf16[1,128,384]{2,1,0:T(8,128)(2,1)S(1)}, bf16[1,128,384]{2,1,0:T(8,128)(2,1)S(1)}, u32[]{:S(2)}, u32[]{:S(2)}) collective-permute-start(bf16[1,128,384]{2,1,0:T(8,128)(2,1)S(1)} %constant_dynamic-slice_fusion), channel_id=1, source_target_pairs={{0,2},{1,3},{2,0},{3,1},{4,6},{5,7},{6,4},{7,5},{8,10},{9,11},{10,... | collective-permute-start | bytes 294920 | tf_op jit(solution)/shard_map/ppermute | solution.py:33
  2.3 2.3 %collective-permute-start.9 = (bf16[1,128,384]{2,1,0:T(8,128)(2,1)S(1)}, bf16[1,128,384]{2,1,0:T(8,128)(2,1)S(1)}, u32[]{:S(2)}, u32[]{:S(2)}) collective-permute-start(bf16[1,128,384]{2,1,0:T(8,128)(2,1)S(1)} %constant_dynamic-slice_fusion), channel_id=1, source_target_pairs={{0,4},{1,5},{2,6},{3,7},{4,0},{5,1},{6,2},{7,3},{8,12},{9,13},{10,... | collective-permute-start | bytes 294920 | tf_op jit(solution)/shard_map/ppermute | solution.py:33
  7.2 6.4 %collective-permute-start.2 = (bf16[1,128,384]{2,1,0:T(8,128)(2,1)S(1)}, bf16[1,128,384]{2,1,0:T(8,128)(2,1)S(1)}, u32[]{:S(2)}, u32[]{:S(2)}) collective-permute-start(bf16[1,128,384]{2,1,0:T(8,128)(2,1)S(1)} %collective-permute-done.1.refs_2_), channel_id=1, source_target_pairs={{0,1},{1,0},{2,3},{3,2},{4,5},{5,4},{6,7},{7,6},{8,9},{9,8},{10,11... | collective-permute-start | bytes 294920 | tf_op jit(solution)/shard_map/ppermute | solution.py:33
  17.3 3.0 %collective-permute-done.12.refs_12_ = bf16[2,128,384]{2,1,0:T(8,128)(2,1)S(1)} collective-permute-done((bf16[2,128,384]{2,1,0:T(8,128)(2,1)S(1)}, bf16[2,128,384]{2,1,0:T(8,128)(2,1)S(1)}, u32[]{:S(2)}, u32[]{:S(2)}) %collective-permute-start.12) | collective-permute-done | bytes 196640 | tf_op jit(solution)/shard_map/ppermute | solution.py:33
  21.5 3.9 %collective-permute-done.14.refs_14_ = bf16[2,128,384]{2,1,0:T(8,128)(2,1)S(1)} collective-permute-done((bf16[2,128,384]{2,1,0:T(8,128)(2,1)S(1)}, bf16[2,128,384]{2,1,0:T(8,128)(2,1)S(1)}, u32[]{:S(2)}, u32[]{:S(2)}) %collective-permute-start.14) | collective-permute-done | bytes 196640 | tf_op jit(solution)/shard_map/ppermute | solution.py:33
  29.2 1.4 %copy-done.11 = bf16[2,24,128,128]{3,2,1,0:T(8,128)(2,1)S(1)} copy-done((bf16[2,24,128,128]{3,2,1,0:T(8,128)(2,1)S(1)}, bf16[2,24,128,128]{3,2,1,0:T(8,128)(2,1)}, u32[]{:S(2)}) %copy-start.11) | copy-done | bytes 1572888
  31.6 3.0 %half_transform.1 = (bf16[4,128,768]{2,1,0:T(8,128)(2,1)S(1)}, bf16[1,128,768]{2,1,0:T(8,128)(2,1)S(1)}, bf16[1,128,768]{2,1,0:T(8,128)(2,1)S(1)}, bf16[1,128,76...) custom-call(s32[1,81]{1,0:T(1,128)S(1)} %pad_add_fusion.meta, ...), custom_call_target="tpu_custom_call" | custom-call | tf_op jit(solution)/shard_map/half_transform/pallas_call | solution.py:121
  34.6 3.4 %collective-permute-start.18 = (bf16[1,128,768]{2,1,0:T(8,128)(2,1)S(1)}, bf16[1,128,768]{2,1,0:T(8,128)(2,1)S(1)}, u32[]{:S(2)}, u32[]{:S(2)}) collective-permute-start(bf16[1,128,768]{2,1,0:T(8,128)(2,1)S(1)} %get-tuple-element.21), channel_id=1, source_target_pairs={{0,6},{1,7},{2,0},{3,1},{4,2},{5,3},{6,4},{7,5},{8,14},{9,15},{10,... | collective-permute-start | bytes 589832 | tf_op jit(solution)/shard_map/ppermute | solution.py:33
  40.7 1.5 %collective-permute-done.18.refs_0_ = bf16[1,128,768]{2,1,0:T(8,128)(2,1)S(1)} collective-permute-done((bf16[1,128,768]{2,1,0:T(8,128)(2,1)S(1)}, bf16[1,128,768]{2,1,0:T(8,128)(2,1)S(1)}, u32[]{:S(2)}, u32[]{:S(2)}) %collective-permute-start.18) | collective-permute-done | bytes 196640 | tf_op jit(solution)/shard_map/ppermute | solution.py:33
  42.1 3.7 %collective-permute-start.22 = (bf16[1,128,768]{2,1,0:T(8,128)(2,1)S(1)}, bf16[1,128,768]{2,1,0:T(8,128)(2,1)S(1)}, u32[]{:S(2)}, u32[]{:S(2)}) collective-permute-start(bf16[1,128,768]{2,1,0:T(8,128)(2,1)S(1)} %collective-permute-done.18.refs_0_), channel_id=1, source_target_pairs={{0,6},{1,7},{2,0},{3,1},{4,2},{5,3},{6,4},{7,5},{8,14},{9,15},{10,... | collective-permute-start | bytes 589832 | tf_op jit(solution)/shard_map/ppermute | solution.py:33
  45.9 3.4 %collective-permute-done.20 = bf16[1,128,768]{2,1,0:T(8,128)(2,1)S(1)} collective-permute-done((bf16[1,128,768]{2,1,0:T(8,128)(2,1)S(1)}, bf16[1,128,768]{2,1,0:T(8,128)(2,1)S(1)}, u32[]{:S(2)}, u32[]{:S(2)}) %collective-permute-start.20) | collective-permute-done | bytes 196640 | tf_op jit(solution)/shard_map/ppermute | solution.py:33
  50.0 4.0 %collective-permute-start.23 = (bf16[3,128,768]{2,1,0:T(8,128)(2,1)S(1)}, bf16[3,128,768]{2,1,0:T(8,128)(2,1)S(1)}, u32[]{:S(2)}, u32[]{:S(2)}) collective-permute-start(bf16[3,128,768]{2,1,0:T(8,128)(2,1)S(1)} %constant_dynamic-update-slice_fusion.2.refs_5_.refs_1_), channel_id=1, source_target_pairs={{0,6},{1,7},{2,0},{3,1},{4,2},{5,3},{6,4},{7,5},{8,14},{9,15},{10,... | collective-permute-start | bytes 1769480 | tf_op jit(solution)/shard_map/ppermute | solution.py:33
  54.0 2.0 %collective-permute-start.26 = (bf16[3,128,768]{2,1,0:T(8,128)(2,1)S(1)}, bf16[3,128,768]{2,1,0:T(8,128)(2,1)S(1)}, u32[]{:S(2)}, u32[]{:S(2)}) collective-permute-start(bf16[3,128,768]{2,1,0:T(8,128)(2,1)S(1)} %get-tuple-element.30), channel_id=1, source_target_pairs={{0,16},{1,17},{2,18},{3,19},{4,20},{5,21},{6,22},{7,23},{8,24},{9,... | collective-permute-start | bytes 1769480 | tf_op jit(solution)/shard_map/ppermute | solution.py:33
  56.6 9.0 %collective-permute-done.23.refs_1_ = bf16[3,128,768]{2,1,0:T(8,128)(2,1)S(1)} collective-permute-done((bf16[3,128,768]{2,1,0:T(8,128)(2,1)S(1)}, bf16[3,128,768]{2,1,0:T(8,128)(2,1)S(1)}, u32[]{:S(2)}, u32[]{:S(2)}) %collective-permute-start.23) | collective-permute-done | bytes 589856 | tf_op jit(solution)/shard_map/ppermute | solution.py:33
  65.7 4.0 %collective-permute-start.24 = (bf16[3,128,768]{2,1,0:T(8,128)(2,1)S(1)}, bf16[3,128,768]{2,1,0:T(8,128)(2,1)S(1)}, u32[]{:S(2)}, u32[]{:S(2)}) collective-permute-start(bf16[3,128,768]{2,1,0:T(8,128)(2,1)S(1)} %collective-permute-done.23.refs_1_), channel_id=1, source_target_pairs={{0,6},{1,7},{2,0},{3,1},{4,2},{5,3},{6,4},{7,5},{8,14},{9,15},{10,... | collective-permute-start | bytes 1769480 | tf_op jit(solution)/shard_map/ppermute | solution.py:33
  69.7 2.2 %collective-permute-start.28 = (bf16[4,128,768]{2,1,0:T(8,128)(2,1)S(1)}, bf16[4,128,768]{2,1,0:T(8,128)(2,1)S(1)}, u32[]{:S(2)}, u32[]{:S(2)}) collective-permute-start(bf16[4,128,768]{2,1,0:T(8,128)(2,1)S(1)} %get-tuple-element.26.refs_4_.refs_0_), channel_id=1, source_target_pairs={{0,1},{1,0},{2,3},{3,2},{4,5},{5,4},{6,7},{7,6},{8,9},{9,8},{10,11... | collective-permute-start | bytes 2359304 | tf_op jit(solution)/shard_map/ppermute | solution.py:33
  72.4 9.6 %collective-permute-done.26.refs_7_.refs_3_ = bf16[3,128,768]{2,1,0:T(8,128)(2,1)S(1)} collective-permute-done((bf16[3,128,768]{2,1,0:T(8,128)(2,1)S(1)}, bf16[3,128,768]{2,1,0:T(8,128)(2,1)S(1)}, u32[]{:S(2)}, u32[]{:S(2)}) %collective-permute-start.26) | collective-permute-done | bytes 589856 | tf_op jit(solution)/shard_map/ppermute | solution.py:33
  86.3 3.0 %pair_blocks.1 = (bf16[1024,128]{1,0:T(8,128)(2,1)}, bf16[1024,128]{1,0:T(8,128)(2,1)S(1)}) custom-call(bf16[1,128,768]{2,1,0:T(8,128)(2,1)S(1)} %collective-permute-done.18.refs_0_, bf16[3,128,768]{2,1,0:T(8,128)(2,1)S(1)} %collective-permute-done.23.refs_1_, bf16[1,128,768]{2,1,0:T(8,128)(2,1)S(1)} %collective-permute-done.22.refs_2_, ...), custom_call_target="tpu_custom_call" | custom-call | tf_op jit(solution)/shard_map/pair_blocks/pallas_call | solution.py:185
  91.6 1.6 %own_block.1.refs_4_ = f32[1024,512]{1,0:T(8,128)} custom-call(bf16[4,128,768]{2,1,0:T(8,128)(2,1)} %copy-done.2, bf16[3,128,768]{2,1,0:T(8,128)(2,1)} %copy-done.1, bf16[3,128,768]{2,1,0:T(8,128)(2,1)} %copy-done.6, bf16[3,128,768]{2,1,0:T(8,128)(2,1)} %copy-done.5, bf16[3,128,768]{2,1,0:T(8,128)(2,1)} %copy-done.4, bf16[4,128,768]{2,1,0:T(8,128)(2,1)} %copy-done.3, ...), custom_call_target="tpu_custom_call" | custom-call | tf_op jit(solution)/shard_map/own_block/pallas_call | solution.py:234
  93.3 5.6 %collective-permute-done.33 = bf16[1024,128]{1,0:T(8,128)(2,1)S(1)} collective-permute-done((bf16[1024,128]{1,0:T(8,128)(2,1)}, bf16[1024,128]{1,0:T(8,128)(2,1)S(1)}, u32[]{:S(2)}, u32[]{:S(2)}) %collective-permute-start.33) | collective-permute-done | bytes 262176 | tf_op jit(solution)/shard_map/ppermute | solution.py:33
  100.0 2.5 %collective-permute-start.36 = (bf16[1024,128]{1,0:T(8,128)(2,1)}, bf16[1024,128]{1,0:T(8,128)(2,1)S(1)}, u32[]{:S(2)}, u32[]{:S(2)}) collective-permute-start(bf16[1024,128]{1,0:T(8,128)(2,1)} %get-tuple-element.39), channel_id=1, source_target_pairs={{0,8},{1,9},{4,12},{5,13},{6,14},{7,15},{10,2},{11,3},{12,4},{13,5... | collective-permute-start | bytes 786440 | tf_op jit(solution)/shard_map/ppermute | solution.py:33
  103.8 4.6 %collective-permute-start.38 = (bf16[1024,128]{1,0:T(8,128)(2,1)}, bf16[1024,128]{1,0:T(8,128)(2,1)S(1)}, u32[]{:S(2)}, u32[]{:S(2)}) collective-permute-start(bf16[1024,128]{1,0:T(8,128)(2,1)} %get-tuple-element.37), channel_id=1, source_target_pairs={{0,24},{1,25},{2,26},{3,27},{4,28},{5,29},{8,16},{9,17},{10,18},{1... | collective-permute-start | bytes 786440 | tf_op jit(solution)/shard_map/ppermute | solution.py:33
  109.4 7.1 %collective-permute-done.37.refs_2_ = bf16[1024,128]{1,0:T(8,128)(2,1)S(1)} collective-permute-done((bf16[1024,128]{1,0:T(8,128)(2,1)}, bf16[1024,128]{1,0:T(8,128)(2,1)S(1)}, u32[]{:S(2)}, u32[]{:S(2)}) %collective-permute-start.37) | collective-permute-done | bytes 262176 | tf_op jit(solution)/shard_map/ppermute | solution.py:33
  116.5 1.7 %place_blocks.1 = f32[1024,512]{1,0:T(8,128)} custom-call(bf16[1024,128]{1,0:T(8,128)(2,1)S(1)} %select_select_fusion.3.refs_0_, bf16[1024,128]{1,0:T(8,128)(2,1)S(1)} %collective-permute-done.36.refs_1_, bf16[1024,128]{1,0:T(8,128)(2,1)S(1)} %collective-permute-done.37.refs_2_, bf16[1024,128]{1,0:T(8,128)(2,1)S(1)} %collective-permute-done.38.refs_3_, ...), custom_call_target="tpu_custom_call" | custom-call | tf_op jit(solution)/shard_map/place_blocks/pallas_call | solution.py:285
  (99 shorter events, 27.0 us)
Async XLA Ops:
  4.6 9.1 %collective-permute-start.10 = (bf16[1,128,384]{2,1,0:T(8,128)(2,1)S(1)}, bf16[1,128,384]{2,1,0:T(8,128)(2,1)S(1)}, u32[]{:S(2)}, u32[]{:S(2)}) collective-permute-start(bf16[1,128,384]{2,1,0:T(8,128)(2,1)S(1)} %constant_dynamic-slice_fusion), channel_id=1, source_target_pairs={{0,6},{1,7},{2,4},{3,5},{4,2},{5,3},{6,0},{7,1},{8,14},{9,15},{10,... | collective-permute-start | bytes 294920 | tf_op jit(solution)/shard_map/ppermute | solution.py:33
  4.6 10.4 %collective-permute-start.3 = (bf16[1,128,384]{2,1,0:T(8,128)(2,1)S(1)}, bf16[1,128,384]{2,1,0:T(8,128)(2,1)S(1)}, u32[]{:S(2)}, u32[]{:S(2)}) collective-permute-start(bf16[1,128,384]{2,1,0:T(8,128)(2,1)S(1)} %collective-permute-done.1.refs_2_), channel_id=1, source_target_pairs={{0,8},{1,9},{2,10},{3,11},{4,12},{5,13},{6,14},{7,15},{8,0},{9,1},... | collective-permute-start | bytes 294920 | tf_op jit(solution)/shard_map/ppermute | solution.py:33
  5.8 9.4 %collective-permute-start.5 = (bf16[1,128,384]{2,1,0:T(8,128)(2,1)S(1)}, bf16[1,128,384]{2,1,0:T(8,128)(2,1)S(1)}, u32[]{:S(2)}, u32[]{:S(2)}) collective-permute-start(bf16[1,128,384]{2,1,0:T(8,128)(2,1)S(1)} %collective-permute-done.1.refs_2_), channel_id=1, source_target_pairs={{0,16},{1,17},{2,18},{3,19},{4,20},{5,21},{6,22},{7,23},{8,24},{9,... | collective-permute-start | bytes 294920 | tf_op jit(solution)/shard_map/ppermute | solution.py:33
  6.0 9.7 %collective-permute-start.7 = (bf16[1,128,384]{2,1,0:T(8,128)(2,1)S(1)}, bf16[1,128,384]{2,1,0:T(8,128)(2,1)S(1)}, u32[]{:S(2)}, u32[]{:S(2)}) collective-permute-start(bf16[1,128,384]{2,1,0:T(8,128)(2,1)S(1)} %collective-permute-done.1.refs_2_), channel_id=1, source_target_pairs={{0,24},{1,25},{2,26},{3,27},{4,28},{5,29},{6,30},{7,31},{8,16},{9,... | collective-permute-start | bytes 294920 | tf_op jit(solution)/shard_map/ppermute | solution.py:33
  7.2 9.8 %collective-permute-start.2 = (bf16[1,128,384]{2,1,0:T(8,128)(2,1)S(1)}, bf16[1,128,384]{2,1,0:T(8,128)(2,1)S(1)}, u32[]{:S(2)}, u32[]{:S(2)}) collective-permute-start(bf16[1,128,384]{2,1,0:T(8,128)(2,1)S(1)} %collective-permute-done.1.refs_2_), channel_id=1, source_target_pairs={{0,1},{1,0},{2,3},{3,2},{4,5},{5,4},{6,7},{7,6},{8,9},{9,8},{10,11... | collective-permute-start | bytes 294920 | tf_op jit(solution)/shard_map/ppermute | solution.py:33
  15.0 10.4 %collective-permute-start.14 = (bf16[2,128,384]{2,1,0:T(8,128)(2,1)S(1)}, bf16[2,128,384]{2,1,0:T(8,128)(2,1)S(1)}, u32[]{:S(2)}, u32[]{:S(2)}) collective-permute-start(bf16[2,128,384]{2,1,0:T(8,128)(2,1)S(1)} %constant_dynamic-update-slice_fusion.refs_10_), channel_id=1, source_target_pairs={{0,16},{1,17},{2,18},{3,19},{4,20},{5,21},{6,22},{7,23},{8,24},{9,... | collective-permute-start | bytes 589832 | tf_op jit(solution)/shard_map/ppermute | solution.py:33
  15.2 14.0 %collective-permute-start = (bf16[4,128,384]{2,1,0:T(8,128)(2,1)}, bf16[4,128,384]{2,1,0:T(8,128)(2,1)S(1)}, u32[]{:S(2)}, u32[]{:S(2)}) collective-permute-start(bf16[4,128,384]{2,1,0:T(8,128)(2,1)} %bitcast.3), channel_id=1, source_target_pairs={{0,1},{1,0},{2,3},{3,2},{4,5},{5,4},{6,7},{7,6},{8,9},{9,8},{10,11... | collective-permute-start | bytes 1179656 | tf_op jit(solution)/shard_map/ppermute | solution.py:33
  15.8 10.7 %collective-permute-start.16 = (bf16[2,128,384]{2,1,0:T(8,128)(2,1)S(1)}, bf16[2,128,384]{2,1,0:T(8,128)(2,1)S(1)}, u32[]{:S(2)}, u32[]{:S(2)}) collective-permute-start(bf16[2,128,384]{2,1,0:T(8,128)(2,1)S(1)} %constant_dynamic-update-slice_fusion.refs_10_), channel_id=1, source_target_pairs={{0,24},{1,25},{2,26},{3,27},{4,28},{5,29},{6,30},{7,31},{8,16},{9,... | collective-permute-start | bytes 589832 | tf_op jit(solution)/shard_map/ppermute | solution.py:33
  17.0 9.5 %collective-permute-start.11 = (bf16[2,128,384]{2,1,0:T(8,128)(2,1)S(1)}, bf16[2,128,384]{2,1,0:T(8,128)(2,1)S(1)}, u32[]{:S(2)}, u32[]{:S(2)}) collective-permute-start(bf16[2,128,384]{2,1,0:T(8,128)(2,1)S(1)} %constant_dynamic-update-slice_fusion.refs_10_), channel_id=1, source_target_pairs={{0,1},{1,0},{2,3},{3,2},{4,5},{5,4},{6,7},{7,6},{8,9},{9,8},{10,11... | collective-permute-start | bytes 589832 | tf_op jit(solution)/shard_map/ppermute | solution.py:33
  38.8 10.4 %collective-permute-start.20 = (bf16[1,128,768]{2,1,0:T(8,128)(2,1)S(1)}, bf16[1,128,768]{2,1,0:T(8,128)(2,1)S(1)}, u32[]{:S(2)}, u32[]{:S(2)}) collective-permute-start(bf16[1,128,768]{2,1,0:T(8,128)(2,1)S(1)} %get-tuple-element.23), channel_id=1, source_target_pairs={{0,16},{1,17},{2,18},{3,19},{4,20},{5,21},{6,22},{7,23},{8,24},{9,... | collective-permute-start | bytes 589832 | tf_op jit(solution)/shard_map/ppermute | solution.py:33
  39.3 10.0 %collective-permute-start.21 = (bf16[1,128,768]{2,1,0:T(8,128)(2,1)S(1)}, bf16[1,128,768]{2,1,0:T(8,128)(2,1)S(1)}, u32[]{:S(2)}, u32[]{:S(2)}) collective-permute-start(bf16[1,128,768]{2,1,0:T(8,128)(2,1)S(1)} %get-tuple-element.24), channel_id=1, source_target_pairs={{0,24},{1,25},{2,26},{3,27},{4,28},{5,29},{6,30},{7,31},{8,16},{9,... | collective-permute-start | bytes 589832 | tf_op jit(solution)/shard_map/ppermute | solution.py:33
  42.1 7.9 %collective-permute-start.22 = (bf16[1,128,768]{2,1,0:T(8,128)(2,1)S(1)}, bf16[1,128,768]{2,1,0:T(8,128)(2,1)S(1)}, u32[]{:S(2)}, u32[]{:S(2)}) collective-permute-start(bf16[1,128,768]{2,1,0:T(8,128)(2,1)S(1)} %collective-permute-done.18.refs_0_), channel_id=1, source_target_pairs={{0,6},{1,7},{2,0},{3,1},{4,2},{5,3},{6,4},{7,5},{8,14},{9,15},{10,... | collective-permute-start | bytes 589832 | tf_op jit(solution)/shard_map/ppermute | solution.py:33
  50.0 15.7 %collective-permute-start.23 = (bf16[3,128,768]{2,1,0:T(8,128)(2,1)S(1)}, bf16[3,128,768]{2,1,0:T(8,128)(2,1)S(1)}, u32[]{:S(2)}, u32[]{:S(2)}) collective-permute-start(bf16[3,128,768]{2,1,0:T(8,128)(2,1)S(1)} %constant_dynamic-update-slice_fusion.2.refs_5_.refs_1_), channel_id=1, source_target_pairs={{0,6},{1,7},{2,0},{3,1},{4,2},{5,3},{6,4},{7,5},{8,14},{9,15},{10,... | collective-permute-start | bytes 1769480 | tf_op jit(solution)/shard_map/ppermute | solution.py:33
  54.0 17.8 %collective-permute-start.27 = (bf16[3,128,768]{2,1,0:T(8,128)(2,1)S(1)}, bf16[3,128,768]{2,1,0:T(8,128)(2,1)S(1)}, u32[]{:S(2)}, u32[]{:S(2)}) collective-permute-start(bf16[3,128,768]{2,1,0:T(8,128)(2,1)S(1)} %get-tuple-element.32), channel_id=1, source_target_pairs={{0,24},{1,25},{2,26},{3,27},{4,28},{5,29},{6,30},{7,31},{8,16},{9,... | collective-permute-start | bytes 1769480 | tf_op jit(solution)/shard_map/ppermute | solution.py:33
  54.0 28.1 %collective-permute-start.26 = (bf16[3,128,768]{2,1,0:T(8,128)(2,1)S(1)}, bf16[3,128,768]{2,1,0:T(8,128)(2,1)S(1)}, u32[]{:S(2)}, u32[]{:S(2)}) collective-permute-start(bf16[3,128,768]{2,1,0:T(8,128)(2,1)S(1)} %get-tuple-element.30), channel_id=1, source_target_pairs={{0,16},{1,17},{2,18},{3,19},{4,20},{5,21},{6,22},{7,23},{8,24},{9,... | collective-permute-start | bytes 1769480 | tf_op jit(solution)/shard_map/ppermute | solution.py:33
  56.0 26.9 %collective-permute-start.25 = (bf16[3,128,768]{2,1,0:T(8,128)(2,1)S(1)}, bf16[3,128,768]{2,1,0:T(8,128)(2,1)S(1)}, u32[]{:S(2)}, u32[]{:S(2)}) collective-permute-start(bf16[3,128,768]{2,1,0:T(8,128)(2,1)S(1)} %get-tuple-element.28), channel_id=1, source_target_pairs={{0,8},{1,9},{2,10},{3,11},{4,12},{5,13},{6,14},{7,15},{8,0},{9,1},... | collective-permute-start | bytes 1769480 | tf_op jit(solution)/shard_map/ppermute | solution.py:33
  65.7 17.4 %collective-permute-start.24 = (bf16[3,128,768]{2,1,0:T(8,128)(2,1)S(1)}, bf16[3,128,768]{2,1,0:T(8,128)(2,1)S(1)}, u32[]{:S(2)}, u32[]{:S(2)}) collective-permute-start(bf16[3,128,768]{2,1,0:T(8,128)(2,1)S(1)} %collective-permute-done.23.refs_1_), channel_id=1, source_target_pairs={{0,6},{1,7},{2,0},{3,1},{4,2},{5,3},{6,4},{7,5},{8,14},{9,15},{10,... | collective-permute-start | bytes 1769480 | tf_op jit(solution)/shard_map/ppermute | solution.py:33
  69.7 13.8 %collective-permute-start.28 = (bf16[4,128,768]{2,1,0:T(8,128)(2,1)S(1)}, bf16[4,128,768]{2,1,0:T(8,128)(2,1)S(1)}, u32[]{:S(2)}, u32[]{:S(2)}) collective-permute-start(bf16[4,128,768]{2,1,0:T(8,128)(2,1)S(1)} %get-tuple-element.26.refs_4_.refs_0_), channel_id=1, source_target_pairs={{0,1},{1,0},{2,3},{3,2},{4,5},{5,4},{6,7},{7,6},{8,9},{9,8},{10,11... | collective-permute-start | bytes 2359304 | tf_op jit(solution)/shard_map/ppermute | solution.py:33
  71.8 11.6 %collective-permute-start.29 = (bf16[3,128,768]{2,1,0:T(8,128)(2,1)S(1)}, bf16[3,128,768]{2,1,0:T(8,128)(2,1)S(1)}, u32[]{:S(2)}, u32[]{:S(2)}) collective-permute-start(bf16[3,128,768]{2,1,0:T(8,128)(2,1)S(1)} %constant_dynamic-update-slice_fusion.2.refs_5_.refs_1_), channel_id=1, source_target_pairs={{0,1},{1,0},{2,3},{3,2},{4,5},{5,4},{6,7},{7,6},{8,9},{9,8},{10,11... | collective-permute-start | bytes 1769480 | tf_op jit(solution)/shard_map/ppermute | solution.py:33
  89.3 9.6 %collective-permute-start.33 = (bf16[1024,128]{1,0:T(8,128)(2,1)}, bf16[1024,128]{1,0:T(8,128)(2,1)S(1)}, u32[]{:S(2)}, u32[]{:S(2)}) collective-permute-start(bf16[1024,128]{1,0:T(8,128)(2,1)} %get-tuple-element.34), channel_id=1, source_target_pairs={{0,2},{1,3},{2,4},{3,5},{4,6},{5,7},{6,0},{7,1},{8,10},{9,11},{10,... | collective-permute-start | bytes 786440 | tf_op jit(solution)/shard_map/ppermute | solution.py:33
  90.0 8.9 %collective-permute-start.34 = (bf16[512,128]{1,0:T(8,128)(2,1)S(1)}, bf16[512,128]{1,0:T(8,128)(2,1)S(1)}, u32[]{:S(2)}, u32[]{:S(2)}) collective-permute-start(bf16[512,128]{1,0:T(8,128)(2,1)S(1)} %get-tuple-element.41), channel_id=1, source_target_pairs={{0,1},{1,0},{2,3},{3,2},{4,5},{5,4},{6,7},{7,6},{8,9},{9,8},{10,11... | collective-permute-start | bytes 393224 | tf_op jit(solution)/shard_map/ppermute | solution.py:33
  100.0 9.4 %collective-permute-start.36 = (bf16[1024,128]{1,0:T(8,128)(2,1)}, bf16[1024,128]{1,0:T(8,128)(2,1)S(1)}, u32[]{:S(2)}, u32[]{:S(2)}) collective-permute-start(bf16[1024,128]{1,0:T(8,128)(2,1)} %get-tuple-element.39), channel_id=1, source_target_pairs={{0,8},{1,9},{4,12},{5,13},{6,14},{7,15},{10,2},{11,3},{12,4},{13,5... | collective-permute-start | bytes 786440 | tf_op jit(solution)/shard_map/ppermute | solution.py:33
  102.5 14.0 %collective-permute-start.37 = (bf16[1024,128]{1,0:T(8,128)(2,1)}, bf16[1024,128]{1,0:T(8,128)(2,1)S(1)}, u32[]{:S(2)}, u32[]{:S(2)}) collective-permute-start(bf16[1024,128]{1,0:T(8,128)(2,1)} %get-tuple-element.38), channel_id=1, source_target_pairs={{0,16},{1,17},{2,18},{3,19},{6,22},{7,23},{8,24},{9,25},{10,26},{1... | collective-permute-start | bytes 786440 | tf_op jit(solution)/shard_map/ppermute | solution.py:33
  103.8 12.7 %collective-permute-start.38 = (bf16[1024,128]{1,0:T(8,128)(2,1)}, bf16[1024,128]{1,0:T(8,128)(2,1)S(1)}, u32[]{:S(2)}, u32[]{:S(2)}) collective-permute-start(bf16[1024,128]{1,0:T(8,128)(2,1)} %get-tuple-element.37), channel_id=1, source_target_pairs={{0,24},{1,25},{2,26},{3,27},{4,28},{5,29},{8,16},{9,17},{10,18},{1... | collective-permute-start | bytes 786440 | tf_op jit(solution)/shard_map/ppermute | solution.py:33
  (30 other events, 240.5 us)

commit v4 on v3

--- a/solution.py
+++ b/solution.py
@@ -141,16 +141,19 @@
     return lax.dot_general(first, second, ROWS, preferred_element_type=jnp.float32)
 
 
-STEPS = ([[0], [1, 2, 3]], [[0], [1, 2, 3]])
+STEPS = ([[0], [1, 2], [3]], [[0, 1, 2], [3]])
 HELD = 5
 
 
 def core_parts(held, s, k):
-    whole, near, *rest = held[s * HELD : (s + 1) * HELD]
-    depth = whole.shape[2]
+    whole, near, first, second, passed = held[s * HELD : (s + 1) * HELD]
+    n, depth = whole.shape[1:]
     if k == 0:
         return [whole[...].reshape(-1, depth)]
-    return [near[k - 1], rest[k - 1][...].reshape(-1, depth)]
+    if k < 3:
+        return [near[k - 1], (first if k == 1 else second)[...].reshape(-1, depth)]
+    rows = [passed[0, :n], passed[1, :n], passed[0, n:], passed[1, n:]]
+    return [near[k - 1], jnp.concatenate(rows, axis=0)]
 
 
 def pair_kernel(*refs):
@@ -193,7 +196,7 @@
 
 
 def own_kernel(*refs):
-    *held, _, out_ref, plane, sems = refs
+    *held, out_ref, plane, sems = refs
     _, count, rows, depth = plane.shape
     n = rows // count
     a = lax.axis_index("aux")
@@ -201,11 +204,22 @@
     z, c = occ_index // CORES, occ_index % CORES
 
     def moves(s, k):
-        whole, near, *rest = held[s * HELD : (s + 1) * HELD]
-        parts = [(whole if k == 0 else rest[k - 1]).at[m] for m in range(count if k == 0 else count - 1)]
-        if k:
-            parts = [near.at[k - 1]] + parts
-        return [pltpu.make_async_copy(x, plane.at[s, k, pl.ds(m * n, n)], sems.at[s, k, m]) for m, x in enumerate(parts)]
+        whole, near, first, second, passed = held[s * HELD : (s + 1) * HELD]
+        half = n // 2
+        if k == 0:
+            parts = [(whole.at[m], m * n, n) for m in range(count)]
+        elif k < 3:
+            rest = first if k == 1 else second
+            parts = [(near.at[k - 1], 0, n)] + [(rest.at[m - 1], m * n, n) for m in range(1, count)]
+        else:
+            parts = [(near.at[k - 1], 0, n)]
+            for side in range(2):
+                parts.append((passed.at[side, pl.ds(0, n)], (1 + side) * n, n))
+                parts.append((passed.at[side, pl.ds(n, half)], 3 * n + side * half, half))
+        return [
+            pltpu.make_async_copy(x, plane.at[s, k, pl.ds(start, size)], sems.at[s, k, i])
+            for i, (x, start, size) in enumerate(parts)
+        ]
 
     @pl.when(a == z)
     def _():
@@ -229,20 +243,20 @@
                     ]
 
 
-def own_block(held, earlier):
+def own_block(held):
     count, n, depth = held[0].shape
     return pl.pallas_call(
         own_kernel,
         out_shape=jax.ShapeDtypeStruct((CORES * count * n, count * n), jnp.float32),
-        in_specs=[ANY] * (len(held) + 1),
+        in_specs=[ANY] * len(held),
         out_specs=IN_VMEM,
         scratch_shapes=[
             pltpu.VMEM((CORES, count, count * n, depth), jnp.bfloat16),
-            pltpu.SemaphoreType.DMA((CORES, count, count)),
+            pltpu.SemaphoreType.DMA((CORES, count, count + 1)),
         ],
         compiler_params=pltpu.CompilerParams(vmem_limit_bytes=VMEM_MOST),
         name="own_block",
-    )(*held, earlier)
+    )(*held)
 
 
 def place_kernel(*refs):
@@ -305,22 +319,26 @@
     toward = lambda v, k: lay.send(v, lambda a_, z_, c_: (a_ ^ k, z_, c_))
     below = lambda v: lay.send(v, lambda a_, z_, c_: (a_, (z_ - 1) % count, c_))
 
-    near = jnp.concatenate([toward(sent[k], k) for k in others])
-    first, later = [sent[0]], [near]
-    for _ in STEPS:
-        first.append(below(first[-1]))
-    for d in range(len(STEPS)):
-        later.append(below(after(later[-1], first[-1]) if d == 0 else later[-1]))
-    rest = [toward(after(sent[count - 1 + k], near), k) for k in others]
-    own = [half, near] + rest
-    held = own + [other(v) for v in own[:-1]] + [other(after(own[-1], later[-1]))]
-
-    ahead = pair_blocks(list(zip(first[1:], later[1:])), held)
+    quarter = {k: toward(sent[k], k) for k in others}
+    beside = jnp.concatenate([quarter[1], quarter[2]])
+    begun = below(sent[0])
+    rows = [[begun, below(beside), below(after(quarter[3], begun))]]
+    rows.append([below(jnp.concatenate(rows[0][:2])), below(rows[0][2])])
+    near = jnp.concatenate([quarter[k] for k in others])
+    crossed = [other(half), other(near)]
+    first, second = (toward(after(sent[count - 1 + k], near, begun, crossed[0]), k) for k in (1, 2))
+    up = toward(after(jnp.concatenate([first[2], first[0, : n // 2]]), crossed[1]), 2)
+    over = toward(after(jnp.concatenate([second[2], second[1, n // 2 :]]), rows[0][2]), 1)
+    passed = jnp.stack([up, over])
+    crossed += [other(first), other(second), other(after(passed, *rows[-1]))]
+    held = [half, near, first, second, passed] + crossed
+
+    ahead = pair_blocks(rows, held)
     mirror = lay.send(ahead[0], lambda a_, z_, c_: (a_, (z_ + 1) % count, c_))
-    out = own_block(held, ahead[1])
+    out = own_block(held)
     width = count * n
     ahead = [jnp.concatenate([v[:width], other(v[width:])]) for v in ahead]
-    apart = {1: ahead[0], 2: ahead[1], 3: after(mirror, out)}
+    apart = {1: ahead[0], 2: after(ahead[1], out), 3: mirror}
 
     quarters = []
     for k in range(count):
@@ -376,6 +394,8 @@
     for group in plane_groups(planes):
         far = [lay.send(mine, lambda a_, z_, c_, d=d: (a_, z_ ^ d, c_)) for d in group]
         far = jnp.concatenate(far, axis=0) if len(far) > 1 else far[0]
+        if group[-1] == planes - 1:
+            far = after(far, meta)
         for k in range(share):
             piece = lay.send(far, lambda a_, z_, c_, k=k: (a_ ^ k, z_, c_)) if k else far
             pieces += [piece, other(piece)]

time: 119 us -> 116 us (0.975)
  other arithmetic: 2.84 us -> 1.26 us
  local copies, waits for them, and re-layouts: 5.04 us -> 3.47 us
  starting transfers between devices: 53.3 us -> 54.6 us
  waiting for transfers between devices: 46.9 us -> 45.7 us
    select_n x2 -> x1, other arithmetic: 2.07 us -> 0.26 us  [mirrored_exchange(): value = jnp.where(distance == d, apart[d], value)]
    pallas_call x1, Pallas kernels: 2.95 us -> 4.6 us  [half_transform(): pl.pallas_call(functools.partial(half_kernel, lay, share, len(pieces), mi...]
    ppermute x39 -> x41, starting transfers between devices: 53.3 us -> 54.6 us  [send(): return lax.ppermute(value, AXES, pairs)]
    ppermute x39 -> x41, waiting for transfers between devices: 46.9 us -> 45.7 us  [send(): return lax.ppermute(value, AXES, pairs)]
    unnamed x33 -> x28, local copies, waits for them, and re-layouts: 3.1 us -> 2.48 us
  transfers between devices with their start and end apart: 39 -> 41, of which waited for: 13 -> 17; matrix products, arithmetic and copies ran while one was open for 2% -> 1% of each run, Pallas kernels for 1% -> 1%
where the time goes in v4:
time: 116 us
  starting transfers between devices  54.6 us (47%)
  waiting for transfers between devices  45.7 us (39%)
  Pallas kernels  10.3 us (9%)
  local copies, waits for them, and re-layouts  3.47 us (3%)
  other arithmetic  1.26 us (1%)
    ppermute x41, starting transfers between devices, send(): return lax.ppermute(value, AXES, pairs)  54.6 us
    ppermute x41, waiting for transfers between devices, send(): return lax.ppermute(value, AXES, pairs)  45.7 us
    pallas_call x1, Pallas kernels, half_transform(): pl.pallas_call(functools.partial(half_kernel, lay, share, len(pieces), mi...  4.6 us
    unnamed x28, local copies, waits for them, and re-layouts  2.48 us
  transfers between devices with their start and end apart: 41, of which 17 were waited for; matrix products, arithmetic and copies ran while one was open for 1% of the time, Pallas kernels for 1%

profile of v4, /device:TPU:5, one launch (start us, length us, event | category | flops | bytes accessed | tf_op | source)
XLA Modules:
  0.0 116.4 jit_solution(15910861974632024466)
XLA Ops:
  2.3 2.2 %collective-permute-start.10 = (bf16[1,128,384]{2,1,0:T(8,128)(2,1)S(1)}, bf16[1,128,384]{2,1,0:T(8,128)(2,1)S(1)}, u32[]{:S(2)}, u32[]{:S(2)}) collective-permute-start(bf16[1,128,384]{2,1,0:T(8,128)(2,1)S(1)} %constant_dynamic-slice_fusion), channel_id=1, source_target_pairs={{0,6},{1,7},{2,4},{3,5},{4,2},{5,3},{6,0},{7,1},{8,14},{9,15},{10,... | collective-permute-start | bytes 294920 | tf_op jit(solution)/shard_map/ppermute | solution.py:33
  10.0 3.8 %collective-permute-done.9 = bf16[1,128,384]{2,1,0:T(8,128)(2,1)S(1)} collective-permute-done((bf16[1,128,384]{2,1,0:T(8,128)(2,1)S(1)}, bf16[1,128,384]{2,1,0:T(8,128)(2,1)S(1)}, u32[]{:S(2)}, u32[]{:S(2)}) %collective-permute-start.9) | collective-permute-done | bytes 98336 | tf_op jit(solution)/shard_map/ppermute | solution.py:33
  17.9 1.6 %collective-permute-start.4 = (bf16[1,128,384]{2,1,0:T(8,128)(2,1)S(1)}, bf16[1,128,384]{2,1,0:T(8,128)(2,1)S(1)}, u32[]{:S(2)}, u32[]{:S(2)}) collective-permute-start(bf16[1,128,384]{2,1,0:T(8,128)(2,1)S(1)} %collective-permute-done.3.refs_4_), channel_id=1, source_target_pairs={{0,1},{1,0},{2,3},{3,2},{4,5},{5,4},{6,7},{7,6},{8,9},{9,8},{10,11... | collective-permute-start | bytes 294920 | tf_op jit(solution)/shard_map/ppermute | solution.py:33
  21.9 2.8 %collective-permute-start.17 = (bf16[2,128,384]{2,1,0:T(8,128)(2,1)S(1)}, bf16[2,128,384]{2,1,0:T(8,128)(2,1)S(1)}, u32[]{:S(2)}, u32[]{:S(2)}) collective-permute-start(bf16[2,128,384]{2,1,0:T(8,128)(2,1)S(1)} %collective-permute-done.16.refs_16_), channel_id=1, source_target_pairs={{0,1},{1,0},{2,3},{3,2},{4,5},{5,4},{6,7},{7,6},{8,9},{9,8},{10,11... | collective-permute-start | bytes 589832 | tf_op jit(solution)/shard_map/ppermute | solution.py:33
  24.7 2.5 %collective-permute-done.14.refs_14_ = bf16[2,128,384]{2,1,0:T(8,128)(2,1)S(1)} collective-permute-done((bf16[2,128,384]{2,1,0:T(8,128)(2,1)S(1)}, bf16[2,128,384]{2,1,0:T(8,128)(2,1)S(1)}, u32[]{:S(2)}, u32[]{:S(2)}) %collective-permute-start.14) | collective-permute-done | bytes 196640 | tf_op jit(solution)/shard_map/ppermute | solution.py:33
  31.5 4.6 %half_transform.1 = (bf16[4,128,768]{2,1,0:T(8,128)(2,1)S(1)}, bf16[1,128,768]{2,1,0:T(8,128)(2,1)S(1)}, bf16[1,128,768]{2,1,0:T(8,128)(2,1)S(1)}, bf16[1,128,76...) custom-call(s32[1,81]{1,0:T(1,128)S(1)} %pad_add_fusion.meta, ...), custom_call_target="tpu_custom_call" | custom-call | tf_op jit(solution)/shard_map/half_transform/pallas_call | solution.py:121
  38.1 3.2 %collective-permute-start.18 = (bf16[1,128,768]{2,1,0:T(8,128)(2,1)S(1)}, bf16[1,128,768]{2,1,0:T(8,128)(2,1)S(1)}, u32[]{:S(2)}, u32[]{:S(2)}) collective-permute-start(bf16[1,128,768]{2,1,0:T(8,128)(2,1)S(1)} %get-tuple-element.23), channel_id=1, source_target_pairs={{0,6},{1,7},{2,0},{3,1},{4,2},{5,3},{6,4},{7,5},{8,14},{9,15},{10,... | collective-permute-start | bytes 589832 | tf_op jit(solution)/shard_map/ppermute | solution.py:33
  43.8 4.3 %collective-permute-done.22 = bf16[1,128,768]{2,1,0:T(8,128)(2,1)S(1)} collective-permute-done((bf16[1,128,768]{2,1,0:T(8,128)(2,1)S(1)}, bf16[1,128,768]{2,1,0:T(8,128)(2,1)S(1)}, u32[]{:S(2)}, u32[]{:S(2)}) %collective-permute-start.22) | collective-permute-done | bytes 196640 | tf_op jit(solution)/shard_map/ppermute | solution.py:33
  48.5 3.8 %collective-permute-start.21 = (bf16[2,128,768]{2,1,0:T(8,128)(2,1)S(1)}, bf16[2,128,768]{2,1,0:T(8,128)(2,1)S(1)}, u32[]{:S(2)}, u32[]{:S(2)}) collective-permute-start(bf16[2,128,768]{2,1,0:T(8,128)(2,1)S(1)} %pad_maximum_fusion.2), channel_id=1, source_target_pairs={{0,6},{1,7},{2,0},{3,1},{4,2},{5,3},{6,4},{7,5},{8,14},{9,15},{10,... | collective-permute-start | bytes 1179656 | tf_op jit(solution)/shard_map/ppermute | solution.py:33
  54.9 4.6 %collective-permute-done.21.refs_1_ = bf16[2,128,768]{2,1,0:T(8,128)(2,1)S(1)} collective-permute-done((bf16[2,128,768]{2,1,0:T(8,128)(2,1)S(1)}, bf16[2,128,768]{2,1,0:T(8,128)(2,1)S(1)}, u32[]{:S(2)}, u32[]{:S(2)}) %collective-permute-start.21) | collective-permute-done | bytes 393248 | tf_op jit(solution)/shard_map/ppermute | solution.py:33
  59.6 4.1 %collective-permute-start.24 = (bf16[3,128,768]{2,1,0:T(8,128)(2,1)S(1)}, bf16[3,128,768]{2,1,0:T(8,128)(2,1)S(1)}, u32[]{:S(2)}, u32[]{:S(2)}) collective-permute-start(bf16[3,128,768]{2,1,0:T(8,128)(2,1)S(1)} %pad_maximum_fusion), channel_id=1, source_target_pairs={{0,6},{1,7},{2,0},{3,1},{4,2},{5,3},{6,4},{7,5},{8,14},{9,15},{10,... | collective-permute-start | bytes 1769480 | tf_op jit(solution)/shard_map/ppermute | solution.py:33
  65.1 3.8 %collective-permute-done.28.refs_8_.refs_3_ = bf16[3,128,768]{2,1,0:T(8,128)(2,1)S(1)} collective-permute-done((bf16[3,128,768]{2,1,0:T(8,128)(2,1)S(1)}, bf16[3,128,768]{2,1,0:T(8,128)(2,1)S(1)}, u32[]{:S(2)}, u32[]{:S(2)}) %collective-permute-start.28) | collective-permute-done | bytes 589856 | tf_op jit(solution)/shard_map/ppermute | solution.py:33
  70.2 2.9 %collective-permute-start.32 = (bf16[3,128,768]{2,1,0:T(8,128)(2,1)S(1)}, bf16[3,128,768]{2,1,0:T(8,128)(2,1)S(1)}, u32[]{:S(2)}, u32[]{:S(2)}) collective-permute-start(bf16[3,128,768]{2,1,0:T(8,128)(2,1)S(1)} %collective-permute-done.27.refs_7_.refs_2_), channel_id=1, source_target_pairs={{0,1},{1,0},{2,3},{3,2},{4,5},{5,4},{6,7},{7,6},{8,9},{9,8},{10,11... | collective-permute-start | bytes 1769480 | tf_op jit(solution)/shard_map/ppermute | solution.py:33
  74.5 1.8 %collective-permute-start.33 = (bf16[3,128,768]{2,1,0:T(8,128)(2,1)S(1)}, bf16[3,128,768]{2,1,0:T(8,128)(2,1)S(1)}, u32[]{:S(2)}, u32[]{:S(2)}) collective-permute-start(bf16[3,128,768]{2,1,0:T(8,128)(2,1)S(1)} %collective-permute-done.28.refs_8_.refs_3_), channel_id=1, source_target_pairs={{0,1},{1,0},{2,3},{3,2},{4,5},{5,4},{6,7},{7,6},{8,9},{9,8},{10,11... | collective-permute-start | bytes 1769480 | tf_op jit(solution)/shard_map/ppermute | solution.py:33
  76.4 3.0 %collective-permute-done.25.refs_4_ = bf16[1,128,768]{2,1,0:T(8,128)(2,1)S(1)} collective-permute-done((bf16[1,128,768]{2,1,0:T(8,128)(2,1)S(1)}, bf16[1,128,768]{2,1,0:T(8,128)(2,1)S(1)}, u32[]{:S(2)}, u32[]{:S(2)}) %collective-permute-start.25) | collective-permute-done | bytes 196640 | tf_op jit(solution)/shard_map/ppermute | solution.py:33
  79.4 3.3 %collective-permute-start.34 = (bf16[2,192,768]{2,1,0:T(8,128)(2,1)S(1)}, bf16[2,192,768]{2,1,0:T(8,128)(2,1)S(1)}, u32[]{:S(2)}, u32[]{:S(2)}) collective-permute-start(bf16[2,192,768]{2,1,0:T(8,128)(2,1)S(1)} %pad_maximum_fusion.1.refs_9_.refs_4_), channel_id=1, source_target_pairs={{0,1},{1,0},{2,3},{3,2},{4,5},{5,4},{6,7},{7,6},{8,9},{9,8},{10,11... | collective-permute-start | bytes 1769480 | tf_op jit(solution)/shard_map/ppermute | solution.py:33
  82.7 1.6 %collective-permute-done.34.refs_14_.refs_9_ = bf16[2,192,768]{2,1,0:T(8,128)(2,1)S(1)} collective-permute-done((bf16[2,192,768]{2,1,0:T(8,128)(2,1)S(1)}, bf16[2,192,768]{2,1,0:T(8,128)(2,1)S(1)}, u32[]{:S(2)}, u32[]{:S(2)}) %collective-permute-start.34) | collective-permute-done | bytes 589856 | tf_op jit(solution)/shard_map/ppermute | solution.py:33
  84.3 2.3 %pair_blocks.1 = (bf16[1024,128]{1,0:T(8,128)(2,1)S(1)}, bf16[1024,128]{1,0:T(8,128)(2,1)S(1)}) custom-call(bf16[1,128,768]{2,1,0:T(8,128)(2,1)S(1)} %collective-permute-done.18.refs_0_, bf16[2,128,768]{2,1,0:T(8,128)(2,1)S(1)} %collective-permute-done.21.refs_1_, bf16[1,128,768]{2,1,0:T(8,128)(2,1)S(1)} %collective-permute-done.23.refs_2_, ...), custom_call_target="tpu_custom_call" | custom-call | tf_op jit(solution)/shard_map/pair_blocks/pallas_call | solution.py:188
  88.3 1.7 %own_block.1.refs_4_ = f32[1024,512]{1,0:T(8,128)} custom-call(bf16[4,128,768]{2,1,0:T(8,128)(2,1)} %copy-done.5, bf16[3,128,768]{2,1,0:T(8,128)(2,1)} %copy-done.4, bf16[3,128,768]{2,1,0:T(8,128)(2,1)} %copy-done.2, bf16[3,128,768]{2,1,0:T(8,128)(2,1)} %copy-done.3, bf16[2,192,768]{2,1,0:T(8,128)(2,1)} %copy-done.1, bf16[4,128,768]{2,1,0:T(8,128)(2,1)} %copy-done.6, ...), custom_call_target="tpu_custom_call" | custom-call | tf_op jit(solution)/shard_map/own_block/pallas_call | solution.py:248
  90.0 7.7 %collective-permute-done.35 = bf16[1024,128]{1,0:T(8,128)(2,1)S(1)} collective-permute-done((bf16[1024,128]{1,0:T(8,128)(2,1)S(1)}, bf16[1024,128]{1,0:T(8,128)(2,1)S(1)}, u32[]{:S(2)}, u32[]{:S(2)}) %collective-permute-start.35) | collective-permute-done | bytes 262176 | tf_op jit(solution)/shard_map/ppermute | solution.py:33
  98.0 3.1 %collective-permute-start.40 = (bf16[1024,128]{1,0:T(8,128)(2,1)S(1)}, bf16[1024,128]{1,0:T(8,128)(2,1)S(1)}, u32[]{:S(2)}, u32[]{:S(2)}) collective-permute-start(bf16[1024,128]{1,0:T(8,128)(2,1)S(1)} %get-tuple-element.39), channel_id=1, source_target_pairs={{0,24},{1,25},{2,26},{3,27},{4,28},{5,29},{8,16},{9,17},{10,18},{1... | collective-permute-start | bytes 786440 | tf_op jit(solution)/shard_map/ppermute | solution.py:33
  102.4 4.0 %collective-permute-start.38 = (bf16[1024,128]{1,0:T(8,128)(2,1)S(1)}, bf16[1024,128]{1,0:T(8,128)(2,1)S(1)}, u32[]{:S(2)}, u32[]{:S(2)}) collective-permute-start(bf16[1024,128]{1,0:T(8,128)(2,1)S(1)} %get-tuple-element.41), channel_id=1, source_target_pairs={{0,8},{1,9},{4,12},{5,13},{6,14},{7,15},{10,2},{11,3},{12,4},{13,5... | collective-permute-start | bytes 786440 | tf_op jit(solution)/shard_map/ppermute | solution.py:33
  107.9 6.7 %collective-permute-done.39.refs_2_ = bf16[1024,128]{1,0:T(8,128)(2,1)S(1)} collective-permute-done((bf16[1024,128]{1,0:T(8,128)(2,1)S(1)}, bf16[1024,128]{1,0:T(8,128)(2,1)S(1)}, u32[]{:S(2)}, u32[]{:S(2)}) %collective-permute-start.39) | collective-permute-done | bytes 262176 | tf_op jit(solution)/shard_map/ppermute | solution.py:33
  114.6 1.7 %place_blocks.1 = f32[1024,512]{1,0:T(8,128)} custom-call(bf16[1024,128]{1,0:T(8,128)(2,1)S(1)} %get-tuple-element.42.refs_0_, bf16[1024,128]{1,0:T(8,128)(2,1)S(1)} %collective-permute-done.38.refs_1_, bf16[1024,128]{1,0:T(8,128)(2,1)S(1)} %collective-permute-done.39.refs_2_, bf16[1024,128]{1,0:T(8,128)(2,1)S(1)} %collective-permute-done.40.refs_3_, ...), custom_call_target="tpu_custom_call" | custom-call | tf_op jit(solution)/shard_map/place_blocks/pallas_call | solution.py:299
  (107 shorter events, 34.4 us)
Async XLA Ops:
  2.3 7.4 %collective-permute-start.10 = (bf16[1,128,384]{2,1,0:T(8,128)(2,1)S(1)}, bf16[1,128,384]{2,1,0:T(8,128)(2,1)S(1)}, u32[]{:S(2)}, u32[]{:S(2)}) collective-permute-start(bf16[1,128,384]{2,1,0:T(8,128)(2,1)S(1)} %constant_dynamic-slice_fusion), channel_id=1, source_target_pairs={{0,6},{1,7},{2,4},{3,5},{4,2},{5,3},{6,0},{7,1},{8,14},{9,15},{10,... | collective-permute-start | bytes 294920 | tf_op jit(solution)/shard_map/ppermute | solution.py:33
  4.5 9.3 %collective-permute-start.9 = (bf16[1,128,384]{2,1,0:T(8,128)(2,1)S(1)}, bf16[1,128,384]{2,1,0:T(8,128)(2,1)S(1)}, u32[]{:S(2)}, u32[]{:S(2)}) collective-permute-start(bf16[1,128,384]{2,1,0:T(8,128)(2,1)S(1)} %constant_dynamic-slice_fusion), channel_id=1, source_target_pairs={{0,4},{1,5},{2,6},{3,7},{4,0},{5,1},{6,2},{7,3},{8,12},{9,13},{10,... | collective-permute-start | bytes 294920 | tf_op jit(solution)/shard_map/ppermute | solution.py:33
  4.6 23.1 %collective-permute-start = (bf16[4,128,384]{2,1,0:T(8,128)(2,1)}, bf16[4,128,384]{2,1,0:T(8,128)(2,1)S(1)}, u32[]{:S(2)}, u32[]{:S(2)}) collective-permute-start(bf16[4,128,384]{2,1,0:T(8,128)(2,1)} %bitcast.13), channel_id=1, source_target_pairs={{0,1},{1,0},{2,3},{3,2},{4,5},{5,4},{6,7},{7,6},{8,9},{9,8},{10,11... | collective-permute-start | bytes 1179656 | tf_op jit(solution)/shard_map/ppermute | solution.py:33
  6.5 8.2 %collective-permute-start.7 = (bf16[1,128,384]{2,1,0:T(8,128)(2,1)S(1)}, bf16[1,128,384]{2,1,0:T(8,128)(2,1)S(1)}, u32[]{:S(2)}, u32[]{:S(2)}) collective-permute-start(bf16[1,128,384]{2,1,0:T(8,128)(2,1)S(1)} %collective-permute-done.1.refs_2_), channel_id=1, source_target_pairs={{0,24},{1,25},{2,26},{3,27},{4,28},{5,29},{6,30},{7,31},{8,16},{9,... | collective-permute-start | bytes 294920 | tf_op jit(solution)/shard_map/ppermute | solution.py:33
  16.4 10.8 %collective-permute-start.14 = (bf16[2,128,384]{2,1,0:T(8,128)(2,1)S(1)}, bf16[2,128,384]{2,1,0:T(8,128)(2,1)S(1)}, u32[]{:S(2)}, u32[]{:S(2)}) collective-permute-start(bf16[2,128,384]{2,1,0:T(8,128)(2,1)S(1)} %pad_maximum_fusion.7.refs_10_), channel_id=1, source_target_pairs={{0,16},{1,17},{2,18},{3,19},{4,20},{5,21},{6,22},{7,23},{8,24},{9,... | collective-permute-start | bytes 589832 | tf_op jit(solution)/shard_map/ppermute | solution.py:33
  17.7 10.0 %collective-permute-start.12 = (bf16[2,128,384]{2,1,0:T(8,128)(2,1)S(1)}, bf16[2,128,384]{2,1,0:T(8,128)(2,1)S(1)}, u32[]{:S(2)}, u32[]{:S(2)}) collective-permute-start(bf16[2,128,384]{2,1,0:T(8,128)(2,1)S(1)} %pad_maximum_fusion.7.refs_10_), channel_id=1, source_target_pairs={{0,8},{1,9},{2,10},{3,11},{4,12},{5,13},{6,14},{7,15},{8,0},{9,1},... | collective-permute-start | bytes 589832 | tf_op jit(solution)/shard_map/ppermute | solution.py:33
  20.4 7.3 %collective-permute-start.11 = (bf16[2,128,384]{2,1,0:T(8,128)(2,1)S(1)}, bf16[2,128,384]{2,1,0:T(8,128)(2,1)S(1)}, u32[]{:S(2)}, u32[]{:S(2)}) collective-permute-start(bf16[2,128,384]{2,1,0:T(8,128)(2,1)S(1)} %pad_maximum_fusion.7.refs_10_), channel_id=1, source_target_pairs={{0,1},{1,0},{2,3},{3,2},{4,5},{5,4},{6,7},{7,6},{8,9},{9,8},{10,11... | collective-permute-start | bytes 589832 | tf_op jit(solution)/shard_map/ppermute | solution.py:33
  36.2 12.0 %collective-permute-start.26 = (bf16[4,128,768]{2,1,0:T(8,128)(2,1)S(1)}, bf16[4,128,768]{2,1,0:T(8,128)(2,1)S(1)}, u32[]{:S(2)}, u32[]{:S(2)}) collective-permute-start(bf16[4,128,768]{2,1,0:T(8,128)(2,1)S(1)} %get-tuple-element.28.refs_5_.refs_0_), channel_id=1, source_target_pairs={{0,1},{1,0},{2,3},{3,2},{4,5},{5,4},{6,7},{7,6},{8,9},{9,8},{10,11... | collective-permute-start | bytes 2359304 | tf_op jit(solution)/shard_map/ppermute | solution.py:33
  38.1 10.1 %collective-permute-start.18 = (bf16[1,128,768]{2,1,0:T(8,128)(2,1)S(1)}, bf16[1,128,768]{2,1,0:T(8,128)(2,1)S(1)}, u32[]{:S(2)}, u32[]{:S(2)}) collective-permute-start(bf16[1,128,768]{2,1,0:T(8,128)(2,1)S(1)} %get-tuple-element.23), channel_id=1, source_target_pairs={{0,6},{1,7},{2,0},{3,1},{4,2},{5,3},{6,4},{7,5},{8,14},{9,15},{10,... | collective-permute-start | bytes 589832 | tf_op jit(solution)/shard_map/ppermute | solution.py:33
  48.2 15.4 %collective-permute-start.27 = (bf16[3,128,768]{2,1,0:T(8,128)(2,1)S(1)}, bf16[3,128,768]{2,1,0:T(8,128)(2,1)S(1)}, u32[]{:S(2)}, u32[]{:S(2)}) collective-permute-start(bf16[3,128,768]{2,1,0:T(8,128)(2,1)S(1)} %get-tuple-element.30), channel_id=1, source_target_pairs={{0,8},{1,9},{2,10},{3,11},{4,12},{5,13},{6,14},{7,15},{8,0},{9,1},... | collective-permute-start | bytes 1769480 | tf_op jit(solution)/shard_map/ppermute | solution.py:33
  48.5 11.0 %collective-permute-start.21 = (bf16[2,128,768]{2,1,0:T(8,128)(2,1)S(1)}, bf16[2,128,768]{2,1,0:T(8,128)(2,1)S(1)}, u32[]{:S(2)}, u32[]{:S(2)}) collective-permute-start(bf16[2,128,768]{2,1,0:T(8,128)(2,1)S(1)} %pad_maximum_fusion.2), channel_id=1, source_target_pairs={{0,6},{1,7},{2,0},{3,1},{4,2},{5,3},{6,4},{7,5},{8,14},{9,15},{10,... | collective-permute-start | bytes 1179656 | tf_op jit(solution)/shard_map/ppermute | solution.py:33
  52.3 11.4 %collective-permute-start.29 = (bf16[3,128,768]{2,1,0:T(8,128)(2,1)S(1)}, bf16[3,128,768]{2,1,0:T(8,128)(2,1)S(1)}, u32[]{:S(2)}, u32[]{:S(2)}) collective-permute-start(bf16[3,128,768]{2,1,0:T(8,128)(2,1)S(1)} %constant_dynamic-update-slice_fusion.refs_6_.refs_1_), channel_id=1, source_target_pairs={{0,1},{1,0},{2,3},{3,2},{4,5},{5,4},{6,7},{7,6},{8,9},{9,8},{10,11... | collective-permute-start | bytes 1769480 | tf_op jit(solution)/shard_map/ppermute | solution.py:33
  53.7 15.3 %collective-permute-start.23 = (bf16[1,128,768]{2,1,0:T(8,128)(2,1)S(1)}, bf16[1,128,768]{2,1,0:T(8,128)(2,1)S(1)}, u32[]{:S(2)}, u32[]{:S(2)}) collective-permute-start(bf16[1,128,768]{2,1,0:T(8,128)(2,1)S(1)} %collective-permute-done.22), channel_id=1, source_target_pairs={{0,6},{1,7},{2,0},{3,1},{4,2},{5,3},{6,4},{7,5},{8,14},{9,15},{10,... | collective-permute-start | bytes 589832 | tf_op jit(solution)/shard_map/ppermute | solution.py:33
  54.3 14.6 %collective-permute-start.28 = (bf16[3,128,768]{2,1,0:T(8,128)(2,1)S(1)}, bf16[3,128,768]{2,1,0:T(8,128)(2,1)S(1)}, u32[]{:S(2)}, u32[]{:S(2)}) collective-permute-start(bf16[3,128,768]{2,1,0:T(8,128)(2,1)S(1)} %get-tuple-element.32), channel_id=1, source_target_pairs={{0,16},{1,17},{2,18},{3,19},{4,20},{5,21},{6,22},{7,23},{8,24},{9,... | collective-permute-start | bytes 1769480 | tf_op jit(solution)/shard_map/ppermute | solution.py:33
  59.6 19.8 %collective-permute-start.24 = (bf16[3,128,768]{2,1,0:T(8,128)(2,1)S(1)}, bf16[3,128,768]{2,1,0:T(8,128)(2,1)S(1)}, u32[]{:S(2)}, u32[]{:S(2)}) collective-permute-start(bf16[3,128,768]{2,1,0:T(8,128)(2,1)S(1)} %pad_maximum_fusion), channel_id=1, source_target_pairs={{0,6},{1,7},{2,0},{3,1},{4,2},{5,3},{6,4},{7,5},{8,14},{9,15},{10,... | collective-permute-start | bytes 1769480 | tf_op jit(solution)/shard_map/ppermute | solution.py:33
  63.8 10.8 %collective-permute-start.30 = (bf16[192,768]{1,0:T(8,128)(2,1)S(1)}, bf16[192,768]{1,0:T(8,128)(2,1)S(1)}, u32[]{:S(2)}, u32[]{:S(2)}) collective-permute-start(bf16[192,768]{1,0:T(8,128)(2,1)S(1)} %pad_maximum_fusion.3), channel_id=1, source_target_pairs={{0,16},{1,17},{2,18},{3,19},{4,20},{5,21},{6,22},{7,23},{8,24},{9,... | collective-permute-start | bytes 884744 | tf_op jit(solution)/shard_map/ppermute | solution.py:33
  69.0 7.3 %collective-permute-start.31 = (bf16[192,768]{1,0:T(8,128)(2,1)S(1)}, bf16[192,768]{1,0:T(8,128)(2,1)S(1)}, u32[]{:S(2)}, u32[]{:S(2)}) collective-permute-start(bf16[192,768]{1,0:T(8,128)(2,1)S(1)} %pad_maximum_fusion.4), channel_id=1, source_target_pairs={{0,8},{1,9},{2,10},{3,11},{4,12},{5,13},{6,14},{7,15},{8,0},{9,1},... | collective-permute-start | bytes 884744 | tf_op jit(solution)/shard_map/ppermute | solution.py:33
  70.0 9.4 %collective-permute-start.25 = (bf16[1,128,768]{2,1,0:T(8,128)(2,1)S(1)}, bf16[1,128,768]{2,1,0:T(8,128)(2,1)S(1)}, u32[]{:S(2)}, u32[]{:S(2)}) collective-permute-start(bf16[1,128,768]{2,1,0:T(8,128)(2,1)S(1)} %collective-permute-done.23.refs_2_), channel_id=1, source_target_pairs={{0,6},{1,7},{2,0},{3,1},{4,2},{5,3},{6,4},{7,5},{8,14},{9,15},{10,... | collective-permute-start | bytes 589832 | tf_op jit(solution)/shard_map/ppermute | solution.py:33
  70.2 12.5 %collective-permute-start.32 = (bf16[3,128,768]{2,1,0:T(8,128)(2,1)S(1)}, bf16[3,128,768]{2,1,0:T(8,128)(2,1)S(1)}, u32[]{:S(2)}, u32[]{:S(2)}) collective-permute-start(bf16[3,128,768]{2,1,0:T(8,128)(2,1)S(1)} %collective-permute-done.27.refs_7_.refs_2_), channel_id=1, source_target_pairs={{0,1},{1,0},{2,3},{3,2},{4,5},{5,4},{6,7},{7,6},{8,9},{9,8},{10,11... | collective-permute-start | bytes 1769480 | tf_op jit(solution)/shard_map/ppermute | solution.py:33
  74.5 8.2 %collective-permute-start.33 = (bf16[3,128,768]{2,1,0:T(8,128)(2,1)S(1)}, bf16[3,128,768]{2,1,0:T(8,128)(2,1)S(1)}, u32[]{:S(2)}, u32[]{:S(2)}) collective-permute-start(bf16[3,128,768]{2,1,0:T(8,128)(2,1)S(1)} %collective-permute-done.28.refs_8_.refs_3_), channel_id=1, source_target_pairs={{0,1},{1,0},{2,3},{3,2},{4,5},{5,4},{6,7},{7,6},{8,9},{9,8},{10,11... | collective-permute-start | bytes 1769480 | tf_op jit(solution)/shard_map/ppermute | solution.py:33
  87.2 10.5 %collective-permute-start.35 = (bf16[1024,128]{1,0:T(8,128)(2,1)S(1)}, bf16[1024,128]{1,0:T(8,128)(2,1)S(1)}, u32[]{:S(2)}, u32[]{:S(2)}) collective-permute-start(bf16[1024,128]{1,0:T(8,128)(2,1)S(1)} %get-tuple-element.36), channel_id=1, source_target_pairs={{0,2},{1,3},{2,4},{3,5},{4,6},{5,7},{6,0},{7,1},{8,10},{9,11},{10,... | collective-permute-start | bytes 786440 | tf_op jit(solution)/shard_map/ppermute | solution.py:33
  98.0 10.0 %collective-permute-start.40 = (bf16[1024,128]{1,0:T(8,128)(2,1)S(1)}, bf16[1024,128]{1,0:T(8,128)(2,1)S(1)}, u32[]{:S(2)}, u32[]{:S(2)}) collective-permute-start(bf16[1024,128]{1,0:T(8,128)(2,1)S(1)} %get-tuple-element.39), channel_id=1, source_target_pairs={{0,24},{1,25},{2,26},{3,27},{4,28},{5,29},{8,16},{9,17},{10,18},{1... | collective-permute-start | bytes 786440 | tf_op jit(solution)/shard_map/ppermute | solution.py:33
  101.1 13.5 %collective-permute-start.39 = (bf16[1024,128]{1,0:T(8,128)(2,1)S(1)}, bf16[1024,128]{1,0:T(8,128)(2,1)S(1)}, u32[]{:S(2)}, u32[]{:S(2)}) collective-permute-start(bf16[1024,128]{1,0:T(8,128)(2,1)S(1)} %get-tuple-element.40), channel_id=1, source_target_pairs={{0,16},{1,17},{2,18},{3,19},{6,22},{7,23},{8,24},{9,25},{10,26},{1... | collective-permute-start | bytes 786440 | tf_op jit(solution)/shard_map/ppermute | solution.py:33
  102.4 12.2 %collective-permute-start.38 = (bf16[1024,128]{1,0:T(8,128)(2,1)S(1)}, bf16[1024,128]{1,0:T(8,128)(2,1)S(1)}, u32[]{:S(2)}, u32[]{:S(2)}) collective-permute-start(bf16[1024,128]{1,0:T(8,128)(2,1)S(1)} %get-tuple-element.41), channel_id=1, source_target_pairs={{0,8},{1,9},{4,12},{5,13},{6,14},{7,15},{10,2},{11,3},{12,4},{13,5... | collective-permute-start | bytes 786440 | tf_op jit(solution)/shard_map/ppermute | solution.py:33
  (30 other events, 305.8 us)

commit v5 on v3

--- a/solution.py
+++ b/solution.py
@@ -102,13 +102,10 @@
             outs[0][row, :, columns] = value
             if mirrored:
                 outs[1 + row][0, :, columns] = value
-                for place in range(1, own_blocks):
-                    if place != row:
-                        outs[own_blocks + place][(place ^ row) - 1, :, columns] = value
 
 
 def plane_groups(planes):
-    return [list(range(1, 2)), list(range(2, planes))] if planes > 2 else [list(range(1, planes))]
+    return [list(range(1, planes))]
 
 
 def half_transform(lay, share, mirrored, own_blocks, integrals, pieces, meta):
@@ -117,7 +114,7 @@
     blocks = sum(piece.shape[0] for piece in pieces)
     sizes = [own_blocks]
     if mirrored:
-        sizes += [1] * own_blocks + [own_blocks - 1] * (own_blocks - 1)
+        sizes += [1] * own_blocks
     return pl.pallas_call(
         functools.partial(half_kernel, lay, share, len(pieces), mirrored),
         out_shape=[jax.ShapeDtypeStruct((size, block, aux_count * orbitals), jnp.bfloat16) for size in sizes],
@@ -141,59 +138,39 @@
     return lax.dot_general(first, second, ROWS, preferred_element_type=jnp.float32)
 
 
-STEPS = ([[0], [1, 2, 3]], [[0], [1, 2, 3]])
-HELD = 5
-
-
-def core_parts(held, s, k):
-    whole, near, *rest = held[s * HELD : (s + 1) * HELD]
-    depth = whole.shape[2]
-    if k == 0:
-        return [whole[...].reshape(-1, depth)]
-    return [near[k - 1], rest[k - 1][...].reshape(-1, depth)]
-
-
 def pair_kernel(*refs):
-    held, outs = refs[-len(STEPS) - CORES * HELD : -len(STEPS)], refs[-len(STEPS) :]
-    count, n, _ = held[0].shape
-    quarters = [[] for _ in range(count)]
-    at = 0
-    for step in STEPS:
-        for group in step:
-            for place, k in enumerate(group):
-                quarters[k].append(refs[at][place])
-            at += 1
-    quarters = [jnp.concatenate(parts, axis=0) for parts in quarters]
+    *ins, near_ref, far_ref = refs
+    rows, held = ins[:2], ins[2:]
+    count, n, depth = held[0].shape
     for s in range(CORES):
-        start = s * count * n
-        lower = upper = None
+        totals = [None] * count
         for k in range(count):
-            parts = [dot_rows(part, quarters[k]) for part in core_parts(held, s, k)]
-            if k == 0:
-                lower, upper = parts[0][:n], parts[0][n:]
-            else:
-                lower, upper = lower + parts[0], upper + parts[1]
-        for d, out in enumerate(outs):
-            out[pl.ds(start, n), :] = lower[:, d * n : (d + 1) * n].astype(jnp.bfloat16)
-            out[pl.ds(start + n, (count - 1) * n), :] = upper[:, d * n : (d + 1) * n].astype(jnp.bfloat16)
+            quarter = jnp.concatenate([part[k] for part in rows], axis=0)
+            value = dot_rows(held[s * count + k][...].reshape(count * n, depth), quarter)
+            for m in range(count):
+                part = value[(m ^ k) * n : ((m ^ k) + 1) * n]
+                totals[m] = part if totals[m] is None else totals[m] + part
+        for m in range(count):
+            at = pl.ds((s * count + m) * n, n)
+            near_ref[at, :] = totals[m][:, :n].astype(jnp.bfloat16)
+            far_ref[at, :] = totals[m][:, n:].astype(jnp.bfloat16)
 
 
 def pair_blocks(rows, held):
     count, n, _ = held[0].shape
-    flat = [part for parts in rows for part in parts]
     shape = jax.ShapeDtypeStruct((CORES * count * n, n), jnp.bfloat16)
     return pl.pallas_call(
         pair_kernel,
-        out_shape=[shape] * len(STEPS),
-        in_specs=[IN_VMEM] * (len(flat) + len(held)),
-        out_specs=[IN_VMEM] * len(STEPS),
+        out_shape=[shape] * len(rows),
+        in_specs=[IN_VMEM] * (len(rows) + len(held)),
+        out_specs=[IN_VMEM] * len(rows),
         compiler_params=pltpu.CompilerParams(vmem_limit_bytes=VMEM_LIMIT),
         name="pair_blocks",
-    )(*flat, *held)
+    )(*rows, *held)
 
 
 def own_kernel(*refs):
-    *held, _, out_ref, plane, sems = refs
+    *held, out_ref, plane, sems = refs
     _, count, rows, depth = plane.shape
     n = rows // count
     a = lax.axis_index("aux")
@@ -201,11 +178,8 @@
     z, c = occ_index // CORES, occ_index % CORES
 
     def moves(s, k):
-        whole, near, *rest = held[s * HELD : (s + 1) * HELD]
-        parts = [(whole if k == 0 else rest[k - 1]).at[m] for m in range(count if k == 0 else count - 1)]
-        if k:
-            parts = [near.at[k - 1]] + parts
-        return [pltpu.make_async_copy(x, plane.at[s, k, pl.ds(m * n, n)], sems.at[s, k, m]) for m, x in enumerate(parts)]
+        parts = [(held[s * count + k].at[m ^ k], plane.at[s, k, pl.ds(m * n, n)]) for m in range(count)]
+        return [pltpu.make_async_copy(x, y, sems.at[s, k, m]) for m, (x, y) in enumerate(parts)]
 
     @pl.when(a == z)
     def _():
@@ -229,12 +203,12 @@
                     ]
 
 
-def own_block(held, earlier):
+def own_block(held):
     count, n, depth = held[0].shape
     return pl.pallas_call(
         own_kernel,
         out_shape=jax.ShapeDtypeStruct((CORES * count * n, count * n), jnp.float32),
-        in_specs=[ANY] * (len(held) + 1),
+        in_specs=[ANY] * len(held),
         out_specs=IN_VMEM,
         scratch_shapes=[
             pltpu.VMEM((CORES, count, count * n, depth), jnp.bfloat16),
@@ -242,7 +216,7 @@
         ],
         compiler_params=pltpu.CompilerParams(vmem_limit_bytes=VMEM_MOST),
         name="own_block",
-    )(*held, earlier)
+    )(*held)
 
 
 def place_kernel(*refs):
@@ -300,27 +274,24 @@
     count, n, _ = half.shape
     a = lax.axis_index("aux")
     z = lax.axis_index("occ") // CORES
-    others = range(1, count)
     other = lambda v: lay.send(v, lambda a_, z_, c_: (a_, z_, 1 - c_))
     toward = lambda v, k: lay.send(v, lambda a_, z_, c_: (a_ ^ k, z_, c_))
-    below = lambda v: lay.send(v, lambda a_, z_, c_: (a_, (z_ - 1) % count, c_))
-
-    near = jnp.concatenate([toward(sent[k], k) for k in others])
-    first, later = [sent[0]], [near]
-    for _ in STEPS:
-        first.append(below(first[-1]))
-    for d in range(len(STEPS)):
-        later.append(below(after(later[-1], first[-1]) if d == 0 else later[-1]))
-    rest = [toward(after(sent[count - 1 + k], near), k) for k in others]
-    own = [half, near] + rest
-    held = own + [other(v) for v in own[:-1]] + [other(after(own[-1], later[-1]))]
-
-    ahead = pair_blocks(list(zip(first[1:], later[1:])), held)
-    mirror = lay.send(ahead[0], lambda a_, z_, c_: (a_, (z_ + 1) % count, c_))
-    out = own_block(held, ahead[1])
+    below = lambda v, k=0: lay.send(v, lambda a_, z_, c_: (a_ ^ k, (z_ - 1) % count, c_))
+
+    ahead = [below(sent[k], k) for k in range(count)]
+    rows = [jnp.concatenate(ahead)]
+    rows.append(below(rows[0]))
+    first, second = (toward(half, k) for k in (1, 2))
+    passed = jnp.concatenate([toward(first[: count // 2], 2), toward(second[count // 2 :], 1)])
+    held = [half, first, second, passed]
+    held += [other(v) for v in held[:-1]] + [other(after(passed, rows[1]))]
+
+    blocks = pair_blocks(rows, held)
+    mirror = lay.send(blocks[0], lambda a_, z_, c_: (a_, (z_ + 1) % count, c_))
+    out = own_block(held)
     width = count * n
-    ahead = [jnp.concatenate([v[:width], other(v[width:])]) for v in ahead]
-    apart = {1: ahead[0], 2: ahead[1], 3: after(mirror, out)}
+    blocks = [jnp.concatenate([v[:width], other(v[width:])]) for v in blocks]
+    apart = {1: blocks[0], 2: after(blocks[1], out), 3: mirror}
 
     quarters = []
     for k in range(count):
@@ -376,6 +347,8 @@
     for group in plane_groups(planes):
         far = [lay.send(mine, lambda a_, z_, c_, d=d: (a_, z_ ^ d, c_)) for d in group]
         far = jnp.concatenate(far, axis=0) if len(far) > 1 else far[0]
+        if group[-1] == planes - 1:
+            far = after(far, meta)
         for k in range(share):
             piece = lay.send(far, lambda a_, z_, c_, k=k: (a_ ^ k, z_, c_)) if k else far
             pieces += [piece, other(piece)]

time: 119 us -> 112 us (0.941)
  starting transfers between devices: 53.3 us -> 37.8 us
  waiting for transfers between devices: 46.9 us -> 59.1 us
  other arithmetic: 2.84 us -> 1.09 us
  local copies, waits for them, and re-layouts: 5.04 us -> 3.54 us
    ppermute x39 -> x30, starting transfers between devices: 53.3 us -> 37.8 us  [send(): return lax.ppermute(value, AXES, pairs)]
    ppermute x39 -> x30, waiting for transfers between devices: 46.9 us -> 59.1 us  [send(): return lax.ppermute(value, AXES, pairs)]
    select_n x2 -> x1, other arithmetic: 2.07 us -> 0.26 us  [mirrored_exchange(): value = jnp.where(distance == d, apart[d], value)]
    pallas_call x1, Pallas kernels: 2.95 us -> 4.23 us  [half_transform(): pl.pallas_call(functools.partial(half_kernel, lay, share, len(pieces), mi...]
    unnamed x33 -> x26, local copies, waits for them, and re-layouts: 3.1 us -> 2.51 us
  transfers between devices with their start and end apart: 39 -> 30, of which waited for: 13 -> 16; matrix products, arithmetic and copies ran while one was open for 2% -> 1% of each run, Pallas kernels for 1% -> 1%
where the time goes in v5:
time: 112 us
  waiting for transfers between devices  59.1 us (53%)
  starting transfers between devices  37.8 us (34%)
  Pallas kernels  9.4 us (8%)
  local copies, waits for them, and re-layouts  3.54 us (3%)
    ppermute x30, waiting for transfers between devices, send(): return lax.ppermute(value, AXES, pairs)  59.1 us
    ppermute x30, starting transfers between devices, send(): return lax.ppermute(value, AXES, pairs)  37.8 us
    pallas_call x1, Pallas kernels, half_transform(): pl.pallas_call(functools.partial(half_kernel, lay, share, len(pieces), mi...  4.23 us
    unnamed x26, local copies, waits for them, and re-layouts  2.51 us
  transfers between devices with their start and end apart: 30, of which 16 were waited for; matrix products, arithmetic and copies ran while one was open for 1% of the time, Pallas kernels for 1%

profile of v5, /device:TPU:5, one launch (start us, length us, event | category | flops | bytes accessed | tf_op | source)
XLA Modules:
  0.0 111.9 jit_solution(878147584405113148)
XLA Ops:
  0.9 3.4 %collective-permute-start.3 = (bf16[1,128,384]{2,1,0:T(8,128)(2,1)S(1)}, bf16[1,128,384]{2,1,0:T(8,128)(2,1)S(1)}, u32[]{:S(2)}, u32[]{:S(2)}) collective-permute-start(bf16[1,128,384]{2,1,0:T(8,128)(2,1)S(1)} %constant_dynamic-slice_fusion), channel_id=1, source_target_pairs={{0,6},{1,7},{2,4},{3,5},{4,2},{5,3},{6,0},{7,1},{8,14},{9,15},{10,... | collective-permute-start | bytes 294920 | tf_op jit(solution)/shard_map/ppermute | solution.py:33
  6.7 5.5 %collective-permute-done.2 = bf16[1,128,384]{2,1,0:T(8,128)(2,1)S(1)} collective-permute-done((bf16[1,128,384]{2,1,0:T(8,128)(2,1)S(1)}, bf16[1,128,384]{2,1,0:T(8,128)(2,1)S(1)}, u32[]{:S(2)}, u32[]{:S(2)}) %collective-permute-start.2) | collective-permute-done | bytes 98336 | tf_op jit(solution)/shard_map/ppermute | solution.py:33
  14.9 2.2 %collective-permute-start = (bf16[4,128,384]{2,1,0:T(8,128)(2,1)}, bf16[4,128,384]{2,1,0:T(8,128)(2,1)S(1)}, u32[]{:S(2)}, u32[]{:S(2)}) collective-permute-start(bf16[4,128,384]{2,1,0:T(8,128)(2,1)} %bitcast.3), channel_id=1, source_target_pairs={{0,1},{1,0},{2,3},{3,2},{4,5},{5,4},{6,7},{7,6},{8,9},{9,8},{10,11... | collective-permute-start | bytes 1179656 | tf_op jit(solution)/shard_map/ppermute | solution.py:33
  17.1 3.2 %collective-permute-done.9.refs_8_ = bf16[3,128,384]{2,1,0:T(8,128)(2,1)S(1)} collective-permute-done((bf16[3,128,384]{2,1,0:T(8,128)(2,1)S(1)}, bf16[3,128,384]{2,1,0:T(8,128)(2,1)S(1)}, u32[]{:S(2)}, u32[]{:S(2)}) %collective-permute-start.9) | collective-permute-done | bytes 294944 | tf_op jit(solution)/shard_map/ppermute | solution.py:33
  20.4 4.1 %collective-permute-start.10 = (bf16[3,128,384]{2,1,0:T(8,128)(2,1)S(1)}, bf16[3,128,384]{2,1,0:T(8,128)(2,1)S(1)}, u32[]{:S(2)}, u32[]{:S(2)}) collective-permute-start(bf16[3,128,384]{2,1,0:T(8,128)(2,1)S(1)} %collective-permute-done.9.refs_8_), channel_id=1, source_target_pairs={{0,1},{1,0},{2,3},{3,2},{4,5},{5,4},{6,7},{7,6},{8,9},{9,8},{10,11... | collective-permute-start | bytes 884744 | tf_op jit(solution)/shard_map/ppermute | solution.py:33
  24.5 3.9 %collective-permute-done.7.refs_6_ = bf16[3,128,384]{2,1,0:T(8,128)(2,1)S(1)} collective-permute-done((bf16[3,128,384]{2,1,0:T(8,128)(2,1)S(1)}, bf16[3,128,384]{2,1,0:T(8,128)(2,1)S(1)}, u32[]{:S(2)}, u32[]{:S(2)}) %collective-permute-start.7) | collective-permute-done | bytes 294944 | tf_op jit(solution)/shard_map/ppermute | solution.py:33
  33.0 4.2 %half_transform.1 = (bf16[4,128,768]{2,1,0:T(8,128)(2,1)S(1)}, bf16[1,128,768]{2,1,0:T(8,128)(2,1)S(1)}, bf16[1,128,768]{2,1,0:T(8,128)(2,1)S(1)}, bf16[1,128,76...) custom-call(s32[1,81]{1,0:T(1,128)S(1)} %pad_add_fusion.meta, bf16[2,24,128,128]{3,2,1,0:T(8,128)(2,1)S(1)} %copy-done.9, ...), custom_call_target="tpu_custom_call" | custom-call | tf_op jit(solution)/shard_map/half_transform/pallas_call | solution.py:118
  38.9 2.2 %collective-permute-start.17 = (bf16[4,128,768]{2,1,0:T(8,128)(2,1)S(1)}, bf16[4,128,768]{2,1,0:T(8,128)(2,1)S(1)}, u32[]{:S(2)}, u32[]{:S(2)}) collective-permute-start(bf16[4,128,768]{2,1,0:T(8,128)(2,1)S(1)} %get-tuple-element.20.refs_2_.refs_0_), channel_id=1, source_target_pairs={{0,16},{1,17},{2,18},{3,19},{4,20},{5,21},{6,22},{7,23},{8,24},{9,... | collective-permute-start | bytes 2359304 | tf_op jit(solution)/shard_map/ppermute | solution.py:33
  41.1 1.6 %collective-permute-done.11 = bf16[1,128,768]{2,1,0:T(8,128)(2,1)S(1)} collective-permute-done((bf16[1,128,768]{2,1,0:T(8,128)(2,1)S(1)}, bf16[1,128,768]{2,1,0:T(8,128)(2,1)S(1)}, u32[]{:S(2)}, u32[]{:S(2)}) %collective-permute-start.11) | collective-permute-done | bytes 196640 | tf_op jit(solution)/shard_map/ppermute | solution.py:33
  42.7 3.0 %collective-permute-start.14 = (bf16[1,128,768]{2,1,0:T(8,128)(2,1)S(1)}, bf16[1,128,768]{2,1,0:T(8,128)(2,1)S(1)}, u32[]{:S(2)}, u32[]{:S(2)}) collective-permute-start(bf16[1,128,768]{2,1,0:T(8,128)(2,1)S(1)} %get-tuple-element.19), channel_id=1, source_target_pairs={{0,30},{1,31},{2,24},{3,25},{4,26},{5,27},{6,28},{7,29},{8,22},{9,... | collective-permute-start | bytes 589832 | tf_op jit(solution)/shard_map/ppermute | solution.py:33
  45.8 5.8 %collective-permute-done.13 = bf16[1,128,768]{2,1,0:T(8,128)(2,1)S(1)} collective-permute-done((bf16[1,128,768]{2,1,0:T(8,128)(2,1)S(1)}, bf16[1,128,768]{2,1,0:T(8,128)(2,1)S(1)}, u32[]{:S(2)}, u32[]{:S(2)}) %collective-permute-start.13) | collective-permute-done | bytes 196640 | tf_op jit(solution)/shard_map/ppermute | solution.py:33
  51.6 6.0 %collective-permute-done.14 = bf16[1,128,768]{2,1,0:T(8,128)(2,1)S(1)} collective-permute-done((bf16[1,128,768]{2,1,0:T(8,128)(2,1)S(1)}, bf16[1,128,768]{2,1,0:T(8,128)(2,1)S(1)}, u32[]{:S(2)}, u32[]{:S(2)}) %collective-permute-start.14) | collective-permute-done | bytes 196640 | tf_op jit(solution)/shard_map/ppermute | solution.py:33
  58.5 5.8 %collective-permute-done.16.refs_3_.refs_1_ = bf16[4,128,768]{2,1,0:T(8,128)(2,1)S(1)} collective-permute-done((bf16[4,128,768]{2,1,0:T(8,128)(2,1)S(1)}, bf16[4,128,768]{2,1,0:T(8,128)(2,1)S(1)}, u32[]{:S(2)}, u32[]{:S(2)}) %collective-permute-start.16) | collective-permute-done | bytes 786464 | tf_op jit(solution)/shard_map/ppermute | solution.py:33
  64.3 3.4 %collective-permute-start.18 = (bf16[2,128,768]{2,1,0:T(8,128)(2,1)S(1)}, bf16[2,128,768]{2,1,0:T(8,128)(2,1)S(1)}, u32[]{:S(2)}, u32[]{:S(2)}) collective-permute-start(bf16[2,128,768]{2,1,0:T(8,128)(2,1)S(1)} %slice.24), channel_id=1, source_target_pairs={{0,16},{1,17},{2,18},{3,19},{4,20},{5,21},{6,22},{7,23},{8,24},{9,... | collective-permute-start | bytes 1179656 | tf_op jit(solution)/shard_map/ppermute | solution.py:33
  69.0 7.5 %collective-permute-done.18 = bf16[2,128,768]{2,1,0:T(8,128)(2,1)S(1)} collective-permute-done((bf16[2,128,768]{2,1,0:T(8,128)(2,1)S(1)}, bf16[2,128,768]{2,1,0:T(8,128)(2,1)S(1)}, u32[]{:S(2)}, u32[]{:S(2)}) %collective-permute-start.18) | collective-permute-done | bytes 393248 | tf_op jit(solution)/shard_map/ppermute | solution.py:33
  77.8 1.6 %collective-permute-start.23 = (bf16[4,128,768]{2,1,0:T(8,128)(2,1)S(1)}, bf16[4,128,768]{2,1,0:T(8,128)(2,1)S(1)}, u32[]{:S(2)}, u32[]{:S(2)}) collective-permute-start(bf16[4,128,768]{2,1,0:T(8,128)(2,1)S(1)} %constant_dynamic-update-slice_fusion.4.refs_5_.refs_3_), channel_id=1, source_target_pairs={{0,1},{1,0},{2,3},{3,2},{4,5},{5,4},{6,7},{7,6},{8,9},{9,8},{10,11... | collective-permute-start | bytes 2359304 | tf_op jit(solution)/shard_map/ppermute | solution.py:33
  79.7 1.7 %collective-permute-done.23.refs_9_.refs_7_ = bf16[4,128,768]{2,1,0:T(8,128)(2,1)S(1)} collective-permute-done((bf16[4,128,768]{2,1,0:T(8,128)(2,1)S(1)}, bf16[4,128,768]{2,1,0:T(8,128)(2,1)S(1)}, u32[]{:S(2)}, u32[]{:S(2)}) %collective-permute-start.23) | collective-permute-done | bytes 786464 | tf_op jit(solution)/shard_map/ppermute | solution.py:33
  81.3 1.8 %pair_blocks.1 = (bf16[1024,128]{1,0:T(8,128)(2,1)S(1)}, bf16[1024,128]{1,0:T(8,128)(2,1)S(1)}) custom-call(bf16[4,128,768]{2,1,0:T(8,128)(2,1)S(1)} %constant_dynamic-update-slice_fusion.refs_0_, bf16[4,128,768]{2,1,0:T(8,128)(2,1)S(1)} %collective-permute-done.15.refs_1_, bf16[4,128,768]{2,1,0:T(8,128)(2,1)S(1)} %get-tuple-element.20.refs_2_.refs_0_, ...), custom_call_target="tpu_custom_call" | custom-call | tf_op jit(solution)/shard_map/pair_blocks/pallas_call | solution.py:162
  84.1 1.6 %own_block.1.refs_4_ = f32[1024,512]{1,0:T(8,128)} custom-call(bf16[4,128,768]{2,1,0:T(8,128)(2,1)} %copy-done.4, bf16[4,128,768]{2,1,0:T(8,128)(2,1)} %copy-done.1, bf16[4,128,768]{2,1,0:T(8,128)(2,1)} %copy-done.2, bf16[4,128,768]{2,1,0:T(8,128)(2,1)} %copy-done.3, bf16[4,128,768]{2,1,0:T(8,128)(2,1)} %copy-done.5, bf16[4,128,768]{2,1,0:T(8,128)(2,1)} %copy-done.7, ...), custom_call_target="tpu_custom_call" | custom-call | tf_op jit(solution)/shard_map/own_block/pallas_call | solution.py:208
  85.8 7.5 %collective-permute-done.24 = bf16[1024,128]{1,0:T(8,128)(2,1)S(1)} collective-permute-done((bf16[1024,128]{1,0:T(8,128)(2,1)S(1)}, bf16[1024,128]{1,0:T(8,128)(2,1)S(1)}, u32[]{:S(2)}, u32[]{:S(2)}) %collective-permute-start.24) | collective-permute-done | bytes 262176 | tf_op jit(solution)/shard_map/ppermute | solution.py:33
  93.5 2.0 %collective-permute-start.29 = (bf16[1024,128]{1,0:T(8,128)(2,1)S(1)}, bf16[1024,128]{1,0:T(8,128)(2,1)S(1)}, u32[]{:S(2)}, u32[]{:S(2)}) collective-permute-start(bf16[1024,128]{1,0:T(8,128)(2,1)S(1)} %get-tuple-element.25), channel_id=1, source_target_pairs={{0,24},{1,25},{2,26},{3,27},{4,28},{5,29},{8,16},{9,17},{10,18},{1... | collective-permute-start | bytes 786440 | tf_op jit(solution)/shard_map/ppermute | solution.py:33
  96.8 5.1 %collective-permute-start.27 = (bf16[1024,128]{1,0:T(8,128)(2,1)S(1)}, bf16[1024,128]{1,0:T(8,128)(2,1)S(1)}, u32[]{:S(2)}, u32[]{:S(2)}) collective-permute-start(bf16[1024,128]{1,0:T(8,128)(2,1)S(1)} %get-tuple-element.27), channel_id=1, source_target_pairs={{0,8},{1,9},{4,12},{5,13},{6,14},{7,15},{10,2},{11,3},{12,4},{13,5... | collective-permute-start | bytes 786440 | tf_op jit(solution)/shard_map/ppermute | solution.py:33
  103.2 6.9 %collective-permute-done.28.refs_2_ = bf16[1024,128]{1,0:T(8,128)(2,1)S(1)} collective-permute-done((bf16[1024,128]{1,0:T(8,128)(2,1)S(1)}, bf16[1024,128]{1,0:T(8,128)(2,1)S(1)}, u32[]{:S(2)}, u32[]{:S(2)}) %collective-permute-start.28) | collective-permute-done | bytes 262176 | tf_op jit(solution)/shard_map/ppermute | solution.py:33
  110.2 1.7 %place_blocks.1 = f32[1024,512]{1,0:T(8,128)} custom-call(bf16[1024,128]{1,0:T(8,128)(2,1)S(1)} %get-tuple-element.28.refs_0_, bf16[1024,128]{1,0:T(8,128)(2,1)S(1)} %collective-permute-done.27.refs_1_, bf16[1024,128]{1,0:T(8,128)(2,1)S(1)} %collective-permute-done.28.refs_2_, bf16[1024,128]{1,0:T(8,128)(2,1)S(1)} %collective-permute-done.29.refs_3_, ...), custom_call_target="tpu_custom_call" | custom-call | tf_op jit(solution)/shard_map/place_blocks/pallas_call | solution.py:259
  (77 shorter events, 19.1 us)
Async XLA Ops:
  0.9 5.8 %collective-permute-start.3 = (bf16[1,128,384]{2,1,0:T(8,128)(2,1)S(1)}, bf16[1,128,384]{2,1,0:T(8,128)(2,1)S(1)}, u32[]{:S(2)}, u32[]{:S(2)}) collective-permute-start(bf16[1,128,384]{2,1,0:T(8,128)(2,1)S(1)} %constant_dynamic-slice_fusion), channel_id=1, source_target_pairs={{0,6},{1,7},{2,4},{3,5},{4,2},{5,3},{6,0},{7,1},{8,14},{9,15},{10,... | collective-permute-start | bytes 294920 | tf_op jit(solution)/shard_map/ppermute | solution.py:33
  4.3 7.9 %collective-permute-start.2 = (bf16[1,128,384]{2,1,0:T(8,128)(2,1)S(1)}, bf16[1,128,384]{2,1,0:T(8,128)(2,1)S(1)}, u32[]{:S(2)}, u32[]{:S(2)}) collective-permute-start(bf16[1,128,384]{2,1,0:T(8,128)(2,1)S(1)} %constant_dynamic-slice_fusion), channel_id=1, source_target_pairs={{0,4},{1,5},{2,6},{3,7},{4,0},{5,1},{6,2},{7,3},{8,12},{9,13},{10,... | collective-permute-start | bytes 294920 | tf_op jit(solution)/shard_map/ppermute | solution.py:33
  4.3 7.9 %collective-permute-start.1 = (bf16[1,128,384]{2,1,0:T(8,128)(2,1)S(1)}, bf16[1,128,384]{2,1,0:T(8,128)(2,1)S(1)}, u32[]{:S(2)}, u32[]{:S(2)}) collective-permute-start(bf16[1,128,384]{2,1,0:T(8,128)(2,1)S(1)} %constant_dynamic-slice_fusion), channel_id=1, source_target_pairs={{0,2},{1,3},{2,0},{3,1},{4,6},{5,7},{6,4},{7,5},{8,10},{9,11},{10,... | collective-permute-start | bytes 294920 | tf_op jit(solution)/shard_map/ppermute | solution.py:33
  12.2 8.2 %collective-permute-start.9 = (bf16[3,128,384]{2,1,0:T(8,128)(2,1)S(1)}, bf16[3,128,384]{2,1,0:T(8,128)(2,1)S(1)}, u32[]{:S(2)}, u32[]{:S(2)}) collective-permute-start(bf16[3,128,384]{2,1,0:T(8,128)(2,1)S(1)} %pad_maximum_fusion.refs_2_), channel_id=1, source_target_pairs={{0,24},{1,25},{2,26},{3,27},{4,28},{5,29},{6,30},{7,31},{8,16},{9,... | collective-permute-start | bytes 884744 | tf_op jit(solution)/shard_map/ppermute | solution.py:33
  13.4 15.0 %collective-permute-start.7 = (bf16[3,128,384]{2,1,0:T(8,128)(2,1)S(1)}, bf16[3,128,384]{2,1,0:T(8,128)(2,1)S(1)}, u32[]{:S(2)}, u32[]{:S(2)}) collective-permute-start(bf16[3,128,384]{2,1,0:T(8,128)(2,1)S(1)} %pad_maximum_fusion.refs_2_), channel_id=1, source_target_pairs={{0,16},{1,17},{2,18},{3,19},{4,20},{5,21},{6,22},{7,23},{8,24},{9,... | collective-permute-start | bytes 884744 | tf_op jit(solution)/shard_map/ppermute | solution.py:33
  14.7 14.3 %collective-permute-start.5 = (bf16[3,128,384]{2,1,0:T(8,128)(2,1)S(1)}, bf16[3,128,384]{2,1,0:T(8,128)(2,1)S(1)}, u32[]{:S(2)}, u32[]{:S(2)}) collective-permute-start(bf16[3,128,384]{2,1,0:T(8,128)(2,1)S(1)} %pad_maximum_fusion.refs_2_), channel_id=1, source_target_pairs={{0,8},{1,9},{2,10},{3,11},{4,12},{5,13},{6,14},{7,15},{8,0},{9,1},... | collective-permute-start | bytes 884744 | tf_op jit(solution)/shard_map/ppermute | solution.py:33
  14.9 14.0 %collective-permute-start = (bf16[4,128,384]{2,1,0:T(8,128)(2,1)}, bf16[4,128,384]{2,1,0:T(8,128)(2,1)S(1)}, u32[]{:S(2)}, u32[]{:S(2)}) collective-permute-start(bf16[4,128,384]{2,1,0:T(8,128)(2,1)} %bitcast.3), channel_id=1, source_target_pairs={{0,1},{1,0},{2,3},{3,2},{4,5},{5,4},{6,7},{7,6},{8,9},{9,8},{10,11... | collective-permute-start | bytes 1179656 | tf_op jit(solution)/shard_map/ppermute | solution.py:33
  17.1 11.8 %collective-permute-start.4 = (bf16[3,128,384]{2,1,0:T(8,128)(2,1)S(1)}, bf16[3,128,384]{2,1,0:T(8,128)(2,1)S(1)}, u32[]{:S(2)}, u32[]{:S(2)}) collective-permute-start(bf16[3,128,384]{2,1,0:T(8,128)(2,1)S(1)} %pad_maximum_fusion.refs_2_), channel_id=1, source_target_pairs={{0,1},{1,0},{2,3},{3,2},{4,5},{5,4},{6,7},{7,6},{8,9},{9,8},{10,11... | collective-permute-start | bytes 884744 | tf_op jit(solution)/shard_map/ppermute | solution.py:33
  20.4 8.6 %collective-permute-start.10 = (bf16[3,128,384]{2,1,0:T(8,128)(2,1)S(1)}, bf16[3,128,384]{2,1,0:T(8,128)(2,1)S(1)}, u32[]{:S(2)}, u32[]{:S(2)}) collective-permute-start(bf16[3,128,384]{2,1,0:T(8,128)(2,1)S(1)} %collective-permute-done.9.refs_8_), channel_id=1, source_target_pairs={{0,1},{1,0},{2,3},{3,2},{4,5},{5,4},{6,7},{7,6},{8,9},{9,8},{10,11... | collective-permute-start | bytes 884744 | tf_op jit(solution)/shard_map/ppermute | solution.py:33
  37.2 5.5 %collective-permute-start.11 = (bf16[1,128,768]{2,1,0:T(8,128)(2,1)S(1)}, bf16[1,128,768]{2,1,0:T(8,128)(2,1)S(1)}, u32[]{:S(2)}, u32[]{:S(2)}) collective-permute-start(bf16[1,128,768]{2,1,0:T(8,128)(2,1)S(1)} %get-tuple-element.16), channel_id=1, source_target_pairs={{0,6},{1,7},{2,0},{3,1},{4,2},{5,3},{6,4},{7,5},{8,14},{9,15},{10,... | collective-permute-start | bytes 589832 | tf_op jit(solution)/shard_map/ppermute | solution.py:33
  37.6 26.6 %collective-permute-start.16 = (bf16[4,128,768]{2,1,0:T(8,128)(2,1)S(1)}, bf16[4,128,768]{2,1,0:T(8,128)(2,1)S(1)}, u32[]{:S(2)}, u32[]{:S(2)}) collective-permute-start(bf16[4,128,768]{2,1,0:T(8,128)(2,1)S(1)} %get-tuple-element.20.refs_2_.refs_0_), channel_id=1, source_target_pairs={{0,8},{1,9},{2,10},{3,11},{4,12},{5,13},{6,14},{7,15},{8,0},{9,1},... | collective-permute-start | bytes 2359304 | tf_op jit(solution)/shard_map/ppermute | solution.py:33
  37.6 8.1 %collective-permute-start.12 = (bf16[1,128,768]{2,1,0:T(8,128)(2,1)S(1)}, bf16[1,128,768]{2,1,0:T(8,128)(2,1)S(1)}, u32[]{:S(2)}, u32[]{:S(2)}) collective-permute-start(bf16[1,128,768]{2,1,0:T(8,128)(2,1)S(1)} %get-tuple-element.17), channel_id=1, source_target_pairs={{0,14},{1,15},{2,8},{3,9},{4,10},{5,11},{6,12},{7,13},{8,6},{9,7},... | collective-permute-start | bytes 589832 | tf_op jit(solution)/shard_map/ppermute | solution.py:33
  38.9 28.8 %collective-permute-start.17 = (bf16[4,128,768]{2,1,0:T(8,128)(2,1)S(1)}, bf16[4,128,768]{2,1,0:T(8,128)(2,1)S(1)}, u32[]{:S(2)}, u32[]{:S(2)}) collective-permute-start(bf16[4,128,768]{2,1,0:T(8,128)(2,1)S(1)} %get-tuple-element.20.refs_2_.refs_0_), channel_id=1, source_target_pairs={{0,16},{1,17},{2,18},{3,19},{4,20},{5,21},{6,22},{7,23},{8,24},{9,... | collective-permute-start | bytes 2359304 | tf_op jit(solution)/shard_map/ppermute | solution.py:33
  41.1 10.4 %collective-permute-start.13 = (bf16[1,128,768]{2,1,0:T(8,128)(2,1)S(1)}, bf16[1,128,768]{2,1,0:T(8,128)(2,1)S(1)}, u32[]{:S(2)}, u32[]{:S(2)}) collective-permute-start(bf16[1,128,768]{2,1,0:T(8,128)(2,1)S(1)} %get-tuple-element.18), channel_id=1, source_target_pairs={{0,22},{1,23},{2,16},{3,17},{4,18},{5,19},{6,20},{7,21},{8,30},{9,... | collective-permute-start | bytes 589832 | tf_op jit(solution)/shard_map/ppermute | solution.py:33
  42.7 14.9 %collective-permute-start.14 = (bf16[1,128,768]{2,1,0:T(8,128)(2,1)S(1)}, bf16[1,128,768]{2,1,0:T(8,128)(2,1)S(1)}, u32[]{:S(2)}, u32[]{:S(2)}) collective-permute-start(bf16[1,128,768]{2,1,0:T(8,128)(2,1)S(1)} %get-tuple-element.19), channel_id=1, source_target_pairs={{0,30},{1,31},{2,24},{3,25},{4,26},{5,27},{6,28},{7,29},{8,22},{9,... | collective-permute-start | bytes 589832 | tf_op jit(solution)/shard_map/ppermute | solution.py:33
  57.6 20.2 %collective-permute-start.15 = (bf16[4,128,768]{2,1,0:T(8,128)(2,1)S(1)}, bf16[4,128,768]{2,1,0:T(8,128)(2,1)S(1)}, u32[]{:S(2)}, u32[]{:S(2)}) collective-permute-start(bf16[4,128,768]{2,1,0:T(8,128)(2,1)S(1)} %constant_dynamic-update-slice_fusion.refs_0_), channel_id=1, source_target_pairs={{0,6},{1,7},{2,0},{3,1},{4,2},{5,3},{6,4},{7,5},{8,14},{9,15},{10,... | collective-permute-start | bytes 2359304 | tf_op jit(solution)/shard_map/ppermute | solution.py:33
  64.3 12.2 %collective-permute-start.18 = (bf16[2,128,768]{2,1,0:T(8,128)(2,1)S(1)}, bf16[2,128,768]{2,1,0:T(8,128)(2,1)S(1)}, u32[]{:S(2)}, u32[]{:S(2)}) collective-permute-start(bf16[2,128,768]{2,1,0:T(8,128)(2,1)S(1)} %slice.24), channel_id=1, source_target_pairs={{0,16},{1,17},{2,18},{3,19},{4,20},{5,21},{6,22},{7,23},{8,24},{9,... | collective-permute-start | bytes 1179656 | tf_op jit(solution)/shard_map/ppermute | solution.py:33
  67.7 10.1 %collective-permute-start.19 = (bf16[2,128,768]{2,1,0:T(8,128)(2,1)S(1)}, bf16[2,128,768]{2,1,0:T(8,128)(2,1)S(1)}, u32[]{:S(2)}, u32[]{:S(2)}) collective-permute-start(bf16[2,128,768]{2,1,0:T(8,128)(2,1)S(1)} %slice.25), channel_id=1, source_target_pairs={{0,8},{1,9},{2,10},{3,11},{4,12},{5,13},{6,14},{7,15},{8,0},{9,1},... | collective-permute-start | bytes 1179656 | tf_op jit(solution)/shard_map/ppermute | solution.py:33
  67.8 11.6 %collective-permute-start.20 = (bf16[4,128,768]{2,1,0:T(8,128)(2,1)S(1)}, bf16[4,128,768]{2,1,0:T(8,128)(2,1)S(1)}, u32[]{:S(2)}, u32[]{:S(2)}) collective-permute-start(bf16[4,128,768]{2,1,0:T(8,128)(2,1)S(1)} %get-tuple-element.20.refs_2_.refs_0_), channel_id=1, source_target_pairs={{0,1},{1,0},{2,3},{3,2},{4,5},{5,4},{6,7},{7,6},{8,9},{9,8},{10,11... | collective-permute-start | bytes 2359304 | tf_op jit(solution)/shard_map/ppermute | solution.py:33
  69.0 10.4 %collective-permute-start.22 = (bf16[4,128,768]{2,1,0:T(8,128)(2,1)S(1)}, bf16[4,128,768]{2,1,0:T(8,128)(2,1)S(1)}, u32[]{:S(2)}, u32[]{:S(2)}) collective-permute-start(bf16[4,128,768]{2,1,0:T(8,128)(2,1)S(1)} %collective-permute-done.17.refs_4_.refs_2_), channel_id=1, source_target_pairs={{0,1},{1,0},{2,3},{3,2},{4,5},{5,4},{6,7},{7,6},{8,9},{9,8},{10,11... | collective-permute-start | bytes 2359304 | tf_op jit(solution)/shard_map/ppermute | solution.py:33
  83.7 9.6 %collective-permute-start.24 = (bf16[1024,128]{1,0:T(8,128)(2,1)S(1)}, bf16[1024,128]{1,0:T(8,128)(2,1)S(1)}, u32[]{:S(2)}, u32[]{:S(2)}) collective-permute-start(bf16[1024,128]{1,0:T(8,128)(2,1)S(1)} %get-tuple-element.22), channel_id=1, source_target_pairs={{0,2},{1,3},{2,4},{3,5},{4,6},{5,7},{6,0},{7,1},{8,10},{9,11},{10,... | collective-permute-start | bytes 786440 | tf_op jit(solution)/shard_map/ppermute | solution.py:33
  93.5 9.7 %collective-permute-start.29 = (bf16[1024,128]{1,0:T(8,128)(2,1)S(1)}, bf16[1024,128]{1,0:T(8,128)(2,1)S(1)}, u32[]{:S(2)}, u32[]{:S(2)}) collective-permute-start(bf16[1024,128]{1,0:T(8,128)(2,1)S(1)} %get-tuple-element.25), channel_id=1, source_target_pairs={{0,24},{1,25},{2,26},{3,27},{4,28},{5,29},{8,16},{9,17},{10,18},{1... | collective-permute-start | bytes 786440 | tf_op jit(solution)/shard_map/ppermute | solution.py:33
  95.5 14.6 %collective-permute-start.28 = (bf16[1024,128]{1,0:T(8,128)(2,1)S(1)}, bf16[1024,128]{1,0:T(8,128)(2,1)S(1)}, u32[]{:S(2)}, u32[]{:S(2)}) collective-permute-start(bf16[1024,128]{1,0:T(8,128)(2,1)S(1)} %get-tuple-element.26), channel_id=1, source_target_pairs={{0,16},{1,17},{2,18},{3,19},{6,22},{7,23},{8,24},{9,25},{10,26},{1... | collective-permute-start | bytes 786440 | tf_op jit(solution)/shard_map/ppermute | solution.py:33
  96.8 13.3 %collective-permute-start.27 = (bf16[1024,128]{1,0:T(8,128)(2,1)S(1)}, bf16[1024,128]{1,0:T(8,128)(2,1)S(1)}, u32[]{:S(2)}, u32[]{:S(2)}) collective-permute-start(bf16[1024,128]{1,0:T(8,128)(2,1)S(1)} %get-tuple-element.27), channel_id=1, source_target_pairs={{0,8},{1,9},{4,12},{5,13},{6,14},{7,15},{10,2},{11,3},{12,4},{13,5... | collective-permute-start | bytes 786440 | tf_op jit(solution)/shard_map/ppermute | solution.py:33
  (17 other events, 138.2 us)

commit v6 on v5

--- a/solution.py
+++ b/solution.py
@@ -10,6 +10,7 @@
 
 AXES = ("aux", "occ")
 CORES = 2
+TOGETHER = 4
 VMEM_LIMIT = 12 * 1024 * 1024
 VMEM_MOST = 60 * 1024 * 1024
 ANY = pl.BlockSpec(memory_space=pl.ANY)
@@ -84,22 +85,25 @@
         number = found[row]
         place = row ^ a if mirrored else row
 
-        def add_two(step, carry, row=row, number=number, place=place):
-            one = listed[row, 2 * step]
-            paired = 2 * step + 1 < number
-            two = jnp.where(paired, listed[row, jnp.where(paired, 2 * step + 1, 2 * step)], one)
-            second = ints_block(two)
-            left = jnp.concatenate([ints_block(one), jnp.where(paired, second, jnp.zeros_like(second))], axis=1)
-            right = jnp.concatenate([coeff_block(one), coeff_block(two)], axis=0)
+        def add_some(step, carry, row=row, number=number, place=place):
+            lefts, rights = [], []
+            for i in range(TOGETHER):
+                at = TOGETHER * step + i
+                there = at < number
+                slot = listed[row, jnp.where(there, at, 0)]
+                left = ints_block(slot)
+                lefts.append(left if i == 0 else jnp.where(there, left, jnp.zeros_like(left)))
+                rights.append(coeff_block(slot))
+            left, right = jnp.concatenate(lefts, axis=1), jnp.concatenate(rights, axis=0)
             total[place] += jnp.dot(left, right, preferred_element_type=jnp.float32)
             return carry
 
-        lax.fori_loop(0, (number + 1) // 2, add_two, 0)
+        lax.fori_loop(0, (number + TOGETHER - 1) // TOGETHER, add_some, 0)
     for row in range(own_blocks):
         for p in range(aux_count):
             value = total[row, pl.ds(p * block, block), :].astype(jnp.bfloat16)
             columns = pl.ds(p * orbitals, orbitals)
-            outs[0][row, :, columns] = value
+            outs[0][row ^ a if mirrored else row, :, columns] = value
             if mirrored:
                 outs[1 + row][0, :, columns] = value
 
@@ -138,22 +142,24 @@
     return lax.dot_general(first, second, ROWS, preferred_element_type=jnp.float32)
 
 
+def places_held(core, s):
+    beside = 1 + (core ^ s)
+    return [0, beside, 3 - beside, 3]
+
+
 def pair_kernel(*refs):
-    *ins, near_ref, far_ref = refs
-    rows, held = ins[:2], ins[2:]
-    count, n, depth = held[0].shape
+    one_ref, two_ref, *held, near_ref, far_ref = refs
+    count, n, depth = one_ref.shape
+    core = lax.axis_index("occ") % CORES
     for s in range(CORES):
-        totals = [None] * count
-        for k in range(count):
-            quarter = jnp.concatenate([part[k] for part in rows], axis=0)
-            value = dot_rows(held[s * count + k][...].reshape(count * n, depth), quarter)
-            for m in range(count):
-                part = value[(m ^ k) * n : ((m ^ k) + 1) * n]
-                totals[m] = part if totals[m] is None else totals[m] + part
-        for m in range(count):
-            at = pl.ds((s * count + m) * n, n)
-            near_ref[at, :] = totals[m][:, :n].astype(jnp.bfloat16)
-            far_ref[at, :] = totals[m][:, n:].astype(jnp.bfloat16)
+        total = None
+        for j, k in enumerate(places_held(core, s)):
+            quarter = jnp.concatenate([one_ref[k], two_ref[k]], axis=0)
+            value = dot_rows(held[s * count + j][...].reshape(count * n, depth), quarter)
+            total = value if total is None else total + value
+        rows = pl.ds(s * count * n, count * n)
+        near_ref[rows, :] = total[:, :n].astype(jnp.bfloat16)
+        far_ref[rows, :] = total[:, n:].astype(jnp.bfloat16)
 
 
 def pair_blocks(rows, held):
@@ -171,36 +177,28 @@
 
 def own_kernel(*refs):
     *held, out_ref, plane, sems = refs
-    _, count, rows, depth = plane.shape
-    n = rows // count
-    a = lax.axis_index("aux")
+    _, count, _, n, depth = plane.shape
     occ_index = lax.axis_index("occ")
     z, c = occ_index // CORES, occ_index % CORES
 
-    def moves(s, k):
-        parts = [(held[s * count + k].at[m ^ k], plane.at[s, k, pl.ds(m * n, n)]) for m in range(count)]
-        return [pltpu.make_async_copy(x, y, sems.at[s, k, m]) for m, (x, y) in enumerate(parts)]
-
-    @pl.when(a == z)
+    @pl.when(lax.axis_index("aux") == z)
     def _():
-        copies = {(s, k): moves(s, k) for s in range(CORES) for k in range(count)}
-        for parts in copies.values():
-            for copy in parts:
-                copy.start()
+        copies = [
+            pltpu.make_async_copy(held[s * count + j], plane.at[s, j], sems.at[s, j])
+            for s in range(CORES)
+            for j in range(count)
+        ]
+        for copy in copies:
+            copy.start()
         for s in range(CORES):
+            total = None
+            for j in range(count):
+                copies[s * count + j].wait()
+                own = plane[0, j if s == 0 else (0, 2, 1, 3)[j]].reshape(count * n, depth)
+                value = dot_rows(plane[s, j].reshape(count * n, depth), own)
+                total = value if total is None else total + value
             core = c if s == 0 else 1 - c
-            total = None
-            for k in range(count):
-                for copy in copies[s, k]:
-                    copy.wait()
-                value = dot_rows(plane[s, k], plane[0, k])
-                total = value if total is None else total + value
-            for m in range(count):
-                row = pl.multiple_of(core * rows + (a ^ m) * n, n)
-                for col in range(count):
-                    out_ref[pl.ds(row, n), pl.ds(pl.multiple_of((a ^ col) * n, n), n)] = total[
-                        m * n : (m + 1) * n, col * n : (col + 1) * n
-                    ]
+            out_ref[pl.ds(pl.multiple_of(core * count * n, n), count * n), :] = total
 
 
 def own_block(held):
@@ -211,8 +209,8 @@
         in_specs=[ANY] * len(held),
         out_specs=IN_VMEM,
         scratch_shapes=[
-            pltpu.VMEM((CORES, count, count * n, depth), jnp.bfloat16),
-            pltpu.SemaphoreType.DMA((CORES, count, count)),
+            pltpu.VMEM((CORES, count, count, n, depth), jnp.bfloat16),
+            pltpu.SemaphoreType.DMA((CORES, count)),
         ],
         compiler_params=pltpu.CompilerParams(vmem_limit_bytes=VMEM_MOST),
         name="own_block",
@@ -220,7 +218,7 @@
 
 
 def place_kernel(*refs):
-    *quarters, own_ref, out_ref = refs
+    *quarters, own_ref, out_ref, laid, sems = refs
     count = len(quarters)
     n = quarters[0].shape[1]
     width = count * n
@@ -228,31 +226,48 @@
     occ_index = lax.axis_index("occ")
     z, c = occ_index // CORES, occ_index % CORES
     apart = lax.rem(a - z + count, count)
+    core = lambda s: c if s == 0 else 1 - c
 
     def tile(row, col, value):
-        out_ref[pl.ds(pl.multiple_of(row, n), n), pl.ds(pl.multiple_of(col, n), n)] = value
+        laid[pl.ds(pl.multiple_of(row, n), n), pl.ds(pl.multiple_of(col, n), n)] = value
+
+    def leave(row, sem):
+        rows = pl.ds(pl.multiple_of(row, n), n)
+        copy = pltpu.make_async_copy(laid.at[rows], out_ref.at[rows], sem)
+        copy.start()
+        return copy
 
     @pl.when(apart == 0)
     def _():
-        out_ref[...] = own_ref[...]
+        copy = pltpu.make_async_copy(own_ref, out_ref, sems.at[0])
+        copy.start()
+        copy.wait()
 
     @pl.when((apart > 0) & (apart <= count // 2))
     def _():
+        copies = []
         for k, quarter in enumerate(quarters):
             for s in range(CORES):
-                row = (c if s == 0 else 1 - c) * width + (a ^ k) * n
+                row = core(s) * width + (a ^ k) * n
                 for m in range(count):
                     value = quarter[pl.ds((s * count + m) * n, n), :].astype(jnp.float32)
-                    tile(row, (a ^ k ^ m) * n, value.T)
+                    tile(row, m * n, value.T)
+                copies.append(leave(row, sems.at[len(copies)]))
+        for copy in copies:
+            copy.wait()
 
     @pl.when(apart > count // 2)
     def _():
-        for k, quarter in enumerate(quarters):
-            for s in range(CORES):
-                core = c if s == 0 else 1 - c
-                for m in range(count):
+        copies = []
+        for s in range(CORES):
+            for m in range(count):
+                row = core(s) * width + m * n
+                for k, quarter in enumerate(quarters):
                     value = quarter[pl.ds((s * count + m) * n, n), :].astype(jnp.float32)
-                    tile(core * width + (a ^ k ^ m) * n, (a ^ k) * n, value)
+                    tile(row, (a ^ k) * n, value)
+                copies.append(leave(row, sems.at[len(copies)]))
+        for copy in copies:
+            copy.wait()
 
 
 def place_blocks(quarters, out):
@@ -260,7 +275,8 @@
         place_kernel,
         out_shape=jax.ShapeDtypeStruct(out.shape, out.dtype),
         in_specs=[IN_VMEM] * (len(quarters) + 1),
-        out_specs=IN_VMEM,
+        out_specs=ANY,
+        scratch_shapes=[pltpu.VMEM(out.shape, out.dtype), pltpu.SemaphoreType.DMA((CORES * len(quarters),))],
         compiler_params=pltpu.CompilerParams(vmem_limit_bytes=VMEM_LIMIT),
         name="place_blocks",
     )(*quarters, out)
@@ -281,10 +297,11 @@
     ahead = [below(sent[k], k) for k in range(count)]
     rows = [jnp.concatenate(ahead)]
     rows.append(below(rows[0]))
-    first, second = (toward(half, k) for k in (1, 2))
-    passed = jnp.concatenate([toward(first[: count // 2], 2), toward(second[count // 2 :], 1)])
-    held = [half, first, second, passed]
-    held += [other(v) for v in held[:-1]] + [other(after(passed, rows[1]))]
+    one_way = lambda v: lay.send(v, lambda a_, z_, c_: (a_ ^ (1 + c_), z_, c_))
+    other_way = lambda v: lay.send(v, lambda a_, z_, c_: (a_ ^ (2 - c_), z_, c_))
+    beside = one_way(half)
+    held = [half, beside, other_way(half), other_way(beside)]
+    held += [other(v) for v in held[:-1]] + [other(after(held[-1], rows[1]))]
 
     blocks = pair_blocks(rows, held)
     mirror = lay.send(blocks[0], lambda a_, z_, c_: (a_, (z_ + 1) % count, c_))
@@ -342,7 +359,8 @@
     blocks = coefficients.reshape(own_blocks, block, orbitals)
     mine = lax.dynamic_slice_in_dim(blocks, (a % share) * part, part, 0)
     other = lambda v: lay.send(v, lambda a_, z_, c_: (a_, z_, 1 - c_))
-    pieces = [blocks, other(blocks)]
+    traded = other(blocks)
+    pieces = [other(traded), traded]
     meta = jnp.concatenate([v.reshape(1, -1) for v in (pair_count, pair_cols, pair_rows, row_blocks)], axis=1)
     for group in plane_groups(planes):
         far = [lay.send(mine, lambda a_, z_, c_, d=d: (a_, z_ ^ d, c_)) for d in group]

time: 112 us -> 112 us (level); the launches traced: 112 us -> 110 us
  starting transfers between devices: 37.8 us -> 43 us
  Pallas kernels: 9.4 us -> 6.14 us
  waiting for transfers between devices: 59.1 us -> 56.4 us
    ppermute x30, starting transfers between devices: 37.8 us -> 43 us  [send(): return lax.ppermute(value, AXES, pairs)]
    pallas_call x1, Pallas kernels: 4.23 us -> 1.46 us  [half_transform(): pl.pallas_call(functools.partial(half_kernel, lay, share, len(pieces), mi...]
    ppermute x30, waiting for transfers between devices: 59.1 us -> 56.4 us  [send(): return lax.ppermute(value, AXES, pairs)]
    unnamed x26 -> x23, local copies, waits for them, and re-layouts: 2.51 us -> 1.49 us
  transfers between devices with their start and end apart: 30 -> 30, of which waited for: 16 -> 15; matrix products, arithmetic and copies ran while one was open for 1% -> 1% of each run, Pallas kernels for 1% -> 1%
where the time goes in v6:
time: 112 us; the launch traced here: 110 us
  waiting for transfers between devices  56.4 us (50%)
  starting transfers between devices  43 us (38%)
  Pallas kernels  6.14 us (5%)
  local copies, waits for them, and re-layouts  2.44 us (2%)
    ppermute x30, waiting for transfers between devices, send(): return lax.ppermute(value, AXES, pairs)  56.4 us
    ppermute x30, starting transfers between devices, send(): return lax.ppermute(value, AXES, pairs)  43 us
  transfers between devices with their start and end apart: 30, of which 15 were waited for; matrix products, arithmetic and copies ran while one was open for 1% of the time, Pallas kernels for 1%

profile of v6, /device:TPU:5, one launch (start us, length us, event | category | flops | bytes accessed | tf_op | source)
XLA Modules:
  0.0 109.9 jit_solution(9837753912630112721)
XLA Ops:
  0.9 3.4 %collective-permute-start.4 = (bf16[1,128,384]{2,1,0:T(8,128)(2,1)S(1)}, bf16[1,128,384]{2,1,0:T(8,128)(2,1)S(1)}, u32[]{:S(2)}, u32[]{:S(2)}) collective-permute-start(bf16[1,128,384]{2,1,0:T(8,128)(2,1)S(1)} %constant_dynamic-slice_fusion), channel_id=1, source_target_pairs={{0,6},{1,7},{2,4},{3,5},{4,2},{5,3},{6,0},{7,1},{8,14},{9,15},{10,... | collective-permute-start | bytes 294920 | tf_op jit(solution)/shard_map/ppermute | solution.py:34
  7.5 4.7 %collective-permute-done.3 = bf16[1,128,384]{2,1,0:T(8,128)(2,1)S(1)} collective-permute-done((bf16[1,128,384]{2,1,0:T(8,128)(2,1)S(1)}, bf16[1,128,384]{2,1,0:T(8,128)(2,1)S(1)}, u32[]{:S(2)}, u32[]{:S(2)}) %collective-permute-start.3) | collective-permute-done | bytes 98336 | tf_op jit(solution)/shard_map/ppermute | solution.py:34
  14.9 2.2 %collective-permute-start.1 = (bf16[4,128,384]{2,1,0:T(8,128)(2,1)S(1)}, bf16[4,128,384]{2,1,0:T(8,128)(2,1)S(1)}, u32[]{:S(2)}, u32[]{:S(2)}) collective-permute-start(bf16[4,128,384]{2,1,0:T(8,128)(2,1)S(1)} %collective-permute-done.refs_1_), channel_id=1, source_target_pairs={{0,1},{1,0},{2,3},{3,2},{4,5},{5,4},{6,7},{7,6},{8,9},{9,8},{10,11... | collective-permute-start | bytes 1179656 | tf_op jit(solution)/shard_map/ppermute | solution.py:34
  17.1 3.2 %collective-permute-done.10.refs_8_ = bf16[3,128,384]{2,1,0:T(8,128)(2,1)S(1)} collective-permute-done((bf16[3,128,384]{2,1,0:T(8,128)(2,1)S(1)}, bf16[3,128,384]{2,1,0:T(8,128)(2,1)S(1)}, u32[]{:S(2)}, u32[]{:S(2)}) %collective-permute-start.10) | collective-permute-done | bytes 294944 | tf_op jit(solution)/shard_map/ppermute | solution.py:34
  20.4 4.1 %collective-permute-start.11 = (bf16[3,128,384]{2,1,0:T(8,128)(2,1)S(1)}, bf16[3,128,384]{2,1,0:T(8,128)(2,1)S(1)}, u32[]{:S(2)}, u32[]{:S(2)}) collective-permute-start(bf16[3,128,384]{2,1,0:T(8,128)(2,1)S(1)} %collective-permute-done.10.refs_8_), channel_id=1, source_target_pairs={{0,1},{1,0},{2,3},{3,2},{4,5},{5,4},{6,7},{7,6},{8,9},{9,8},{10,11... | collective-permute-start | bytes 884744 | tf_op jit(solution)/shard_map/ppermute | solution.py:34
  24.5 3.9 %collective-permute-done.8.refs_6_ = bf16[3,128,384]{2,1,0:T(8,128)(2,1)S(1)} collective-permute-done((bf16[3,128,384]{2,1,0:T(8,128)(2,1)S(1)}, bf16[3,128,384]{2,1,0:T(8,128)(2,1)S(1)}, u32[]{:S(2)}, u32[]{:S(2)}) %collective-permute-start.8) | collective-permute-done | bytes 294944 | tf_op jit(solution)/shard_map/ppermute | solution.py:34
  32.0 1.5 %half_transform.1 = (bf16[4,128,768]{2,1,0:T(8,128)(2,1)S(1)}, bf16[1,128,768]{2,1,0:T(8,128)(2,1)S(1)}, bf16[1,128,768]{2,1,0:T(8,128)(2,1)S(1)}, bf16[1,128,76...) custom-call(s32[1,81]{1,0:T(1,128)S(1)} %pad_add_fusion.meta, bf16[2,24,128,128]{3,2,1,0:T(8,128)(2,1)S(1)} %copy-done.9, ...), custom_call_target="tpu_custom_call" | custom-call | tf_op jit(solution)/shard_map/half_transform/pallas_call | solution.py:122
  34.8 2.9 %collective-permute-start.12 = (bf16[1,128,768]{2,1,0:T(8,128)(2,1)S(1)}, bf16[1,128,768]{2,1,0:T(8,128)(2,1)S(1)}, u32[]{:S(2)}, u32[]{:S(2)}) collective-permute-start(bf16[1,128,768]{2,1,0:T(8,128)(2,1)S(1)} %get-tuple-element.16), channel_id=1, source_target_pairs={{0,6},{1,7},{2,0},{3,1},{4,2},{5,3},{6,4},{7,5},{8,14},{9,15},{10,... | collective-permute-start | bytes 589832 | tf_op jit(solution)/shard_map/ppermute | solution.py:34
  38.9 3.2 %collective-permute-done.12 = bf16[1,128,768]{2,1,0:T(8,128)(2,1)S(1)} collective-permute-done((bf16[1,128,768]{2,1,0:T(8,128)(2,1)S(1)}, bf16[1,128,768]{2,1,0:T(8,128)(2,1)S(1)}, u32[]{:S(2)}, u32[]{:S(2)}) %collective-permute-start.12) | collective-permute-done | bytes 196640 | tf_op jit(solution)/shard_map/ppermute | solution.py:34
  42.1 3.5 %collective-permute-start.15 = (bf16[1,128,768]{2,1,0:T(8,128)(2,1)S(1)}, bf16[1,128,768]{2,1,0:T(8,128)(2,1)S(1)}, u32[]{:S(2)}, u32[]{:S(2)}) collective-permute-start(bf16[1,128,768]{2,1,0:T(8,128)(2,1)S(1)} %get-tuple-element.19), channel_id=1, source_target_pairs={{0,30},{1,31},{2,24},{3,25},{4,26},{5,27},{6,28},{7,29},{8,22},{9,... | collective-permute-start | bytes 589832 | tf_op jit(solution)/shard_map/ppermute | solution.py:34
  46.4 4.1 %collective-permute-done.14 = bf16[1,128,768]{2,1,0:T(8,128)(2,1)S(1)} collective-permute-done((bf16[1,128,768]{2,1,0:T(8,128)(2,1)S(1)}, bf16[1,128,768]{2,1,0:T(8,128)(2,1)S(1)}, u32[]{:S(2)}, u32[]{:S(2)}) %collective-permute-start.14) | collective-permute-done | bytes 196640 | tf_op jit(solution)/shard_map/ppermute | solution.py:34
  50.6 5.1 %collective-permute-done.15 = bf16[1,128,768]{2,1,0:T(8,128)(2,1)S(1)} collective-permute-done((bf16[1,128,768]{2,1,0:T(8,128)(2,1)S(1)}, bf16[1,128,768]{2,1,0:T(8,128)(2,1)S(1)}, u32[]{:S(2)}, u32[]{:S(2)}) %collective-permute-start.15) | collective-permute-done | bytes 196640 | tf_op jit(solution)/shard_map/ppermute | solution.py:34
  55.7 2.7 %collective-permute-start.16 = (bf16[4,128,768]{2,1,0:T(8,128)(2,1)S(1)}, bf16[4,128,768]{2,1,0:T(8,128)(2,1)S(1)}, u32[]{:S(2)}, u32[]{:S(2)}) collective-permute-start(bf16[4,128,768]{2,1,0:T(8,128)(2,1)S(1)} %constant_dynamic-update-slice_fusion.refs_0_), channel_id=1, source_target_pairs={{0,6},{1,7},{2,0},{3,1},{4,2},{5,3},{6,4},{7,5},{8,14},{9,15},{10,... | collective-permute-start | bytes 2359304 | tf_op jit(solution)/shard_map/ppermute | solution.py:34
  58.4 3.4 %collective-permute-start.19 = (bf16[4,128,768]{2,1,0:T(8,128)(2,1)S(1)}, bf16[4,128,768]{2,1,0:T(8,128)(2,1)S(1)}, u32[]{:S(2)}, u32[]{:S(2)}) collective-permute-start(bf16[4,128,768]{2,1,0:T(8,128)(2,1)S(1)} %collective-permute-done.17.refs_3_.refs_1_), channel_id=1, source_target_pairs={{0,16},{1,9},{2,18},{3,11},{4,20},{5,13},{6,22},{7,15},{8,24},{9,1... | collective-permute-start | bytes 2359304 | tf_op jit(solution)/shard_map/ppermute | solution.py:34
  63.0 10.5 %collective-permute-done.16.refs_1_ = bf16[4,128,768]{2,1,0:T(8,128)(2,1)S(1)} collective-permute-done((bf16[4,128,768]{2,1,0:T(8,128)(2,1)S(1)}, bf16[4,128,768]{2,1,0:T(8,128)(2,1)S(1)}, u32[]{:S(2)}, u32[]{:S(2)}) %collective-permute-start.16) | collective-permute-done | bytes 786464 | tf_op jit(solution)/shard_map/ppermute | solution.py:34
  73.5 2.6 %collective-permute-start.23 = (bf16[4,128,768]{2,1,0:T(8,128)(2,1)S(1)}, bf16[4,128,768]{2,1,0:T(8,128)(2,1)S(1)}, u32[]{:S(2)}, u32[]{:S(2)}) collective-permute-start(bf16[4,128,768]{2,1,0:T(8,128)(2,1)S(1)} %collective-permute-done.19.refs_5_.refs_3_), channel_id=1, source_target_pairs={{0,1},{1,0},{2,3},{3,2},{4,5},{5,4},{6,7},{7,6},{8,9},{9,8},{10,11... | collective-permute-start | bytes 2359304 | tf_op jit(solution)/shard_map/ppermute | solution.py:34
  76.2 1.9 %collective-permute-done.23.refs_9_.refs_7_ = bf16[4,128,768]{2,1,0:T(8,128)(2,1)S(1)} collective-permute-done((bf16[4,128,768]{2,1,0:T(8,128)(2,1)S(1)}, bf16[4,128,768]{2,1,0:T(8,128)(2,1)S(1)}, u32[]{:S(2)}, u32[]{:S(2)}) %collective-permute-start.23) | collective-permute-done | bytes 786464 | tf_op jit(solution)/shard_map/ppermute | solution.py:34
  78.0 1.8 %pair_blocks.1 = (bf16[1024,128]{1,0:T(8,128)(2,1)S(1)}, bf16[1024,128]{1,0:T(8,128)(2,1)S(1)}) custom-call(bf16[4,128,768]{2,1,0:T(8,128)(2,1)S(1)} %constant_dynamic-update-slice_fusion.refs_0_, bf16[4,128,768]{2,1,0:T(8,128)(2,1)S(1)} %collective-permute-done.16.refs_1_, bf16[4,128,768]{2,1,0:T(8,128)(2,1)S(1)} %get-tuple-element.20.refs_2_.refs_0_, ...), custom_call_target="tpu_custom_call" | custom-call | tf_op jit(solution)/shard_map/pair_blocks/pallas_call | solution.py:168
  82.1 8.9 %collective-permute-done.24 = bf16[1024,128]{1,0:T(8,128)(2,1)S(1)} collective-permute-done((bf16[1024,128]{1,0:T(8,128)(2,1)S(1)}, bf16[1024,128]{1,0:T(8,128)(2,1)S(1)}, u32[]{:S(2)}, u32[]{:S(2)}) %collective-permute-start.24) | collective-permute-done | bytes 262176 | tf_op jit(solution)/shard_map/ppermute | solution.py:34
  91.2 4.8 %collective-permute-start.29 = (bf16[1024,128]{1,0:T(8,128)(2,1)S(1)}, bf16[1024,128]{1,0:T(8,128)(2,1)S(1)}, u32[]{:S(2)}, u32[]{:S(2)}) collective-permute-start(bf16[1024,128]{1,0:T(8,128)(2,1)S(1)} %get-tuple-element.25), channel_id=1, source_target_pairs={{0,24},{1,25},{2,26},{3,27},{4,28},{5,29},{8,16},{9,17},{10,18},{1... | collective-permute-start | bytes 786440 | tf_op jit(solution)/shard_map/ppermute | solution.py:34
  97.4 2.8 %collective-permute-start.27 = (bf16[1024,128]{1,0:T(8,128)(2,1)S(1)}, bf16[1024,128]{1,0:T(8,128)(2,1)S(1)}, u32[]{:S(2)}, u32[]{:S(2)}) collective-permute-start(bf16[1024,128]{1,0:T(8,128)(2,1)S(1)} %get-tuple-element.27), channel_id=1, source_target_pairs={{0,8},{1,9},{4,12},{5,13},{6,14},{7,15},{10,2},{11,3},{12,4},{13,5... | collective-permute-start | bytes 786440 | tf_op jit(solution)/shard_map/ppermute | solution.py:34
  100.2 1.8 %collective-permute-done.29.refs_3_ = bf16[1024,128]{1,0:T(8,128)(2,1)S(1)} collective-permute-done((bf16[1024,128]{1,0:T(8,128)(2,1)S(1)}, bf16[1024,128]{1,0:T(8,128)(2,1)S(1)}, u32[]{:S(2)}, u32[]{:S(2)}) %collective-permute-start.29) | collective-permute-done | bytes 262176 | tf_op jit(solution)/shard_map/ppermute | solution.py:34
  102.0 6.4 %collective-permute-done.28.refs_2_ = bf16[1024,128]{1,0:T(8,128)(2,1)S(1)} collective-permute-done((bf16[1024,128]{1,0:T(8,128)(2,1)S(1)}, bf16[1024,128]{1,0:T(8,128)(2,1)S(1)}, u32[]{:S(2)}, u32[]{:S(2)}) %collective-permute-start.28) | collective-permute-done | bytes 262176 | tf_op jit(solution)/shard_map/ppermute | solution.py:34
  108.4 1.5 %place_blocks.1 = f32[1024,512]{1,0:T(8,128)} custom-call(bf16[1024,128]{1,0:T(8,128)(2,1)S(1)} %get-tuple-element.28.refs_0_, bf16[1024,128]{1,0:T(8,128)(2,1)S(1)} %collective-permute-done.27.refs_1_, bf16[1024,128]{1,0:T(8,128)(2,1)S(1)} %collective-permute-done.28.refs_2_, bf16[1024,128]{1,0:T(8,128)(2,1)S(1)} %collective-permute-done.29.refs_3_, ...), custom_call_target="tpu_custom_call" | custom-call | tf_op jit(solution)/shard_map/place_blocks/pallas_call | solution.py:274
  (71 shorter events, 18.0 us)
Async XLA Ops:
  4.3 7.9 %collective-permute-start.3 = (bf16[1,128,384]{2,1,0:T(8,128)(2,1)S(1)}, bf16[1,128,384]{2,1,0:T(8,128)(2,1)S(1)}, u32[]{:S(2)}, u32[]{:S(2)}) collective-permute-start(bf16[1,128,384]{2,1,0:T(8,128)(2,1)S(1)} %constant_dynamic-slice_fusion), channel_id=1, source_target_pairs={{0,4},{1,5},{2,6},{3,7},{4,0},{5,1},{6,2},{7,3},{8,12},{9,13},{10,... | collective-permute-start | bytes 294920 | tf_op jit(solution)/shard_map/ppermute | solution.py:34
  4.3 7.9 %collective-permute-start.2 = (bf16[1,128,384]{2,1,0:T(8,128)(2,1)S(1)}, bf16[1,128,384]{2,1,0:T(8,128)(2,1)S(1)}, u32[]{:S(2)}, u32[]{:S(2)}) collective-permute-start(bf16[1,128,384]{2,1,0:T(8,128)(2,1)S(1)} %constant_dynamic-slice_fusion), channel_id=1, source_target_pairs={{0,2},{1,3},{2,0},{3,1},{4,6},{5,7},{6,4},{7,5},{8,10},{9,11},{10,... | collective-permute-start | bytes 294920 | tf_op jit(solution)/shard_map/ppermute | solution.py:34
  4.7 10.3 %collective-permute-start = (bf16[4,128,384]{2,1,0:T(8,128)(2,1)}, bf16[4,128,384]{2,1,0:T(8,128)(2,1)S(1)}, u32[]{:S(2)}, u32[]{:S(2)}) collective-permute-start(bf16[4,128,384]{2,1,0:T(8,128)(2,1)} %bitcast.3), channel_id=1, source_target_pairs={{0,1},{1,0},{2,3},{3,2},{4,5},{5,4},{6,7},{7,6},{8,9},{9,8},{10,11... | collective-permute-start | bytes 1179656 | tf_op jit(solution)/shard_map/ppermute | solution.py:34
  12.2 8.2 %collective-permute-start.10 = (bf16[3,128,384]{2,1,0:T(8,128)(2,1)S(1)}, bf16[3,128,384]{2,1,0:T(8,128)(2,1)S(1)}, u32[]{:S(2)}, u32[]{:S(2)}) collective-permute-start(bf16[3,128,384]{2,1,0:T(8,128)(2,1)S(1)} %pad_maximum_fusion.refs_2_), channel_id=1, source_target_pairs={{0,24},{1,25},{2,26},{3,27},{4,28},{5,29},{6,30},{7,31},{8,16},{9,... | collective-permute-start | bytes 884744 | tf_op jit(solution)/shard_map/ppermute | solution.py:34
  13.4 15.0 %collective-permute-start.8 = (bf16[3,128,384]{2,1,0:T(8,128)(2,1)S(1)}, bf16[3,128,384]{2,1,0:T(8,128)(2,1)S(1)}, u32[]{:S(2)}, u32[]{:S(2)}) collective-permute-start(bf16[3,128,384]{2,1,0:T(8,128)(2,1)S(1)} %pad_maximum_fusion.refs_2_), channel_id=1, source_target_pairs={{0,16},{1,17},{2,18},{3,19},{4,20},{5,21},{6,22},{7,23},{8,24},{9,... | collective-permute-start | bytes 884744 | tf_op jit(solution)/shard_map/ppermute | solution.py:34
  14.7 14.3 %collective-permute-start.6 = (bf16[3,128,384]{2,1,0:T(8,128)(2,1)S(1)}, bf16[3,128,384]{2,1,0:T(8,128)(2,1)S(1)}, u32[]{:S(2)}, u32[]{:S(2)}) collective-permute-start(bf16[3,128,384]{2,1,0:T(8,128)(2,1)S(1)} %pad_maximum_fusion.refs_2_), channel_id=1, source_target_pairs={{0,8},{1,9},{2,10},{3,11},{4,12},{5,13},{6,14},{7,15},{8,0},{9,1},... | collective-permute-start | bytes 884744 | tf_op jit(solution)/shard_map/ppermute | solution.py:34
  14.9 15.6 %collective-permute-start.1 = (bf16[4,128,384]{2,1,0:T(8,128)(2,1)S(1)}, bf16[4,128,384]{2,1,0:T(8,128)(2,1)S(1)}, u32[]{:S(2)}, u32[]{:S(2)}) collective-permute-start(bf16[4,128,384]{2,1,0:T(8,128)(2,1)S(1)} %collective-permute-done.refs_1_), channel_id=1, source_target_pairs={{0,1},{1,0},{2,3},{3,2},{4,5},{5,4},{6,7},{7,6},{8,9},{9,8},{10,11... | collective-permute-start | bytes 1179656 | tf_op jit(solution)/shard_map/ppermute | solution.py:34
  17.1 11.8 %collective-permute-start.5 = (bf16[3,128,384]{2,1,0:T(8,128)(2,1)S(1)}, bf16[3,128,384]{2,1,0:T(8,128)(2,1)S(1)}, u32[]{:S(2)}, u32[]{:S(2)}) collective-permute-start(bf16[3,128,384]{2,1,0:T(8,128)(2,1)S(1)} %pad_maximum_fusion.refs_2_), channel_id=1, source_target_pairs={{0,1},{1,0},{2,3},{3,2},{4,5},{5,4},{6,7},{7,6},{8,9},{9,8},{10,11... | collective-permute-start | bytes 884744 | tf_op jit(solution)/shard_map/ppermute | solution.py:34
  20.4 8.6 %collective-permute-start.11 = (bf16[3,128,384]{2,1,0:T(8,128)(2,1)S(1)}, bf16[3,128,384]{2,1,0:T(8,128)(2,1)S(1)}, u32[]{:S(2)}, u32[]{:S(2)}) collective-permute-start(bf16[3,128,384]{2,1,0:T(8,128)(2,1)S(1)} %collective-permute-done.10.refs_8_), channel_id=1, source_target_pairs={{0,1},{1,0},{2,3},{3,2},{4,5},{5,4},{6,7},{7,6},{8,9},{9,8},{10,11... | collective-permute-start | bytes 884744 | tf_op jit(solution)/shard_map/ppermute | solution.py:34
  33.4 24.9 %collective-permute-start.17 = (bf16[4,128,768]{2,1,0:T(8,128)(2,1)S(1)}, bf16[4,128,768]{2,1,0:T(8,128)(2,1)S(1)}, u32[]{:S(2)}, u32[]{:S(2)}) collective-permute-start(bf16[4,128,768]{2,1,0:T(8,128)(2,1)S(1)} %get-tuple-element.20.refs_2_.refs_0_), channel_id=1, source_target_pairs={{0,8},{1,17},{2,10},{3,19},{4,12},{5,21},{6,14},{7,23},{8,0},{9,25... | collective-permute-start | bytes 2359304 | tf_op jit(solution)/shard_map/ppermute | solution.py:34
  34.8 7.3 %collective-permute-start.12 = (bf16[1,128,768]{2,1,0:T(8,128)(2,1)S(1)}, bf16[1,128,768]{2,1,0:T(8,128)(2,1)S(1)}, u32[]{:S(2)}, u32[]{:S(2)}) collective-permute-start(bf16[1,128,768]{2,1,0:T(8,128)(2,1)S(1)} %get-tuple-element.16), channel_id=1, source_target_pairs={{0,6},{1,7},{2,0},{3,1},{4,2},{5,3},{6,4},{7,5},{8,14},{9,15},{10,... | collective-permute-start | bytes 589832 | tf_op jit(solution)/shard_map/ppermute | solution.py:34
  37.7 8.7 %collective-permute-start.13 = (bf16[1,128,768]{2,1,0:T(8,128)(2,1)S(1)}, bf16[1,128,768]{2,1,0:T(8,128)(2,1)S(1)}, u32[]{:S(2)}, u32[]{:S(2)}) collective-permute-start(bf16[1,128,768]{2,1,0:T(8,128)(2,1)S(1)} %get-tuple-element.17), channel_id=1, source_target_pairs={{0,14},{1,15},{2,8},{3,9},{4,10},{5,11},{6,12},{7,13},{8,6},{9,7},... | collective-permute-start | bytes 589832 | tf_op jit(solution)/shard_map/ppermute | solution.py:34
  37.7 25.0 %collective-permute-start.18 = (bf16[4,128,768]{2,1,0:T(8,128)(2,1)S(1)}, bf16[4,128,768]{2,1,0:T(8,128)(2,1)S(1)}, u32[]{:S(2)}, u32[]{:S(2)}) collective-permute-start(bf16[4,128,768]{2,1,0:T(8,128)(2,1)S(1)} %get-tuple-element.20.refs_2_.refs_0_), channel_id=1, source_target_pairs={{0,16},{1,9},{2,18},{3,11},{4,20},{5,13},{6,22},{7,15},{8,24},{9,1... | collective-permute-start | bytes 2359304 | tf_op jit(solution)/shard_map/ppermute | solution.py:34
  38.9 11.6 %collective-permute-start.14 = (bf16[1,128,768]{2,1,0:T(8,128)(2,1)S(1)}, bf16[1,128,768]{2,1,0:T(8,128)(2,1)S(1)}, u32[]{:S(2)}, u32[]{:S(2)}) collective-permute-start(bf16[1,128,768]{2,1,0:T(8,128)(2,1)S(1)} %get-tuple-element.18), channel_id=1, source_target_pairs={{0,22},{1,23},{2,16},{3,17},{4,18},{5,19},{6,20},{7,21},{8,30},{9,... | collective-permute-start | bytes 589832 | tf_op jit(solution)/shard_map/ppermute | solution.py:34
  42.1 13.5 %collective-permute-start.15 = (bf16[1,128,768]{2,1,0:T(8,128)(2,1)S(1)}, bf16[1,128,768]{2,1,0:T(8,128)(2,1)S(1)}, u32[]{:S(2)}, u32[]{:S(2)}) collective-permute-start(bf16[1,128,768]{2,1,0:T(8,128)(2,1)S(1)} %get-tuple-element.19), channel_id=1, source_target_pairs={{0,30},{1,31},{2,24},{3,25},{4,26},{5,27},{6,28},{7,29},{8,22},{9,... | collective-permute-start | bytes 589832 | tf_op jit(solution)/shard_map/ppermute | solution.py:34
  55.7 17.8 %collective-permute-start.16 = (bf16[4,128,768]{2,1,0:T(8,128)(2,1)S(1)}, bf16[4,128,768]{2,1,0:T(8,128)(2,1)S(1)}, u32[]{:S(2)}, u32[]{:S(2)}) collective-permute-start(bf16[4,128,768]{2,1,0:T(8,128)(2,1)S(1)} %constant_dynamic-update-slice_fusion.refs_0_), channel_id=1, source_target_pairs={{0,6},{1,7},{2,0},{3,1},{4,2},{5,3},{6,4},{7,5},{8,14},{9,15},{10,... | collective-permute-start | bytes 2359304 | tf_op jit(solution)/shard_map/ppermute | solution.py:34
  58.4 15.1 %collective-permute-start.19 = (bf16[4,128,768]{2,1,0:T(8,128)(2,1)S(1)}, bf16[4,128,768]{2,1,0:T(8,128)(2,1)S(1)}, u32[]{:S(2)}, u32[]{:S(2)}) collective-permute-start(bf16[4,128,768]{2,1,0:T(8,128)(2,1)S(1)} %collective-permute-done.17.refs_3_.refs_1_), channel_id=1, source_target_pairs={{0,16},{1,9},{2,18},{3,11},{4,20},{5,13},{6,22},{7,15},{8,24},{9,1... | collective-permute-start | bytes 2359304 | tf_op jit(solution)/shard_map/ppermute | solution.py:34
  61.8 14.3 %collective-permute-start.20 = (bf16[4,128,768]{2,1,0:T(8,128)(2,1)S(1)}, bf16[4,128,768]{2,1,0:T(8,128)(2,1)S(1)}, u32[]{:S(2)}, u32[]{:S(2)}) collective-permute-start(bf16[4,128,768]{2,1,0:T(8,128)(2,1)S(1)} %get-tuple-element.20.refs_2_.refs_0_), channel_id=1, source_target_pairs={{0,1},{1,0},{2,3},{3,2},{4,5},{5,4},{6,7},{7,6},{8,9},{9,8},{10,11... | collective-permute-start | bytes 2359304 | tf_op jit(solution)/shard_map/ppermute | solution.py:34
  62.5 13.7 %collective-permute-start.21 = (bf16[4,128,768]{2,1,0:T(8,128)(2,1)S(1)}, bf16[4,128,768]{2,1,0:T(8,128)(2,1)S(1)}, u32[]{:S(2)}, u32[]{:S(2)}) collective-permute-start(bf16[4,128,768]{2,1,0:T(8,128)(2,1)S(1)} %collective-permute-done.17.refs_3_.refs_1_), channel_id=1, source_target_pairs={{0,1},{1,0},{2,3},{3,2},{4,5},{5,4},{6,7},{7,6},{8,9},{9,8},{10,11... | collective-permute-start | bytes 2359304 | tf_op jit(solution)/shard_map/ppermute | solution.py:34
  62.7 13.4 %collective-permute-start.22 = (bf16[4,128,768]{2,1,0:T(8,128)(2,1)S(1)}, bf16[4,128,768]{2,1,0:T(8,128)(2,1)S(1)}, u32[]{:S(2)}, u32[]{:S(2)}) collective-permute-start(bf16[4,128,768]{2,1,0:T(8,128)(2,1)S(1)} %collective-permute-done.18.refs_4_.refs_2_), channel_id=1, source_target_pairs={{0,1},{1,0},{2,3},{3,2},{4,5},{5,4},{6,7},{7,6},{8,9},{9,8},{10,11... | collective-permute-start | bytes 2359304 | tf_op jit(solution)/shard_map/ppermute | solution.py:34
  80.4 10.5 %collective-permute-start.24 = (bf16[1024,128]{1,0:T(8,128)(2,1)S(1)}, bf16[1024,128]{1,0:T(8,128)(2,1)S(1)}, u32[]{:S(2)}, u32[]{:S(2)}) collective-permute-start(bf16[1024,128]{1,0:T(8,128)(2,1)S(1)} %get-tuple-element.22), channel_id=1, source_target_pairs={{0,2},{1,3},{2,4},{3,5},{4,6},{5,7},{6,0},{7,1},{8,10},{9,11},{10,... | collective-permute-start | bytes 786440 | tf_op jit(solution)/shard_map/ppermute | solution.py:34
  91.2 10.8 %collective-permute-start.29 = (bf16[1024,128]{1,0:T(8,128)(2,1)S(1)}, bf16[1024,128]{1,0:T(8,128)(2,1)S(1)}, u32[]{:S(2)}, u32[]{:S(2)}) collective-permute-start(bf16[1024,128]{1,0:T(8,128)(2,1)S(1)} %get-tuple-element.25), channel_id=1, source_target_pairs={{0,24},{1,25},{2,26},{3,27},{4,28},{5,29},{8,16},{9,17},{10,18},{1... | collective-permute-start | bytes 786440 | tf_op jit(solution)/shard_map/ppermute | solution.py:34
  96.1 12.4 %collective-permute-start.28 = (bf16[1024,128]{1,0:T(8,128)(2,1)S(1)}, bf16[1024,128]{1,0:T(8,128)(2,1)S(1)}, u32[]{:S(2)}, u32[]{:S(2)}) collective-permute-start(bf16[1024,128]{1,0:T(8,128)(2,1)S(1)} %get-tuple-element.26), channel_id=1, source_target_pairs={{0,16},{1,17},{2,18},{3,19},{6,22},{7,23},{8,24},{9,25},{10,26},{1... | collective-permute-start | bytes 786440 | tf_op jit(solution)/shard_map/ppermute | solution.py:34
  97.4 11.1 %collective-permute-start.27 = (bf16[1024,128]{1,0:T(8,128)(2,1)S(1)}, bf16[1024,128]{1,0:T(8,128)(2,1)S(1)}, u32[]{:S(2)}, u32[]{:S(2)}) collective-permute-start(bf16[1024,128]{1,0:T(8,128)(2,1)S(1)} %get-tuple-element.27), channel_id=1, source_target_pairs={{0,8},{1,9},{4,12},{5,13},{6,14},{7,15},{10,2},{11,3},{12,4},{13,5... | collective-permute-start | bytes 786440 | tf_op jit(solution)/shard_map/ppermute | solution.py:34
  (16 other events, 150.7 us)

commit v7 on v6

--- a/solution.py
+++ b/solution.py
@@ -11,7 +11,7 @@
 AXES = ("aux", "occ")
 CORES = 2
 TOGETHER = 4
-VMEM_LIMIT = 12 * 1024 * 1024
+VMEM_LIMIT = 30 * 1024 * 1024
 VMEM_MOST = 60 * 1024 * 1024
 ANY = pl.BlockSpec(memory_space=pl.ANY)
 IN_SMEM = pl.BlockSpec(memory_space=pltpu.SMEM)
@@ -308,7 +308,7 @@
     out = own_block(held)
     width = count * n
     blocks = [jnp.concatenate([v[:width], other(v[width:])]) for v in blocks]
-    apart = {1: blocks[0], 2: after(blocks[1], out), 3: mirror}
+    apart = {1: after(blocks[0], out), 2: blocks[1], 3: mirror}
 
     quarters = []
     for k in range(count):

time: 112 us -> 111 us (level)
  waiting for transfers between devices: 56.4 us -> 53.4 us
  Pallas kernels: 6.14 us -> 8.14 us
    ppermute x30, waiting for transfers between devices: 56.4 us -> 53.4 us  [send(): return lax.ppermute(value, AXES, pairs)]
    pallas_call x1, Pallas kernels: 1.46 us -> 3.46 us  [half_transform(): pl.pallas_call(functools.partial(half_kernel, lay, share, len(pieces), mi...]
  transfers between devices with their start and end apart: 30 -> 30, of which waited for: 15 -> 14; matrix products, arithmetic and copies ran while one was open for 1% -> 1% of each run, Pallas kernels for 1% -> 1%
where the time goes in v7:
time: 111 us; the launch traced here: 110 us
  waiting for transfers between devices  53.4 us (48%)
  starting transfers between devices  43.8 us (39%)
  Pallas kernels  8.14 us (7%)
  local copies, waits for them, and re-layouts  2.44 us (2%)
    ppermute x30, waiting for transfers between devices, send(): return lax.ppermute(value, AXES, pairs)  53.4 us
    ppermute x30, starting transfers between devices, send(): return lax.ppermute(value, AXES, pairs)  43.8 us
    pallas_call x1, Pallas kernels, half_transform(): pl.pallas_call(functools.partial(half_kernel, lay, share, len(pieces), mi...  3.46 us
  transfers between devices with their start and end apart: 30, of which 14 were waited for; matrix products, arithmetic and copies ran while one was open for 1% of the time, Pallas kernels for 1%

profile of v7, /device:TPU:5, one launch (start us, length us, event | category | flops | bytes accessed | tf_op | source)
XLA Modules:
  0.0 109.8 jit_solution(4761397920541653723)
XLA Ops:
  0.9 3.4 %collective-permute-start.4 = (bf16[1,128,384]{2,1,0:T(8,128)(2,1)S(1)}, bf16[1,128,384]{2,1,0:T(8,128)(2,1)S(1)}, u32[]{:S(2)}, u32[]{:S(2)}) collective-permute-start(bf16[1,128,384]{2,1,0:T(8,128)(2,1)S(1)} %constant_dynamic-slice_fusion), channel_id=1, source_target_pairs={{0,6},{1,7},{2,4},{3,5},{4,2},{5,3},{6,0},{7,1},{8,14},{9,15},{10,... | collective-permute-start | bytes 294920 | tf_op jit(solution)/shard_map/ppermute | solution.py:34
  7.5 4.7 %collective-permute-done.3 = bf16[1,128,384]{2,1,0:T(8,128)(2,1)S(1)} collective-permute-done((bf16[1,128,384]{2,1,0:T(8,128)(2,1)S(1)}, bf16[1,128,384]{2,1,0:T(8,128)(2,1)S(1)}, u32[]{:S(2)}, u32[]{:S(2)}) %collective-permute-start.3) | collective-permute-done | bytes 98336 | tf_op jit(solution)/shard_map/ppermute | solution.py:34
  14.9 2.2 %collective-permute-start.1 = (bf16[4,128,384]{2,1,0:T(8,128)(2,1)S(1)}, bf16[4,128,384]{2,1,0:T(8,128)(2,1)S(1)}, u32[]{:S(2)}, u32[]{:S(2)}) collective-permute-start(bf16[4,128,384]{2,1,0:T(8,128)(2,1)S(1)} %collective-permute-done.refs_1_), channel_id=1, source_target_pairs={{0,1},{1,0},{2,3},{3,2},{4,5},{5,4},{6,7},{7,6},{8,9},{9,8},{10,11... | collective-permute-start | bytes 1179656 | tf_op jit(solution)/shard_map/ppermute | solution.py:34
  17.1 3.2 %collective-permute-done.10.refs_8_ = bf16[3,128,384]{2,1,0:T(8,128)(2,1)S(1)} collective-permute-done((bf16[3,128,384]{2,1,0:T(8,128)(2,1)S(1)}, bf16[3,128,384]{2,1,0:T(8,128)(2,1)S(1)}, u32[]{:S(2)}, u32[]{:S(2)}) %collective-permute-start.10) | collective-permute-done | bytes 294944 | tf_op jit(solution)/shard_map/ppermute | solution.py:34
  20.4 4.1 %collective-permute-start.11 = (bf16[3,128,384]{2,1,0:T(8,128)(2,1)S(1)}, bf16[3,128,384]{2,1,0:T(8,128)(2,1)S(1)}, u32[]{:S(2)}, u32[]{:S(2)}) collective-permute-start(bf16[3,128,384]{2,1,0:T(8,128)(2,1)S(1)} %collective-permute-done.10.refs_8_), channel_id=1, source_target_pairs={{0,1},{1,0},{2,3},{3,2},{4,5},{5,4},{6,7},{7,6},{8,9},{9,8},{10,11... | collective-permute-start | bytes 884744 | tf_op jit(solution)/shard_map/ppermute | solution.py:34
  24.5 3.9 %collective-permute-done.8.refs_6_ = bf16[3,128,384]{2,1,0:T(8,128)(2,1)S(1)} collective-permute-done((bf16[3,128,384]{2,1,0:T(8,128)(2,1)S(1)}, bf16[3,128,384]{2,1,0:T(8,128)(2,1)S(1)}, u32[]{:S(2)}, u32[]{:S(2)}) %collective-permute-start.8) | collective-permute-done | bytes 294944 | tf_op jit(solution)/shard_map/ppermute | solution.py:34
  32.0 3.5 %half_transform.1 = (bf16[4,128,768]{2,1,0:T(8,128)(2,1)S(1)}, bf16[1,128,768]{2,1,0:T(8,128)(2,1)S(1)}, bf16[1,128,768]{2,1,0:T(8,128)(2,1)S(1)}, bf16[1,128,76...) custom-call(s32[1,81]{1,0:T(1,128)S(1)} %pad_add_fusion.meta, bf16[2,24,128,128]{3,2,1,0:T(8,128)(2,1)S(1)} %copy-done.9, ...), custom_call_target="tpu_custom_call" | custom-call | tf_op jit(solution)/shard_map/half_transform/pallas_call | solution.py:122
  35.5 1.6 %collective-permute-start.12 = (bf16[1,128,768]{2,1,0:T(8,128)(2,1)S(1)}, bf16[1,128,768]{2,1,0:T(8,128)(2,1)S(1)}, u32[]{:S(2)}, u32[]{:S(2)}) collective-permute-start(bf16[1,128,768]{2,1,0:T(8,128)(2,1)S(1)} %get-tuple-element.16), channel_id=1, source_target_pairs={{0,6},{1,7},{2,0},{3,1},{4,2},{5,3},{6,4},{7,5},{8,14},{9,15},{10,... | collective-permute-start | bytes 589832 | tf_op jit(solution)/shard_map/ppermute | solution.py:34
  37.1 1.7 %collective-permute-start.13 = (bf16[1,128,768]{2,1,0:T(8,128)(2,1)S(1)}, bf16[1,128,768]{2,1,0:T(8,128)(2,1)S(1)}, u32[]{:S(2)}, u32[]{:S(2)}) collective-permute-start(bf16[1,128,768]{2,1,0:T(8,128)(2,1)S(1)} %get-tuple-element.17), channel_id=1, source_target_pairs={{0,14},{1,15},{2,8},{3,9},{4,10},{5,11},{6,12},{7,13},{8,6},{9,7},... | collective-permute-start | bytes 589832 | tf_op jit(solution)/shard_map/ppermute | solution.py:34
  39.8 1.5 %collective-permute-done.12 = bf16[1,128,768]{2,1,0:T(8,128)(2,1)S(1)} collective-permute-done((bf16[1,128,768]{2,1,0:T(8,128)(2,1)S(1)}, bf16[1,128,768]{2,1,0:T(8,128)(2,1)S(1)}, u32[]{:S(2)}, u32[]{:S(2)}) %collective-permute-start.12) | collective-permute-done | bytes 196640 | tf_op jit(solution)/shard_map/ppermute | solution.py:34
  41.3 5.1 %collective-permute-start.15 = (bf16[1,128,768]{2,1,0:T(8,128)(2,1)S(1)}, bf16[1,128,768]{2,1,0:T(8,128)(2,1)S(1)}, u32[]{:S(2)}, u32[]{:S(2)}) collective-permute-start(bf16[1,128,768]{2,1,0:T(8,128)(2,1)S(1)} %get-tuple-element.19), channel_id=1, source_target_pairs={{0,30},{1,31},{2,24},{3,25},{4,26},{5,27},{6,28},{7,29},{8,22},{9,... | collective-permute-start | bytes 589832 | tf_op jit(solution)/shard_map/ppermute | solution.py:34
  46.4 6.0 %collective-permute-done.14 = bf16[1,128,768]{2,1,0:T(8,128)(2,1)S(1)} collective-permute-done((bf16[1,128,768]{2,1,0:T(8,128)(2,1)S(1)}, bf16[1,128,768]{2,1,0:T(8,128)(2,1)S(1)}, u32[]{:S(2)}, u32[]{:S(2)}) %collective-permute-start.14) | collective-permute-done | bytes 196640 | tf_op jit(solution)/shard_map/ppermute | solution.py:34
  52.4 2.9 %collective-permute-done.15 = bf16[1,128,768]{2,1,0:T(8,128)(2,1)S(1)} collective-permute-done((bf16[1,128,768]{2,1,0:T(8,128)(2,1)S(1)}, bf16[1,128,768]{2,1,0:T(8,128)(2,1)S(1)}, u32[]{:S(2)}, u32[]{:S(2)}) %collective-permute-start.15) | collective-permute-done | bytes 196640 | tf_op jit(solution)/shard_map/ppermute | solution.py:34
  55.4 4.0 %collective-permute-start.16 = (bf16[4,128,768]{2,1,0:T(8,128)(2,1)S(1)}, bf16[4,128,768]{2,1,0:T(8,128)(2,1)S(1)}, u32[]{:S(2)}, u32[]{:S(2)}) collective-permute-start(bf16[4,128,768]{2,1,0:T(8,128)(2,1)S(1)} %constant_dynamic-update-slice_fusion.refs_0_), channel_id=1, source_target_pairs={{0,6},{1,7},{2,0},{3,1},{4,2},{5,3},{6,4},{7,5},{8,14},{9,15},{10,... | collective-permute-start | bytes 2359304 | tf_op jit(solution)/shard_map/ppermute | solution.py:34
  59.4 4.0 %collective-permute-start.20 = (bf16[4,128,768]{2,1,0:T(8,128)(2,1)S(1)}, bf16[4,128,768]{2,1,0:T(8,128)(2,1)S(1)}, u32[]{:S(2)}, u32[]{:S(2)}) collective-permute-start(bf16[4,128,768]{2,1,0:T(8,128)(2,1)S(1)} %get-tuple-element.20.refs_2_.refs_0_), channel_id=1, source_target_pairs={{0,1},{1,0},{2,3},{3,2},{4,5},{5,4},{6,7},{7,6},{8,9},{9,8},{10,11... | collective-permute-start | bytes 2359304 | tf_op jit(solution)/shard_map/ppermute | solution.py:34
  64.7 9.9 %collective-permute-done.16.refs_1_ = bf16[4,128,768]{2,1,0:T(8,128)(2,1)S(1)} collective-permute-done((bf16[4,128,768]{2,1,0:T(8,128)(2,1)S(1)}, bf16[4,128,768]{2,1,0:T(8,128)(2,1)S(1)}, u32[]{:S(2)}, u32[]{:S(2)}) %collective-permute-start.16) | collective-permute-done | bytes 786464 | tf_op jit(solution)/shard_map/ppermute | solution.py:34
  74.6 2.5 %collective-permute-start.23 = (bf16[4,128,768]{2,1,0:T(8,128)(2,1)S(1)}, bf16[4,128,768]{2,1,0:T(8,128)(2,1)S(1)}, u32[]{:S(2)}, u32[]{:S(2)}) collective-permute-start(bf16[4,128,768]{2,1,0:T(8,128)(2,1)S(1)} %collective-permute-done.19.refs_5_.refs_3_), channel_id=1, source_target_pairs={{0,1},{1,0},{2,3},{3,2},{4,5},{5,4},{6,7},{7,6},{8,9},{9,8},{10,11... | collective-permute-start | bytes 2359304 | tf_op jit(solution)/shard_map/ppermute | solution.py:34
  77.1 1.9 %collective-permute-done.23.refs_9_.refs_7_ = bf16[4,128,768]{2,1,0:T(8,128)(2,1)S(1)} collective-permute-done((bf16[4,128,768]{2,1,0:T(8,128)(2,1)S(1)}, bf16[4,128,768]{2,1,0:T(8,128)(2,1)S(1)}, u32[]{:S(2)}, u32[]{:S(2)}) %collective-permute-start.23) | collective-permute-done | bytes 786464 | tf_op jit(solution)/shard_map/ppermute | solution.py:34
  79.0 1.8 %pair_blocks.1 = (bf16[1024,128]{1,0:T(8,128)(2,1)S(1)}, bf16[1024,128]{1,0:T(8,128)(2,1)S(1)}) custom-call(bf16[4,128,768]{2,1,0:T(8,128)(2,1)S(1)} %constant_dynamic-update-slice_fusion.refs_0_, bf16[4,128,768]{2,1,0:T(8,128)(2,1)S(1)} %collective-permute-done.16.refs_1_, bf16[4,128,768]{2,1,0:T(8,128)(2,1)S(1)} %get-tuple-element.20.refs_2_.refs_0_, ...), custom_call_target="tpu_custom_call" | custom-call | tf_op jit(solution)/shard_map/pair_blocks/pallas_call | solution.py:168
  83.1 8.2 %collective-permute-done.24 = bf16[1024,128]{1,0:T(8,128)(2,1)S(1)} collective-permute-done((bf16[1024,128]{1,0:T(8,128)(2,1)S(1)}, bf16[1024,128]{1,0:T(8,128)(2,1)S(1)}, u32[]{:S(2)}, u32[]{:S(2)}) %collective-permute-start.24) | collective-permute-done | bytes 262176 | tf_op jit(solution)/shard_map/ppermute | solution.py:34
  91.6 1.9 %collective-permute-start.29 = (bf16[1024,128]{1,0:T(8,128)(2,1)S(1)}, bf16[1024,128]{1,0:T(8,128)(2,1)S(1)}, u32[]{:S(2)}, u32[]{:S(2)}) collective-permute-start(bf16[1024,128]{1,0:T(8,128)(2,1)S(1)} %get-tuple-element.25), channel_id=1, source_target_pairs={{0,24},{1,25},{2,26},{3,27},{4,28},{5,29},{8,16},{9,17},{10,18},{1... | collective-permute-start | bytes 786440 | tf_op jit(solution)/shard_map/ppermute | solution.py:34
  94.9 5.2 %collective-permute-start.27 = (bf16[1024,128]{1,0:T(8,128)(2,1)S(1)}, bf16[1024,128]{1,0:T(8,128)(2,1)S(1)}, u32[]{:S(2)}, u32[]{:S(2)}) collective-permute-start(bf16[1024,128]{1,0:T(8,128)(2,1)S(1)} %get-tuple-element.27), channel_id=1, source_target_pairs={{0,8},{1,9},{4,12},{5,13},{6,14},{7,15},{10,2},{11,3},{12,4},{13,5... | collective-permute-start | bytes 786440 | tf_op jit(solution)/shard_map/ppermute | solution.py:34
  101.4 6.9 %collective-permute-done.28.refs_2_ = bf16[1024,128]{1,0:T(8,128)(2,1)S(1)} collective-permute-done((bf16[1024,128]{1,0:T(8,128)(2,1)S(1)}, bf16[1024,128]{1,0:T(8,128)(2,1)S(1)}, u32[]{:S(2)}, u32[]{:S(2)}) %collective-permute-start.28) | collective-permute-done | bytes 262176 | tf_op jit(solution)/shard_map/ppermute | solution.py:34
  108.3 1.5 %place_blocks.1 = f32[1024,512]{1,0:T(8,128)} custom-call(bf16[1024,128]{1,0:T(8,128)(2,1)S(1)} %get-tuple-element.28.refs_0_, bf16[1024,128]{1,0:T(8,128)(2,1)S(1)} %collective-permute-done.27.refs_1_, bf16[1024,128]{1,0:T(8,128)(2,1)S(1)} %collective-permute-done.28.refs_2_, bf16[1024,128]{1,0:T(8,128)(2,1)S(1)} %collective-permute-done.29.refs_3_, ...), custom_call_target="tpu_custom_call" | custom-call | tf_op jit(solution)/shard_map/place_blocks/pallas_call | solution.py:274
  (71 shorter events, 17.2 us)
Async XLA Ops:
  0.9 6.6 %collective-permute-start.4 = (bf16[1,128,384]{2,1,0:T(8,128)(2,1)S(1)}, bf16[1,128,384]{2,1,0:T(8,128)(2,1)S(1)}, u32[]{:S(2)}, u32[]{:S(2)}) collective-permute-start(bf16[1,128,384]{2,1,0:T(8,128)(2,1)S(1)} %constant_dynamic-slice_fusion), channel_id=1, source_target_pairs={{0,6},{1,7},{2,4},{3,5},{4,2},{5,3},{6,0},{7,1},{8,14},{9,15},{10,... | collective-permute-start | bytes 294920 | tf_op jit(solution)/shard_map/ppermute | solution.py:34
  4.3 7.9 %collective-permute-start.3 = (bf16[1,128,384]{2,1,0:T(8,128)(2,1)S(1)}, bf16[1,128,384]{2,1,0:T(8,128)(2,1)S(1)}, u32[]{:S(2)}, u32[]{:S(2)}) collective-permute-start(bf16[1,128,384]{2,1,0:T(8,128)(2,1)S(1)} %constant_dynamic-slice_fusion), channel_id=1, source_target_pairs={{0,4},{1,5},{2,6},{3,7},{4,0},{5,1},{6,2},{7,3},{8,12},{9,13},{10,... | collective-permute-start | bytes 294920 | tf_op jit(solution)/shard_map/ppermute | solution.py:34
  4.3 7.9 %collective-permute-start.2 = (bf16[1,128,384]{2,1,0:T(8,128)(2,1)S(1)}, bf16[1,128,384]{2,1,0:T(8,128)(2,1)S(1)}, u32[]{:S(2)}, u32[]{:S(2)}) collective-permute-start(bf16[1,128,384]{2,1,0:T(8,128)(2,1)S(1)} %constant_dynamic-slice_fusion), channel_id=1, source_target_pairs={{0,2},{1,3},{2,0},{3,1},{4,6},{5,7},{6,4},{7,5},{8,10},{9,11},{10,... | collective-permute-start | bytes 294920 | tf_op jit(solution)/shard_map/ppermute | solution.py:34
  4.7 10.3 %collective-permute-start = (bf16[4,128,384]{2,1,0:T(8,128)(2,1)}, bf16[4,128,384]{2,1,0:T(8,128)(2,1)S(1)}, u32[]{:S(2)}, u32[]{:S(2)}) collective-permute-start(bf16[4,128,384]{2,1,0:T(8,128)(2,1)} %bitcast.3), channel_id=1, source_target_pairs={{0,1},{1,0},{2,3},{3,2},{4,5},{5,4},{6,7},{7,6},{8,9},{9,8},{10,11... | collective-permute-start | bytes 1179656 | tf_op jit(solution)/shard_map/ppermute | solution.py:34
  12.2 8.2 %collective-permute-start.10 = (bf16[3,128,384]{2,1,0:T(8,128)(2,1)S(1)}, bf16[3,128,384]{2,1,0:T(8,128)(2,1)S(1)}, u32[]{:S(2)}, u32[]{:S(2)}) collective-permute-start(bf16[3,128,384]{2,1,0:T(8,128)(2,1)S(1)} %pad_maximum_fusion.refs_2_), channel_id=1, source_target_pairs={{0,24},{1,25},{2,26},{3,27},{4,28},{5,29},{6,30},{7,31},{8,16},{9,... | collective-permute-start | bytes 884744 | tf_op jit(solution)/shard_map/ppermute | solution.py:34
  13.4 15.0 %collective-permute-start.8 = (bf16[3,128,384]{2,1,0:T(8,128)(2,1)S(1)}, bf16[3,128,384]{2,1,0:T(8,128)(2,1)S(1)}, u32[]{:S(2)}, u32[]{:S(2)}) collective-permute-start(bf16[3,128,384]{2,1,0:T(8,128)(2,1)S(1)} %pad_maximum_fusion.refs_2_), channel_id=1, source_target_pairs={{0,16},{1,17},{2,18},{3,19},{4,20},{5,21},{6,22},{7,23},{8,24},{9,... | collective-permute-start | bytes 884744 | tf_op jit(solution)/shard_map/ppermute | solution.py:34
  14.7 14.3 %collective-permute-start.6 = (bf16[3,128,384]{2,1,0:T(8,128)(2,1)S(1)}, bf16[3,128,384]{2,1,0:T(8,128)(2,1)S(1)}, u32[]{:S(2)}, u32[]{:S(2)}) collective-permute-start(bf16[3,128,384]{2,1,0:T(8,128)(2,1)S(1)} %pad_maximum_fusion.refs_2_), channel_id=1, source_target_pairs={{0,8},{1,9},{2,10},{3,11},{4,12},{5,13},{6,14},{7,15},{8,0},{9,1},... | collective-permute-start | bytes 884744 | tf_op jit(solution)/shard_map/ppermute | solution.py:34
  14.9 15.6 %collective-permute-start.1 = (bf16[4,128,384]{2,1,0:T(8,128)(2,1)S(1)}, bf16[4,128,384]{2,1,0:T(8,128)(2,1)S(1)}, u32[]{:S(2)}, u32[]{:S(2)}) collective-permute-start(bf16[4,128,384]{2,1,0:T(8,128)(2,1)S(1)} %collective-permute-done.refs_1_), channel_id=1, source_target_pairs={{0,1},{1,0},{2,3},{3,2},{4,5},{5,4},{6,7},{7,6},{8,9},{9,8},{10,11... | collective-permute-start | bytes 1179656 | tf_op jit(solution)/shard_map/ppermute | solution.py:34
  17.1 11.8 %collective-permute-start.5 = (bf16[3,128,384]{2,1,0:T(8,128)(2,1)S(1)}, bf16[3,128,384]{2,1,0:T(8,128)(2,1)S(1)}, u32[]{:S(2)}, u32[]{:S(2)}) collective-permute-start(bf16[3,128,384]{2,1,0:T(8,128)(2,1)S(1)} %pad_maximum_fusion.refs_2_), channel_id=1, source_target_pairs={{0,1},{1,0},{2,3},{3,2},{4,5},{5,4},{6,7},{7,6},{8,9},{9,8},{10,11... | collective-permute-start | bytes 884744 | tf_op jit(solution)/shard_map/ppermute | solution.py:34
  20.4 8.6 %collective-permute-start.11 = (bf16[3,128,384]{2,1,0:T(8,128)(2,1)S(1)}, bf16[3,128,384]{2,1,0:T(8,128)(2,1)S(1)}, u32[]{:S(2)}, u32[]{:S(2)}) collective-permute-start(bf16[3,128,384]{2,1,0:T(8,128)(2,1)S(1)} %collective-permute-done.10.refs_8_), channel_id=1, source_target_pairs={{0,1},{1,0},{2,3},{3,2},{4,5},{5,4},{6,7},{7,6},{8,9},{9,8},{10,11... | collective-permute-start | bytes 884744 | tf_op jit(solution)/shard_map/ppermute | solution.py:34
  35.4 23.9 %collective-permute-start.17 = (bf16[4,128,768]{2,1,0:T(8,128)(2,1)S(1)}, bf16[4,128,768]{2,1,0:T(8,128)(2,1)S(1)}, u32[]{:S(2)}, u32[]{:S(2)}) collective-permute-start(bf16[4,128,768]{2,1,0:T(8,128)(2,1)S(1)} %get-tuple-element.20.refs_2_.refs_0_), channel_id=1, source_target_pairs={{0,8},{1,17},{2,10},{3,19},{4,12},{5,21},{6,14},{7,23},{8,0},{9,25... | collective-permute-start | bytes 2359304 | tf_op jit(solution)/shard_map/ppermute | solution.py:34
  37.1 9.3 %collective-permute-start.13 = (bf16[1,128,768]{2,1,0:T(8,128)(2,1)S(1)}, bf16[1,128,768]{2,1,0:T(8,128)(2,1)S(1)}, u32[]{:S(2)}, u32[]{:S(2)}) collective-permute-start(bf16[1,128,768]{2,1,0:T(8,128)(2,1)S(1)} %get-tuple-element.17), channel_id=1, source_target_pairs={{0,14},{1,15},{2,8},{3,9},{4,10},{5,11},{6,12},{7,13},{8,6},{9,7},... | collective-permute-start | bytes 589832 | tf_op jit(solution)/shard_map/ppermute | solution.py:34
  38.8 25.9 %collective-permute-start.18 = (bf16[4,128,768]{2,1,0:T(8,128)(2,1)S(1)}, bf16[4,128,768]{2,1,0:T(8,128)(2,1)S(1)}, u32[]{:S(2)}, u32[]{:S(2)}) collective-permute-start(bf16[4,128,768]{2,1,0:T(8,128)(2,1)S(1)} %get-tuple-element.20.refs_2_.refs_0_), channel_id=1, source_target_pairs={{0,16},{1,9},{2,18},{3,11},{4,20},{5,13},{6,22},{7,15},{8,24},{9,1... | collective-permute-start | bytes 2359304 | tf_op jit(solution)/shard_map/ppermute | solution.py:34
  39.1 13.3 %collective-permute-start.14 = (bf16[1,128,768]{2,1,0:T(8,128)(2,1)S(1)}, bf16[1,128,768]{2,1,0:T(8,128)(2,1)S(1)}, u32[]{:S(2)}, u32[]{:S(2)}) collective-permute-start(bf16[1,128,768]{2,1,0:T(8,128)(2,1)S(1)} %get-tuple-element.18), channel_id=1, source_target_pairs={{0,22},{1,23},{2,16},{3,17},{4,18},{5,19},{6,20},{7,21},{8,30},{9,... | collective-permute-start | bytes 589832 | tf_op jit(solution)/shard_map/ppermute | solution.py:34
  41.3 14.1 %collective-permute-start.15 = (bf16[1,128,768]{2,1,0:T(8,128)(2,1)S(1)}, bf16[1,128,768]{2,1,0:T(8,128)(2,1)S(1)}, u32[]{:S(2)}, u32[]{:S(2)}) collective-permute-start(bf16[1,128,768]{2,1,0:T(8,128)(2,1)S(1)} %get-tuple-element.19), channel_id=1, source_target_pairs={{0,30},{1,31},{2,24},{3,25},{4,26},{5,27},{6,28},{7,29},{8,22},{9,... | collective-permute-start | bytes 589832 | tf_op jit(solution)/shard_map/ppermute | solution.py:34
  55.4 19.2 %collective-permute-start.16 = (bf16[4,128,768]{2,1,0:T(8,128)(2,1)S(1)}, bf16[4,128,768]{2,1,0:T(8,128)(2,1)S(1)}, u32[]{:S(2)}, u32[]{:S(2)}) collective-permute-start(bf16[4,128,768]{2,1,0:T(8,128)(2,1)S(1)} %constant_dynamic-update-slice_fusion.refs_0_), channel_id=1, source_target_pairs={{0,6},{1,7},{2,0},{3,1},{4,2},{5,3},{6,4},{7,5},{8,14},{9,15},{10,... | collective-permute-start | bytes 2359304 | tf_op jit(solution)/shard_map/ppermute | solution.py:34
  59.3 15.2 %collective-permute-start.19 = (bf16[4,128,768]{2,1,0:T(8,128)(2,1)S(1)}, bf16[4,128,768]{2,1,0:T(8,128)(2,1)S(1)}, u32[]{:S(2)}, u32[]{:S(2)}) collective-permute-start(bf16[4,128,768]{2,1,0:T(8,128)(2,1)S(1)} %collective-permute-done.17.refs_3_.refs_1_), channel_id=1, source_target_pairs={{0,16},{1,9},{2,18},{3,11},{4,20},{5,13},{6,22},{7,15},{8,24},{9,1... | collective-permute-start | bytes 2359304 | tf_op jit(solution)/shard_map/ppermute | solution.py:34
  59.4 17.8 %collective-permute-start.20 = (bf16[4,128,768]{2,1,0:T(8,128)(2,1)S(1)}, bf16[4,128,768]{2,1,0:T(8,128)(2,1)S(1)}, u32[]{:S(2)}, u32[]{:S(2)}) collective-permute-start(bf16[4,128,768]{2,1,0:T(8,128)(2,1)S(1)} %get-tuple-element.20.refs_2_.refs_0_), channel_id=1, source_target_pairs={{0,1},{1,0},{2,3},{3,2},{4,5},{5,4},{6,7},{7,6},{8,9},{9,8},{10,11... | collective-permute-start | bytes 2359304 | tf_op jit(solution)/shard_map/ppermute | solution.py:34
  63.4 13.8 %collective-permute-start.21 = (bf16[4,128,768]{2,1,0:T(8,128)(2,1)S(1)}, bf16[4,128,768]{2,1,0:T(8,128)(2,1)S(1)}, u32[]{:S(2)}, u32[]{:S(2)}) collective-permute-start(bf16[4,128,768]{2,1,0:T(8,128)(2,1)S(1)} %collective-permute-done.17.refs_3_.refs_1_), channel_id=1, source_target_pairs={{0,1},{1,0},{2,3},{3,2},{4,5},{5,4},{6,7},{7,6},{8,9},{9,8},{10,11... | collective-permute-start | bytes 2359304 | tf_op jit(solution)/shard_map/ppermute | solution.py:34
  64.7 12.4 %collective-permute-start.22 = (bf16[4,128,768]{2,1,0:T(8,128)(2,1)S(1)}, bf16[4,128,768]{2,1,0:T(8,128)(2,1)S(1)}, u32[]{:S(2)}, u32[]{:S(2)}) collective-permute-start(bf16[4,128,768]{2,1,0:T(8,128)(2,1)S(1)} %collective-permute-done.18.refs_4_.refs_2_), channel_id=1, source_target_pairs={{0,1},{1,0},{2,3},{3,2},{4,5},{5,4},{6,7},{7,6},{8,9},{9,8},{10,11... | collective-permute-start | bytes 2359304 | tf_op jit(solution)/shard_map/ppermute | solution.py:34
  80.9 10.4 %collective-permute-start.24 = (bf16[1024,128]{1,0:T(8,128)(2,1)S(1)}, bf16[1024,128]{1,0:T(8,128)(2,1)S(1)}, u32[]{:S(2)}, u32[]{:S(2)}) collective-permute-start(bf16[1024,128]{1,0:T(8,128)(2,1)S(1)} %get-tuple-element.22), channel_id=1, source_target_pairs={{0,2},{1,3},{2,4},{3,5},{4,6},{5,7},{6,0},{7,1},{8,10},{9,11},{10,... | collective-permute-start | bytes 786440 | tf_op jit(solution)/shard_map/ppermute | solution.py:34
  91.6 9.8 %collective-permute-start.29 = (bf16[1024,128]{1,0:T(8,128)(2,1)S(1)}, bf16[1024,128]{1,0:T(8,128)(2,1)S(1)}, u32[]{:S(2)}, u32[]{:S(2)}) collective-permute-start(bf16[1024,128]{1,0:T(8,128)(2,1)S(1)} %get-tuple-element.25), channel_id=1, source_target_pairs={{0,24},{1,25},{2,26},{3,27},{4,28},{5,29},{8,16},{9,17},{10,18},{1... | collective-permute-start | bytes 786440 | tf_op jit(solution)/shard_map/ppermute | solution.py:34
  93.6 14.7 %collective-permute-start.28 = (bf16[1024,128]{1,0:T(8,128)(2,1)S(1)}, bf16[1024,128]{1,0:T(8,128)(2,1)S(1)}, u32[]{:S(2)}, u32[]{:S(2)}) collective-permute-start(bf16[1024,128]{1,0:T(8,128)(2,1)S(1)} %get-tuple-element.26), channel_id=1, source_target_pairs={{0,16},{1,17},{2,18},{3,19},{6,22},{7,23},{8,24},{9,25},{10,26},{1... | collective-permute-start | bytes 786440 | tf_op jit(solution)/shard_map/ppermute | solution.py:34
  94.9 13.4 %collective-permute-start.27 = (bf16[1024,128]{1,0:T(8,128)(2,1)S(1)}, bf16[1024,128]{1,0:T(8,128)(2,1)S(1)}, u32[]{:S(2)}, u32[]{:S(2)}) collective-permute-start(bf16[1024,128]{1,0:T(8,128)(2,1)S(1)} %get-tuple-element.27), channel_id=1, source_target_pairs={{0,8},{1,9},{4,12},{5,13},{6,14},{7,15},{10,2},{11,3},{12,4},{13,5... | collective-permute-start | bytes 786440 | tf_op jit(solution)/shard_map/ppermute | solution.py:34
  (16 other events, 146.5 us)

commit v8 on v7

--- a/solution.py
+++ b/solution.py
@@ -246,7 +246,7 @@
     @pl.when((apart > 0) & (apart <= count // 2))
     def _():
         copies = []
-        for k, quarter in enumerate(quarters):
+        for k, quarter in zip(places_held(c, 0), quarters):
             for s in range(CORES):
                 row = core(s) * width + (a ^ k) * n
                 for m in range(count):
@@ -262,7 +262,7 @@
         for s in range(CORES):
             for m in range(count):
                 row = core(s) * width + m * n
-                for k, quarter in enumerate(quarters):
+                for k, quarter in zip(places_held(c, 0), quarters):
                     value = quarter[pl.ds((s * count + m) * n, n), :].astype(jnp.float32)
                     tile(row, (a ^ k) * n, value)
                 copies.append(leave(row, sems.at[len(copies)]))
@@ -310,14 +310,20 @@
     blocks = [jnp.concatenate([v[:width], other(v[width:])]) for v in blocks]
     apart = {1: after(blocks[0], out), 2: blocks[1], 3: mirror}
 
+    core = lax.axis_index("occ") % CORES
     quarters = []
-    for k in range(count):
-        distance = lax.rem((a ^ k) - z + count, count)
+    for j in range(count):
+        distance = lax.rem((a ^ places_held(core, 0)[j]) - z + count, count)
         value = apart[1]
         for d in range(2, count):
             value = jnp.where(distance == d, apart[d], value)
-        if k:
-            value = lay.send(value, lambda a_, z_, c_: (a_ ^ k, z_, c_) if a_ ^ k != z_ else None)
+        if j:
+
+            def where(a_, z_, c_, j=j):
+                place = a_ ^ places_held(c_, 0)[j]
+                return (place, z_, c_) if place != z_ else None
+
+            value = lay.send(value, where)
         quarters.append(value)
     return place_blocks(quarters, out)
 

time: 111 us -> 109 us (0.982)
  starting transfers between devices: 43.8 us -> 36.6 us
  waiting for transfers between devices: 53.4 us -> 58.5 us
    ppermute x30, starting transfers between devices: 43.8 us -> 36.6 us  [send(): return lax.ppermute(value, AXES, pairs)]
    ppermute x30, waiting for transfers between devices: 53.4 us -> 58.5 us  [send(): return lax.ppermute(value, AXES, pairs)]
  transfers between devices with their start and end apart: 30 -> 30, of which waited for: 14 -> 17; matrix products, arithmetic and copies ran while one was open for 1% -> 1% of each run, Pallas kernels for 1% -> 1%
where the time goes in v8:
time: 109 us; the launch traced here: 107 us
  waiting for transfers between devices  58.5 us (54%)
  starting transfers between devices  36.6 us (34%)
  Pallas kernels  7.76 us (7%)
  local copies, waits for them, and re-layouts  2.44 us (2%)
  other arithmetic  1.09 us (1%)
    ppermute x30, waiting for transfers between devices, send(): return lax.ppermute(value, AXES, pairs)  58.5 us
    ppermute x30, starting transfers between devices, send(): return lax.ppermute(value, AXES, pairs)  36.6 us
    pallas_call x1, Pallas kernels, half_transform(): pl.pallas_call(functools.partial(half_kernel, lay, share, len(pieces), mi...  3.05 us
  transfers between devices with their start and end apart: 30, of which 17 were waited for; matrix products, arithmetic and copies ran while one was open for 1% of the time, Pallas kernels for 1%

profile of v8, /device:TPU:5, one launch (start us, length us, event | category | flops | bytes accessed | tf_op | source)
XLA Modules:
  0.0 107.3 jit_solution(204139339438019507)
XLA Ops:
  0.9 3.4 %collective-permute-start.4 = (bf16[1,128,384]{2,1,0:T(8,128)(2,1)S(1)}, bf16[1,128,384]{2,1,0:T(8,128)(2,1)S(1)}, u32[]{:S(2)}, u32[]{:S(2)}) collective-permute-start(bf16[1,128,384]{2,1,0:T(8,128)(2,1)S(1)} %constant_dynamic-slice_fusion), channel_id=1, source_target_pairs={{0,6},{1,7},{2,4},{3,5},{4,2},{5,3},{6,0},{7,1},{8,14},{9,15},{10,... | collective-permute-start | bytes 294920 | tf_op jit(solution)/shard_map/ppermute | solution.py:34
  7.5 4.7 %collective-permute-done.3 = bf16[1,128,384]{2,1,0:T(8,128)(2,1)S(1)} collective-permute-done((bf16[1,128,384]{2,1,0:T(8,128)(2,1)S(1)}, bf16[1,128,384]{2,1,0:T(8,128)(2,1)S(1)}, u32[]{:S(2)}, u32[]{:S(2)}) %collective-permute-start.3) | collective-permute-done | bytes 98336 | tf_op jit(solution)/shard_map/ppermute | solution.py:34
  14.9 2.2 %collective-permute-start.1 = (bf16[4,128,384]{2,1,0:T(8,128)(2,1)S(1)}, bf16[4,128,384]{2,1,0:T(8,128)(2,1)S(1)}, u32[]{:S(2)}, u32[]{:S(2)}) collective-permute-start(bf16[4,128,384]{2,1,0:T(8,128)(2,1)S(1)} %collective-permute-done.refs_1_), channel_id=1, source_target_pairs={{0,1},{1,0},{2,3},{3,2},{4,5},{5,4},{6,7},{7,6},{8,9},{9,8},{10,11... | collective-permute-start | bytes 1179656 | tf_op jit(solution)/shard_map/ppermute | solution.py:34
  17.1 3.2 %collective-permute-done.10.refs_8_ = bf16[3,128,384]{2,1,0:T(8,128)(2,1)S(1)} collective-permute-done((bf16[3,128,384]{2,1,0:T(8,128)(2,1)S(1)}, bf16[3,128,384]{2,1,0:T(8,128)(2,1)S(1)}, u32[]{:S(2)}, u32[]{:S(2)}) %collective-permute-start.10) | collective-permute-done | bytes 294944 | tf_op jit(solution)/shard_map/ppermute | solution.py:34
  20.4 4.1 %collective-permute-start.11 = (bf16[3,128,384]{2,1,0:T(8,128)(2,1)S(1)}, bf16[3,128,384]{2,1,0:T(8,128)(2,1)S(1)}, u32[]{:S(2)}, u32[]{:S(2)}) collective-permute-start(bf16[3,128,384]{2,1,0:T(8,128)(2,1)S(1)} %collective-permute-done.10.refs_8_), channel_id=1, source_target_pairs={{0,1},{1,0},{2,3},{3,2},{4,5},{5,4},{6,7},{7,6},{8,9},{9,8},{10,11... | collective-permute-start | bytes 884744 | tf_op jit(solution)/shard_map/ppermute | solution.py:34
  24.5 3.9 %collective-permute-done.8.refs_6_ = bf16[3,128,384]{2,1,0:T(8,128)(2,1)S(1)} collective-permute-done((bf16[3,128,384]{2,1,0:T(8,128)(2,1)S(1)}, bf16[3,128,384]{2,1,0:T(8,128)(2,1)S(1)}, u32[]{:S(2)}, u32[]{:S(2)}) %collective-permute-start.8) | collective-permute-done | bytes 294944 | tf_op jit(solution)/shard_map/ppermute | solution.py:34
  32.0 3.1 %half_transform.1 = (bf16[4,128,768]{2,1,0:T(8,128)(2,1)S(1)}, bf16[1,128,768]{2,1,0:T(8,128)(2,1)S(1)}, bf16[1,128,768]{2,1,0:T(8,128)(2,1)S(1)}, bf16[1,128,76...) custom-call(s32[1,81]{1,0:T(1,128)S(1)} %pad_add_fusion.meta, bf16[2,24,128,128]{3,2,1,0:T(8,128)(2,1)S(1)} %copy-done.9, ...), custom_call_target="tpu_custom_call" | custom-call | tf_op jit(solution)/shard_map/half_transform/pallas_call | solution.py:122
  39.3 3.1 %collective-permute-done.12 = bf16[1,128,768]{2,1,0:T(8,128)(2,1)S(1)} collective-permute-done((bf16[1,128,768]{2,1,0:T(8,128)(2,1)S(1)}, bf16[1,128,768]{2,1,0:T(8,128)(2,1)S(1)}, u32[]{:S(2)}, u32[]{:S(2)}) %collective-permute-start.12) | collective-permute-done | bytes 196640 | tf_op jit(solution)/shard_map/ppermute | solution.py:34
  43.8 2.2 %collective-permute-done.13 = bf16[1,128,768]{2,1,0:T(8,128)(2,1)S(1)} collective-permute-done((bf16[1,128,768]{2,1,0:T(8,128)(2,1)S(1)}, bf16[1,128,768]{2,1,0:T(8,128)(2,1)S(1)}, u32[]{:S(2)}, u32[]{:S(2)}) %collective-permute-start.13) | collective-permute-done | bytes 196640 | tf_op jit(solution)/shard_map/ppermute | solution.py:34
  46.0 6.2 %collective-permute-done.14 = bf16[1,128,768]{2,1,0:T(8,128)(2,1)S(1)} collective-permute-done((bf16[1,128,768]{2,1,0:T(8,128)(2,1)S(1)}, bf16[1,128,768]{2,1,0:T(8,128)(2,1)S(1)}, u32[]{:S(2)}, u32[]{:S(2)}) %collective-permute-start.14) | collective-permute-done | bytes 196640 | tf_op jit(solution)/shard_map/ppermute | solution.py:34
  52.3 2.6 %collective-permute-done.15 = bf16[1,128,768]{2,1,0:T(8,128)(2,1)S(1)} collective-permute-done((bf16[1,128,768]{2,1,0:T(8,128)(2,1)S(1)}, bf16[1,128,768]{2,1,0:T(8,128)(2,1)S(1)}, u32[]{:S(2)}, u32[]{:S(2)}) %collective-permute-start.15) | collective-permute-done | bytes 196640 | tf_op jit(solution)/shard_map/ppermute | solution.py:34
  54.8 2.0 %collective-permute-start.16 = (bf16[4,128,768]{2,1,0:T(8,128)(2,1)S(1)}, bf16[4,128,768]{2,1,0:T(8,128)(2,1)S(1)}, u32[]{:S(2)}, u32[]{:S(2)}) collective-permute-start(bf16[4,128,768]{2,1,0:T(8,128)(2,1)S(1)} %constant_dynamic-update-slice_fusion.refs_0_), channel_id=1, source_target_pairs={{0,6},{1,7},{2,0},{3,1},{4,2},{5,3},{6,4},{7,5},{8,14},{9,15},{10,... | collective-permute-start | bytes 2359304 | tf_op jit(solution)/shard_map/ppermute | solution.py:34
  59.0 2.6 %collective-permute-start.20 = (bf16[4,128,768]{2,1,0:T(8,128)(2,1)S(1)}, bf16[4,128,768]{2,1,0:T(8,128)(2,1)S(1)}, u32[]{:S(2)}, u32[]{:S(2)}) collective-permute-start(bf16[4,128,768]{2,1,0:T(8,128)(2,1)S(1)} %get-tuple-element.20.refs_2_.refs_0_), channel_id=1, source_target_pairs={{0,1},{1,0},{2,3},{3,2},{4,5},{5,4},{6,7},{7,6},{8,9},{9,8},{10,11... | collective-permute-start | bytes 2359304 | tf_op jit(solution)/shard_map/ppermute | solution.py:34
  61.6 1.5 %collective-permute-done.18.refs_4_.refs_2_ = bf16[4,128,768]{2,1,0:T(8,128)(2,1)S(1)} collective-permute-done((bf16[4,128,768]{2,1,0:T(8,128)(2,1)S(1)}, bf16[4,128,768]{2,1,0:T(8,128)(2,1)S(1)}, u32[]{:S(2)}, u32[]{:S(2)}) %collective-permute-start.18) | collective-permute-done | bytes 786464 | tf_op jit(solution)/shard_map/ppermute | solution.py:34
  63.5 8.9 %collective-permute-done.16.refs_1_ = bf16[4,128,768]{2,1,0:T(8,128)(2,1)S(1)} collective-permute-done((bf16[4,128,768]{2,1,0:T(8,128)(2,1)S(1)}, bf16[4,128,768]{2,1,0:T(8,128)(2,1)S(1)}, u32[]{:S(2)}, u32[]{:S(2)}) %collective-permute-start.16) | collective-permute-done | bytes 786464 | tf_op jit(solution)/shard_map/ppermute | solution.py:34
  72.4 2.5 %collective-permute-start.23 = (bf16[4,128,768]{2,1,0:T(8,128)(2,1)S(1)}, bf16[4,128,768]{2,1,0:T(8,128)(2,1)S(1)}, u32[]{:S(2)}, u32[]{:S(2)}) collective-permute-start(bf16[4,128,768]{2,1,0:T(8,128)(2,1)S(1)} %collective-permute-done.19.refs_5_.refs_3_), channel_id=1, source_target_pairs={{0,1},{1,0},{2,3},{3,2},{4,5},{5,4},{6,7},{7,6},{8,9},{9,8},{10,11... | collective-permute-start | bytes 2359304 | tf_op jit(solution)/shard_map/ppermute | solution.py:34
  74.9 1.9 %collective-permute-done.23.refs_9_.refs_7_ = bf16[4,128,768]{2,1,0:T(8,128)(2,1)S(1)} collective-permute-done((bf16[4,128,768]{2,1,0:T(8,128)(2,1)S(1)}, bf16[4,128,768]{2,1,0:T(8,128)(2,1)S(1)}, u32[]{:S(2)}, u32[]{:S(2)}) %collective-permute-start.23) | collective-permute-done | bytes 786464 | tf_op jit(solution)/shard_map/ppermute | solution.py:34
  76.8 1.8 %pair_blocks.1 = (bf16[1024,128]{1,0:T(8,128)(2,1)S(1)}, bf16[1024,128]{1,0:T(8,128)(2,1)S(1)}) custom-call(bf16[4,128,768]{2,1,0:T(8,128)(2,1)S(1)} %constant_dynamic-update-slice_fusion.refs_0_, bf16[4,128,768]{2,1,0:T(8,128)(2,1)S(1)} %collective-permute-done.16.refs_1_, bf16[4,128,768]{2,1,0:T(8,128)(2,1)S(1)} %get-tuple-element.20.refs_2_.refs_0_, ...), custom_call_target="tpu_custom_call" | custom-call | tf_op jit(solution)/shard_map/pair_blocks/pallas_call | solution.py:168
  81.5 7.4 %collective-permute-done.24 = bf16[1024,128]{1,0:T(8,128)(2,1)S(1)} collective-permute-done((bf16[1024,128]{1,0:T(8,128)(2,1)S(1)}, bf16[1024,128]{1,0:T(8,128)(2,1)S(1)}, u32[]{:S(2)}, u32[]{:S(2)}) %collective-permute-start.24) | collective-permute-done | bytes 262176 | tf_op jit(solution)/shard_map/ppermute | solution.py:34
  89.1 3.5 %collective-permute-start.29 = (bf16[1024,128]{1,0:T(8,128)(2,1)S(1)}, bf16[1024,128]{1,0:T(8,128)(2,1)S(1)}, u32[]{:S(2)}, u32[]{:S(2)}) collective-permute-start(bf16[1024,128]{1,0:T(8,128)(2,1)S(1)} %get-tuple-element.25), channel_id=1, source_target_pairs={{0,24},{1,25},{2,26},{3,27},{4,28},{5,29},{8,16},{9,17},{10,18},{1... | collective-permute-start | bytes 786440 | tf_op jit(solution)/shard_map/ppermute | solution.py:34
  92.7 1.9 %collective-permute-start.28 = (bf16[1024,128]{1,0:T(8,128)(2,1)S(1)}, bf16[1024,128]{1,0:T(8,128)(2,1)S(1)}, u32[]{:S(2)}, u32[]{:S(2)}) collective-permute-start(bf16[1024,128]{1,0:T(8,128)(2,1)S(1)} %get-tuple-element.26), channel_id=1, source_target_pairs={{0,16},{1,9},{2,18},{5,13},{6,22},{7,15},{8,24},{10,26},{11,3},{12... | collective-permute-start | bytes 786440 | tf_op jit(solution)/shard_map/ppermute | solution.py:34
  95.9 3.0 %collective-permute-done.29.refs_3_ = bf16[1024,128]{1,0:T(8,128)(2,1)S(1)} collective-permute-done((bf16[1024,128]{1,0:T(8,128)(2,1)S(1)}, bf16[1024,128]{1,0:T(8,128)(2,1)S(1)}, u32[]{:S(2)}, u32[]{:S(2)}) %collective-permute-start.29) | collective-permute-done | bytes 262176 | tf_op jit(solution)/shard_map/ppermute | solution.py:34
  98.9 3.8 %collective-permute-done.28.refs_2_ = bf16[1024,128]{1,0:T(8,128)(2,1)S(1)} collective-permute-done((bf16[1024,128]{1,0:T(8,128)(2,1)S(1)}, bf16[1024,128]{1,0:T(8,128)(2,1)S(1)}, u32[]{:S(2)}, u32[]{:S(2)}) %collective-permute-start.28) | collective-permute-done | bytes 262176 | tf_op jit(solution)/shard_map/ppermute | solution.py:34
  102.6 3.2 %collective-permute-done.27.refs_1_ = bf16[1024,128]{1,0:T(8,128)(2,1)S(1)} collective-permute-done((bf16[1024,128]{1,0:T(8,128)(2,1)S(1)}, bf16[1024,128]{1,0:T(8,128)(2,1)S(1)}, u32[]{:S(2)}, u32[]{:S(2)}) %collective-permute-start.27) | collective-permute-done | bytes 262176 | tf_op jit(solution)/shard_map/ppermute | solution.py:34
  (71 shorter events, 23.7 us)
Async XLA Ops:
  0.9 6.6 %collective-permute-start.4 = (bf16[1,128,384]{2,1,0:T(8,128)(2,1)S(1)}, bf16[1,128,384]{2,1,0:T(8,128)(2,1)S(1)}, u32[]{:S(2)}, u32[]{:S(2)}) collective-permute-start(bf16[1,128,384]{2,1,0:T(8,128)(2,1)S(1)} %constant_dynamic-slice_fusion), channel_id=1, source_target_pairs={{0,6},{1,7},{2,4},{3,5},{4,2},{5,3},{6,0},{7,1},{8,14},{9,15},{10,... | collective-permute-start | bytes 294920 | tf_op jit(solution)/shard_map/ppermute | solution.py:34
  4.3 7.9 %collective-permute-start.3 = (bf16[1,128,384]{2,1,0:T(8,128)(2,1)S(1)}, bf16[1,128,384]{2,1,0:T(8,128)(2,1)S(1)}, u32[]{:S(2)}, u32[]{:S(2)}) collective-permute-start(bf16[1,128,384]{2,1,0:T(8,128)(2,1)S(1)} %constant_dynamic-slice_fusion), channel_id=1, source_target_pairs={{0,4},{1,5},{2,6},{3,7},{4,0},{5,1},{6,2},{7,3},{8,12},{9,13},{10,... | collective-permute-start | bytes 294920 | tf_op jit(solution)/shard_map/ppermute | solution.py:34
  4.3 7.9 %collective-permute-start.2 = (bf16[1,128,384]{2,1,0:T(8,128)(2,1)S(1)}, bf16[1,128,384]{2,1,0:T(8,128)(2,1)S(1)}, u32[]{:S(2)}, u32[]{:S(2)}) collective-permute-start(bf16[1,128,384]{2,1,0:T(8,128)(2,1)S(1)} %constant_dynamic-slice_fusion), channel_id=1, source_target_pairs={{0,2},{1,3},{2,0},{3,1},{4,6},{5,7},{6,4},{7,5},{8,10},{9,11},{10,... | collective-permute-start | bytes 294920 | tf_op jit(solution)/shard_map/ppermute | solution.py:34
  4.7 10.3 %collective-permute-start = (bf16[4,128,384]{2,1,0:T(8,128)(2,1)}, bf16[4,128,384]{2,1,0:T(8,128)(2,1)S(1)}, u32[]{:S(2)}, u32[]{:S(2)}) collective-permute-start(bf16[4,128,384]{2,1,0:T(8,128)(2,1)} %bitcast.3), channel_id=1, source_target_pairs={{0,1},{1,0},{2,3},{3,2},{4,5},{5,4},{6,7},{7,6},{8,9},{9,8},{10,11... | collective-permute-start | bytes 1179656 | tf_op jit(solution)/shard_map/ppermute | solution.py:34
  12.2 8.2 %collective-permute-start.10 = (bf16[3,128,384]{2,1,0:T(8,128)(2,1)S(1)}, bf16[3,128,384]{2,1,0:T(8,128)(2,1)S(1)}, u32[]{:S(2)}, u32[]{:S(2)}) collective-permute-start(bf16[3,128,384]{2,1,0:T(8,128)(2,1)S(1)} %pad_maximum_fusion.refs_2_), channel_id=1, source_target_pairs={{0,24},{1,25},{2,26},{3,27},{4,28},{5,29},{6,30},{7,31},{8,16},{9,... | collective-permute-start | bytes 884744 | tf_op jit(solution)/shard_map/ppermute | solution.py:34
  13.4 15.0 %collective-permute-start.8 = (bf16[3,128,384]{2,1,0:T(8,128)(2,1)S(1)}, bf16[3,128,384]{2,1,0:T(8,128)(2,1)S(1)}, u32[]{:S(2)}, u32[]{:S(2)}) collective-permute-start(bf16[3,128,384]{2,1,0:T(8,128)(2,1)S(1)} %pad_maximum_fusion.refs_2_), channel_id=1, source_target_pairs={{0,16},{1,17},{2,18},{3,19},{4,20},{5,21},{6,22},{7,23},{8,24},{9,... | collective-permute-start | bytes 884744 | tf_op jit(solution)/shard_map/ppermute | solution.py:34
  14.7 14.3 %collective-permute-start.6 = (bf16[3,128,384]{2,1,0:T(8,128)(2,1)S(1)}, bf16[3,128,384]{2,1,0:T(8,128)(2,1)S(1)}, u32[]{:S(2)}, u32[]{:S(2)}) collective-permute-start(bf16[3,128,384]{2,1,0:T(8,128)(2,1)S(1)} %pad_maximum_fusion.refs_2_), channel_id=1, source_target_pairs={{0,8},{1,9},{2,10},{3,11},{4,12},{5,13},{6,14},{7,15},{8,0},{9,1},... | collective-permute-start | bytes 884744 | tf_op jit(solution)/shard_map/ppermute | solution.py:34
  14.9 15.6 %collective-permute-start.1 = (bf16[4,128,384]{2,1,0:T(8,128)(2,1)S(1)}, bf16[4,128,384]{2,1,0:T(8,128)(2,1)S(1)}, u32[]{:S(2)}, u32[]{:S(2)}) collective-permute-start(bf16[4,128,384]{2,1,0:T(8,128)(2,1)S(1)} %collective-permute-done.refs_1_), channel_id=1, source_target_pairs={{0,1},{1,0},{2,3},{3,2},{4,5},{5,4},{6,7},{7,6},{8,9},{9,8},{10,11... | collective-permute-start | bytes 1179656 | tf_op jit(solution)/shard_map/ppermute | solution.py:34
  17.1 11.8 %collective-permute-start.5 = (bf16[3,128,384]{2,1,0:T(8,128)(2,1)S(1)}, bf16[3,128,384]{2,1,0:T(8,128)(2,1)S(1)}, u32[]{:S(2)}, u32[]{:S(2)}) collective-permute-start(bf16[3,128,384]{2,1,0:T(8,128)(2,1)S(1)} %pad_maximum_fusion.refs_2_), channel_id=1, source_target_pairs={{0,1},{1,0},{2,3},{3,2},{4,5},{5,4},{6,7},{7,6},{8,9},{9,8},{10,11... | collective-permute-start | bytes 884744 | tf_op jit(solution)/shard_map/ppermute | solution.py:34
  20.4 8.6 %collective-permute-start.11 = (bf16[3,128,384]{2,1,0:T(8,128)(2,1)S(1)}, bf16[3,128,384]{2,1,0:T(8,128)(2,1)S(1)}, u32[]{:S(2)}, u32[]{:S(2)}) collective-permute-start(bf16[3,128,384]{2,1,0:T(8,128)(2,1)S(1)} %collective-permute-done.10.refs_8_), channel_id=1, source_target_pairs={{0,1},{1,0},{2,3},{3,2},{4,5},{5,4},{6,7},{7,6},{8,9},{9,8},{10,11... | collective-permute-start | bytes 884744 | tf_op jit(solution)/shard_map/ppermute | solution.py:34
  35.0 23.2 %collective-permute-start.17 = (bf16[4,128,768]{2,1,0:T(8,128)(2,1)S(1)}, bf16[4,128,768]{2,1,0:T(8,128)(2,1)S(1)}, u32[]{:S(2)}, u32[]{:S(2)}) collective-permute-start(bf16[4,128,768]{2,1,0:T(8,128)(2,1)S(1)} %get-tuple-element.20.refs_2_.refs_0_), channel_id=1, source_target_pairs={{0,8},{1,17},{2,10},{3,19},{4,12},{5,21},{6,14},{7,23},{8,0},{9,25... | collective-permute-start | bytes 2359304 | tf_op jit(solution)/shard_map/ppermute | solution.py:34
  37.1 8.9 %collective-permute-start.13 = (bf16[1,128,768]{2,1,0:T(8,128)(2,1)S(1)}, bf16[1,128,768]{2,1,0:T(8,128)(2,1)S(1)}, u32[]{:S(2)}, u32[]{:S(2)}) collective-permute-start(bf16[1,128,768]{2,1,0:T(8,128)(2,1)S(1)} %get-tuple-element.17), channel_id=1, source_target_pairs={{0,14},{1,15},{2,8},{3,9},{4,10},{5,11},{6,12},{7,13},{8,6},{9,7},... | collective-permute-start | bytes 589832 | tf_op jit(solution)/shard_map/ppermute | solution.py:34
  37.5 25.6 %collective-permute-start.18 = (bf16[4,128,768]{2,1,0:T(8,128)(2,1)S(1)}, bf16[4,128,768]{2,1,0:T(8,128)(2,1)S(1)}, u32[]{:S(2)}, u32[]{:S(2)}) collective-permute-start(bf16[4,128,768]{2,1,0:T(8,128)(2,1)S(1)} %get-tuple-element.20.refs_2_.refs_0_), channel_id=1, source_target_pairs={{0,16},{1,9},{2,18},{3,11},{4,20},{5,13},{6,22},{7,15},{8,24},{9,1... | collective-permute-start | bytes 2359304 | tf_op jit(solution)/shard_map/ppermute | solution.py:34
  38.2 14.0 %collective-permute-start.14 = (bf16[1,128,768]{2,1,0:T(8,128)(2,1)S(1)}, bf16[1,128,768]{2,1,0:T(8,128)(2,1)S(1)}, u32[]{:S(2)}, u32[]{:S(2)}) collective-permute-start(bf16[1,128,768]{2,1,0:T(8,128)(2,1)S(1)} %get-tuple-element.18), channel_id=1, source_target_pairs={{0,22},{1,23},{2,16},{3,17},{4,18},{5,19},{6,20},{7,21},{8,30},{9,... | collective-permute-start | bytes 589832 | tf_op jit(solution)/shard_map/ppermute | solution.py:34
  42.4 12.4 %collective-permute-start.15 = (bf16[1,128,768]{2,1,0:T(8,128)(2,1)S(1)}, bf16[1,128,768]{2,1,0:T(8,128)(2,1)S(1)}, u32[]{:S(2)}, u32[]{:S(2)}) collective-permute-start(bf16[1,128,768]{2,1,0:T(8,128)(2,1)S(1)} %get-tuple-element.19), channel_id=1, source_target_pairs={{0,30},{1,31},{2,24},{3,25},{4,26},{5,27},{6,28},{7,29},{8,22},{9,... | collective-permute-start | bytes 589832 | tf_op jit(solution)/shard_map/ppermute | solution.py:34
  54.8 17.5 %collective-permute-start.16 = (bf16[4,128,768]{2,1,0:T(8,128)(2,1)S(1)}, bf16[4,128,768]{2,1,0:T(8,128)(2,1)S(1)}, u32[]{:S(2)}, u32[]{:S(2)}) collective-permute-start(bf16[4,128,768]{2,1,0:T(8,128)(2,1)S(1)} %constant_dynamic-update-slice_fusion.refs_0_), channel_id=1, source_target_pairs={{0,6},{1,7},{2,0},{3,1},{4,2},{5,3},{6,4},{7,5},{8,14},{9,15},{10,... | collective-permute-start | bytes 2359304 | tf_op jit(solution)/shard_map/ppermute | solution.py:34
  58.2 14.2 %collective-permute-start.19 = (bf16[4,128,768]{2,1,0:T(8,128)(2,1)S(1)}, bf16[4,128,768]{2,1,0:T(8,128)(2,1)S(1)}, u32[]{:S(2)}, u32[]{:S(2)}) collective-permute-start(bf16[4,128,768]{2,1,0:T(8,128)(2,1)S(1)} %collective-permute-done.17.refs_3_.refs_1_), channel_id=1, source_target_pairs={{0,16},{1,9},{2,18},{3,11},{4,20},{5,13},{6,22},{7,15},{8,24},{9,1... | collective-permute-start | bytes 2359304 | tf_op jit(solution)/shard_map/ppermute | solution.py:34
  59.0 15.8 %collective-permute-start.20 = (bf16[4,128,768]{2,1,0:T(8,128)(2,1)S(1)}, bf16[4,128,768]{2,1,0:T(8,128)(2,1)S(1)}, u32[]{:S(2)}, u32[]{:S(2)}) collective-permute-start(bf16[4,128,768]{2,1,0:T(8,128)(2,1)S(1)} %get-tuple-element.20.refs_2_.refs_0_), channel_id=1, source_target_pairs={{0,1},{1,0},{2,3},{3,2},{4,5},{5,4},{6,7},{7,6},{8,9},{9,8},{10,11... | collective-permute-start | bytes 2359304 | tf_op jit(solution)/shard_map/ppermute | solution.py:34
  61.6 13.2 %collective-permute-start.21 = (bf16[4,128,768]{2,1,0:T(8,128)(2,1)S(1)}, bf16[4,128,768]{2,1,0:T(8,128)(2,1)S(1)}, u32[]{:S(2)}, u32[]{:S(2)}) collective-permute-start(bf16[4,128,768]{2,1,0:T(8,128)(2,1)S(1)} %collective-permute-done.17.refs_3_.refs_1_), channel_id=1, source_target_pairs={{0,1},{1,0},{2,3},{3,2},{4,5},{5,4},{6,7},{7,6},{8,9},{9,8},{10,11... | collective-permute-start | bytes 2359304 | tf_op jit(solution)/shard_map/ppermute | solution.py:34
  63.1 11.7 %collective-permute-start.22 = (bf16[4,128,768]{2,1,0:T(8,128)(2,1)S(1)}, bf16[4,128,768]{2,1,0:T(8,128)(2,1)S(1)}, u32[]{:S(2)}, u32[]{:S(2)}) collective-permute-start(bf16[4,128,768]{2,1,0:T(8,128)(2,1)S(1)} %collective-permute-done.18.refs_4_.refs_2_), channel_id=1, source_target_pairs={{0,1},{1,0},{2,3},{3,2},{4,5},{5,4},{6,7},{7,6},{8,9},{9,8},{10,11... | collective-permute-start | bytes 2359304 | tf_op jit(solution)/shard_map/ppermute | solution.py:34
  78.7 10.2 %collective-permute-start.24 = (bf16[1024,128]{1,0:T(8,128)(2,1)S(1)}, bf16[1024,128]{1,0:T(8,128)(2,1)S(1)}, u32[]{:S(2)}, u32[]{:S(2)}) collective-permute-start(bf16[1024,128]{1,0:T(8,128)(2,1)S(1)} %get-tuple-element.22), channel_id=1, source_target_pairs={{0,2},{1,3},{2,4},{3,5},{4,6},{5,7},{6,0},{7,1},{8,10},{9,11},{10,... | collective-permute-start | bytes 786440 | tf_op jit(solution)/shard_map/ppermute | solution.py:34
  89.1 9.7 %collective-permute-start.29 = (bf16[1024,128]{1,0:T(8,128)(2,1)S(1)}, bf16[1024,128]{1,0:T(8,128)(2,1)S(1)}, u32[]{:S(2)}, u32[]{:S(2)}) collective-permute-start(bf16[1024,128]{1,0:T(8,128)(2,1)S(1)} %get-tuple-element.25), channel_id=1, source_target_pairs={{0,24},{1,25},{2,26},{3,27},{4,28},{5,29},{8,16},{9,17},{10,18},{1... | collective-permute-start | bytes 786440 | tf_op jit(solution)/shard_map/ppermute | solution.py:34
  92.7 10.0 %collective-permute-start.28 = (bf16[1024,128]{1,0:T(8,128)(2,1)S(1)}, bf16[1024,128]{1,0:T(8,128)(2,1)S(1)}, u32[]{:S(2)}, u32[]{:S(2)}) collective-permute-start(bf16[1024,128]{1,0:T(8,128)(2,1)S(1)} %get-tuple-element.26), channel_id=1, source_target_pairs={{0,16},{1,9},{2,18},{5,13},{6,22},{7,15},{8,24},{10,26},{11,3},{12... | collective-permute-start | bytes 786440 | tf_op jit(solution)/shard_map/ppermute | solution.py:34
  94.6 11.3 %collective-permute-start.27 = (bf16[1024,128]{1,0:T(8,128)(2,1)S(1)}, bf16[1024,128]{1,0:T(8,128)(2,1)S(1)}, u32[]{:S(2)}, u32[]{:S(2)}) collective-permute-start(bf16[1024,128]{1,0:T(8,128)(2,1)S(1)} %get-tuple-element.27), channel_id=1, source_target_pairs={{0,8},{1,17},{3,19},{4,12},{6,14},{7,23},{9,25},{10,2},{11,27},{12... | collective-permute-start | bytes 786440 | tf_op jit(solution)/shard_map/ppermute | solution.py:34
  (16 other events, 142.8 us)

commit v9 on v8

--- a/solution.py
+++ b/solution.py
@@ -274,7 +274,7 @@
     return pl.pallas_call(
         place_kernel,
         out_shape=jax.ShapeDtypeStruct(out.shape, out.dtype),
-        in_specs=[IN_VMEM] * (len(quarters) + 1),
+        in_specs=[IN_VMEM] * len(quarters) + [ANY],
         out_specs=ANY,
         scratch_shapes=[pltpu.VMEM(out.shape, out.dtype), pltpu.SemaphoreType.DMA((CORES * len(quarters),))],
         compiler_params=pltpu.CompilerParams(vmem_limit_bytes=VMEM_LIMIT),

time: 109 us -> 111 us (1.018)
  waiting for transfers between devices: 58.5 us -> 59.8 us
    ppermute x30, waiting for transfers between devices: 58.5 us -> 59.8 us  [send(): return lax.ppermute(value, AXES, pairs)]
where the time goes in v9:
time: 111 us; the launch traced here: 110 us
  waiting for transfers between devices  59.8 us (54%)
  starting transfers between devices  36.7 us (33%)
  Pallas kernels  8.82 us (8%)
  local copies, waits for them, and re-layouts  2.44 us (2%)
    ppermute x30, waiting for transfers between devices, send(): return lax.ppermute(value, AXES, pairs)  59.8 us
    ppermute x30, starting transfers between devices, send(): return lax.ppermute(value, AXES, pairs)  36.7 us
    pallas_call x1, Pallas kernels, half_transform(): pl.pallas_call(functools.partial(half_kernel, lay, share, len(pieces), mi...  4.13 us
  transfers between devices with their start and end apart: 30, of which 17 were waited for; matrix products, arithmetic and copies ran while one was open for 1% of the time, Pallas kernels for 1%

profile of v9, /device:TPU:5, one launch (start us, length us, event | category | flops | bytes accessed | tf_op | source)
XLA Modules:
  0.0 109.8 jit_solution(204139339438019507)
XLA Ops:
  0.9 3.4 %collective-permute-start.4 = (bf16[1,128,384]{2,1,0:T(8,128)(2,1)S(1)}, bf16[1,128,384]{2,1,0:T(8,128)(2,1)S(1)}, u32[]{:S(2)}, u32[]{:S(2)}) collective-permute-start(bf16[1,128,384]{2,1,0:T(8,128)(2,1)S(1)} %constant_dynamic-slice_fusion), channel_id=1, source_target_pairs={{0,6},{1,7},{2,4},{3,5},{4,2},{5,3},{6,0},{7,1},{8,14},{9,15},{10,... | collective-permute-start | bytes 294920 | tf_op jit(solution)/shard_map/ppermute | solution.py:34
  7.5 4.7 %collective-permute-done.3 = bf16[1,128,384]{2,1,0:T(8,128)(2,1)S(1)} collective-permute-done((bf16[1,128,384]{2,1,0:T(8,128)(2,1)S(1)}, bf16[1,128,384]{2,1,0:T(8,128)(2,1)S(1)}, u32[]{:S(2)}, u32[]{:S(2)}) %collective-permute-start.3) | collective-permute-done | bytes 98336 | tf_op jit(solution)/shard_map/ppermute | solution.py:34
  14.9 2.2 %collective-permute-start.1 = (bf16[4,128,384]{2,1,0:T(8,128)(2,1)S(1)}, bf16[4,128,384]{2,1,0:T(8,128)(2,1)S(1)}, u32[]{:S(2)}, u32[]{:S(2)}) collective-permute-start(bf16[4,128,384]{2,1,0:T(8,128)(2,1)S(1)} %collective-permute-done.refs_1_), channel_id=1, source_target_pairs={{0,1},{1,0},{2,3},{3,2},{4,5},{5,4},{6,7},{7,6},{8,9},{9,8},{10,11... | collective-permute-start | bytes 1179656 | tf_op jit(solution)/shard_map/ppermute | solution.py:34
  17.1 3.2 %collective-permute-done.10.refs_8_ = bf16[3,128,384]{2,1,0:T(8,128)(2,1)S(1)} collective-permute-done((bf16[3,128,384]{2,1,0:T(8,128)(2,1)S(1)}, bf16[3,128,384]{2,1,0:T(8,128)(2,1)S(1)}, u32[]{:S(2)}, u32[]{:S(2)}) %collective-permute-start.10) | collective-permute-done | bytes 294944 | tf_op jit(solution)/shard_map/ppermute | solution.py:34
  20.4 4.1 %collective-permute-start.11 = (bf16[3,128,384]{2,1,0:T(8,128)(2,1)S(1)}, bf16[3,128,384]{2,1,0:T(8,128)(2,1)S(1)}, u32[]{:S(2)}, u32[]{:S(2)}) collective-permute-start(bf16[3,128,384]{2,1,0:T(8,128)(2,1)S(1)} %collective-permute-done.10.refs_8_), channel_id=1, source_target_pairs={{0,1},{1,0},{2,3},{3,2},{4,5},{5,4},{6,7},{7,6},{8,9},{9,8},{10,11... | collective-permute-start | bytes 884744 | tf_op jit(solution)/shard_map/ppermute | solution.py:34
  24.5 3.9 %collective-permute-done.8.refs_6_ = bf16[3,128,384]{2,1,0:T(8,128)(2,1)S(1)} collective-permute-done((bf16[3,128,384]{2,1,0:T(8,128)(2,1)S(1)}, bf16[3,128,384]{2,1,0:T(8,128)(2,1)S(1)}, u32[]{:S(2)}, u32[]{:S(2)}) %collective-permute-start.8) | collective-permute-done | bytes 294944 | tf_op jit(solution)/shard_map/ppermute | solution.py:34
  32.0 4.1 %half_transform.1 = (bf16[4,128,768]{2,1,0:T(8,128)(2,1)S(1)}, bf16[1,128,768]{2,1,0:T(8,128)(2,1)S(1)}, bf16[1,128,768]{2,1,0:T(8,128)(2,1)S(1)}, bf16[1,128,76...) custom-call(s32[1,81]{1,0:T(1,128)S(1)} %pad_add_fusion.meta, bf16[2,24,128,128]{3,2,1,0:T(8,128)(2,1)S(1)} %copy-done.9, ...), custom_call_target="tpu_custom_call" | custom-call | tf_op jit(solution)/shard_map/half_transform/pallas_call | solution.py:122
  36.2 1.9 %collective-permute-start.12 = (bf16[1,128,768]{2,1,0:T(8,128)(2,1)S(1)}, bf16[1,128,768]{2,1,0:T(8,128)(2,1)S(1)}, u32[]{:S(2)}, u32[]{:S(2)}) collective-permute-start(bf16[1,128,768]{2,1,0:T(8,128)(2,1)S(1)} %get-tuple-element.16), channel_id=1, source_target_pairs={{0,6},{1,7},{2,0},{3,1},{4,2},{5,3},{6,4},{7,5},{8,14},{9,15},{10,... | collective-permute-start | bytes 589832 | tf_op jit(solution)/shard_map/ppermute | solution.py:34
  39.5 3.3 %collective-permute-done.12 = bf16[1,128,768]{2,1,0:T(8,128)(2,1)S(1)} collective-permute-done((bf16[1,128,768]{2,1,0:T(8,128)(2,1)S(1)}, bf16[1,128,768]{2,1,0:T(8,128)(2,1)S(1)}, u32[]{:S(2)}, u32[]{:S(2)}) %collective-permute-start.12) | collective-permute-done | bytes 196640 | tf_op jit(solution)/shard_map/ppermute | solution.py:34
  42.8 3.8 %collective-permute-start.15 = (bf16[1,128,768]{2,1,0:T(8,128)(2,1)S(1)}, bf16[1,128,768]{2,1,0:T(8,128)(2,1)S(1)}, u32[]{:S(2)}, u32[]{:S(2)}) collective-permute-start(bf16[1,128,768]{2,1,0:T(8,128)(2,1)S(1)} %get-tuple-element.19), channel_id=1, source_target_pairs={{0,30},{1,31},{2,24},{3,25},{4,26},{5,27},{6,28},{7,29},{8,22},{9,... | collective-permute-start | bytes 589832 | tf_op jit(solution)/shard_map/ppermute | solution.py:34
  47.6 5.2 %collective-permute-done.14 = bf16[1,128,768]{2,1,0:T(8,128)(2,1)S(1)} collective-permute-done((bf16[1,128,768]{2,1,0:T(8,128)(2,1)S(1)}, bf16[1,128,768]{2,1,0:T(8,128)(2,1)S(1)}, u32[]{:S(2)}, u32[]{:S(2)}) %collective-permute-start.14) | collective-permute-done | bytes 196640 | tf_op jit(solution)/shard_map/ppermute | solution.py:34
  52.7 3.6 %collective-permute-done.15 = bf16[1,128,768]{2,1,0:T(8,128)(2,1)S(1)} collective-permute-done((bf16[1,128,768]{2,1,0:T(8,128)(2,1)S(1)}, bf16[1,128,768]{2,1,0:T(8,128)(2,1)S(1)}, u32[]{:S(2)}, u32[]{:S(2)}) %collective-permute-start.15) | collective-permute-done | bytes 196640 | tf_op jit(solution)/shard_map/ppermute | solution.py:34
  56.4 2.9 %collective-permute-start.16 = (bf16[4,128,768]{2,1,0:T(8,128)(2,1)S(1)}, bf16[4,128,768]{2,1,0:T(8,128)(2,1)S(1)}, u32[]{:S(2)}, u32[]{:S(2)}) collective-permute-start(bf16[4,128,768]{2,1,0:T(8,128)(2,1)S(1)} %constant_dynamic-update-slice_fusion.refs_0_), channel_id=1, source_target_pairs={{0,6},{1,7},{2,0},{3,1},{4,2},{5,3},{6,4},{7,5},{8,14},{9,15},{10,... | collective-permute-start | bytes 2359304 | tf_op jit(solution)/shard_map/ppermute | solution.py:34
  59.3 2.0 %collective-permute-done.17.refs_3_.refs_1_ = bf16[4,128,768]{2,1,0:T(8,128)(2,1)S(1)} collective-permute-done((bf16[4,128,768]{2,1,0:T(8,128)(2,1)S(1)}, bf16[4,128,768]{2,1,0:T(8,128)(2,1)S(1)}, u32[]{:S(2)}, u32[]{:S(2)}) %collective-permute-start.17) | collective-permute-done | bytes 786464 | tf_op jit(solution)/shard_map/ppermute | solution.py:34
  64.6 11.1 %collective-permute-done.16.refs_1_ = bf16[4,128,768]{2,1,0:T(8,128)(2,1)S(1)} collective-permute-done((bf16[4,128,768]{2,1,0:T(8,128)(2,1)S(1)}, bf16[4,128,768]{2,1,0:T(8,128)(2,1)S(1)}, u32[]{:S(2)}, u32[]{:S(2)}) %collective-permute-start.16) | collective-permute-done | bytes 786464 | tf_op jit(solution)/shard_map/ppermute | solution.py:34
  77.1 1.9 %collective-permute-done.23.refs_9_.refs_7_ = bf16[4,128,768]{2,1,0:T(8,128)(2,1)S(1)} collective-permute-done((bf16[4,128,768]{2,1,0:T(8,128)(2,1)S(1)}, bf16[4,128,768]{2,1,0:T(8,128)(2,1)S(1)}, u32[]{:S(2)}, u32[]{:S(2)}) %collective-permute-start.23) | collective-permute-done | bytes 786464 | tf_op jit(solution)/shard_map/ppermute | solution.py:34
  78.9 1.8 %pair_blocks.1 = (bf16[1024,128]{1,0:T(8,128)(2,1)S(1)}, bf16[1024,128]{1,0:T(8,128)(2,1)S(1)}) custom-call(bf16[4,128,768]{2,1,0:T(8,128)(2,1)S(1)} %constant_dynamic-update-slice_fusion.refs_0_, bf16[4,128,768]{2,1,0:T(8,128)(2,1)S(1)} %collective-permute-done.16.refs_1_, bf16[4,128,768]{2,1,0:T(8,128)(2,1)S(1)} %get-tuple-element.20.refs_2_.refs_0_, ...), custom_call_target="tpu_custom_call" | custom-call | tf_op jit(solution)/shard_map/pair_blocks/pallas_call | solution.py:168
  83.1 8.2 %collective-permute-done.24 = bf16[1024,128]{1,0:T(8,128)(2,1)S(1)} collective-permute-done((bf16[1024,128]{1,0:T(8,128)(2,1)S(1)}, bf16[1024,128]{1,0:T(8,128)(2,1)S(1)}, u32[]{:S(2)}, u32[]{:S(2)}) %collective-permute-start.24) | collective-permute-done | bytes 262176 | tf_op jit(solution)/shard_map/ppermute | solution.py:34
  91.6 4.1 %collective-permute-start.29 = (bf16[1024,128]{1,0:T(8,128)(2,1)S(1)}, bf16[1024,128]{1,0:T(8,128)(2,1)S(1)}, u32[]{:S(2)}, u32[]{:S(2)}) collective-permute-start(bf16[1024,128]{1,0:T(8,128)(2,1)S(1)} %get-tuple-element.25), channel_id=1, source_target_pairs={{0,24},{1,25},{2,26},{3,27},{4,28},{5,29},{8,16},{9,17},{10,18},{1... | collective-permute-start | bytes 786440 | tf_op jit(solution)/shard_map/ppermute | solution.py:34
  95.7 1.9 %collective-permute-start.28 = (bf16[1024,128]{1,0:T(8,128)(2,1)S(1)}, bf16[1024,128]{1,0:T(8,128)(2,1)S(1)}, u32[]{:S(2)}, u32[]{:S(2)}) collective-permute-start(bf16[1024,128]{1,0:T(8,128)(2,1)S(1)} %get-tuple-element.26), channel_id=1, source_target_pairs={{0,16},{1,9},{2,18},{5,13},{6,22},{7,15},{8,24},{10,26},{11,3},{12... | collective-permute-start | bytes 786440 | tf_op jit(solution)/shard_map/ppermute | solution.py:34
  98.9 2.4 %collective-permute-done.29.refs_3_ = bf16[1024,128]{1,0:T(8,128)(2,1)S(1)} collective-permute-done((bf16[1024,128]{1,0:T(8,128)(2,1)S(1)}, bf16[1024,128]{1,0:T(8,128)(2,1)S(1)}, u32[]{:S(2)}, u32[]{:S(2)}) %collective-permute-start.29) | collective-permute-done | bytes 262176 | tf_op jit(solution)/shard_map/ppermute | solution.py:34
  101.3 4.7 %collective-permute-done.28.refs_2_ = bf16[1024,128]{1,0:T(8,128)(2,1)S(1)} collective-permute-done((bf16[1024,128]{1,0:T(8,128)(2,1)S(1)}, bf16[1024,128]{1,0:T(8,128)(2,1)S(1)}, u32[]{:S(2)}, u32[]{:S(2)}) %collective-permute-start.28) | collective-permute-done | bytes 262176 | tf_op jit(solution)/shard_map/ppermute | solution.py:34
  106.0 2.2 %collective-permute-done.27.refs_1_ = bf16[1024,128]{1,0:T(8,128)(2,1)S(1)} collective-permute-done((bf16[1024,128]{1,0:T(8,128)(2,1)S(1)}, bf16[1024,128]{1,0:T(8,128)(2,1)S(1)}, u32[]{:S(2)}, u32[]{:S(2)}) %collective-permute-start.27) | collective-permute-done | bytes 262176 | tf_op jit(solution)/shard_map/ppermute | solution.py:34
  108.3 1.5 %place_blocks.1 = f32[1024,512]{1,0:T(8,128)} custom-call(bf16[1024,128]{1,0:T(8,128)(2,1)S(1)} %get-tuple-element.28.refs_0_, bf16[1024,128]{1,0:T(8,128)(2,1)S(1)} %collective-permute-done.27.refs_1_, bf16[1024,128]{1,0:T(8,128)(2,1)S(1)} %collective-permute-done.28.refs_2_, bf16[1024,128]{1,0:T(8,128)(2,1)S(1)} %collective-permute-done.29.refs_3_, ...), custom_call_target="tpu_custom_call" | custom-call | tf_op jit(solution)/shard_map/place_blocks/pallas_call | solution.py:274
  (71 shorter events, 20.6 us)
Async XLA Ops:
  4.3 7.9 %collective-permute-start.3 = (bf16[1,128,384]{2,1,0:T(8,128)(2,1)S(1)}, bf16[1,128,384]{2,1,0:T(8,128)(2,1)S(1)}, u32[]{:S(2)}, u32[]{:S(2)}) collective-permute-start(bf16[1,128,384]{2,1,0:T(8,128)(2,1)S(1)} %constant_dynamic-slice_fusion), channel_id=1, source_target_pairs={{0,4},{1,5},{2,6},{3,7},{4,0},{5,1},{6,2},{7,3},{8,12},{9,13},{10,... | collective-permute-start | bytes 294920 | tf_op jit(solution)/shard_map/ppermute | solution.py:34
  4.3 7.9 %collective-permute-start.2 = (bf16[1,128,384]{2,1,0:T(8,128)(2,1)S(1)}, bf16[1,128,384]{2,1,0:T(8,128)(2,1)S(1)}, u32[]{:S(2)}, u32[]{:S(2)}) collective-permute-start(bf16[1,128,384]{2,1,0:T(8,128)(2,1)S(1)} %constant_dynamic-slice_fusion), channel_id=1, source_target_pairs={{0,2},{1,3},{2,0},{3,1},{4,6},{5,7},{6,4},{7,5},{8,10},{9,11},{10,... | collective-permute-start | bytes 294920 | tf_op jit(solution)/shard_map/ppermute | solution.py:34
  4.7 10.3 %collective-permute-start = (bf16[4,128,384]{2,1,0:T(8,128)(2,1)}, bf16[4,128,384]{2,1,0:T(8,128)(2,1)S(1)}, u32[]{:S(2)}, u32[]{:S(2)}) collective-permute-start(bf16[4,128,384]{2,1,0:T(8,128)(2,1)} %bitcast.3), channel_id=1, source_target_pairs={{0,1},{1,0},{2,3},{3,2},{4,5},{5,4},{6,7},{7,6},{8,9},{9,8},{10,11... | collective-permute-start | bytes 1179656 | tf_op jit(solution)/shard_map/ppermute | solution.py:34
  12.2 8.2 %collective-permute-start.10 = (bf16[3,128,384]{2,1,0:T(8,128)(2,1)S(1)}, bf16[3,128,384]{2,1,0:T(8,128)(2,1)S(1)}, u32[]{:S(2)}, u32[]{:S(2)}) collective-permute-start(bf16[3,128,384]{2,1,0:T(8,128)(2,1)S(1)} %pad_maximum_fusion.refs_2_), channel_id=1, source_target_pairs={{0,24},{1,25},{2,26},{3,27},{4,28},{5,29},{6,30},{7,31},{8,16},{9,... | collective-permute-start | bytes 884744 | tf_op jit(solution)/shard_map/ppermute | solution.py:34
  13.4 15.0 %collective-permute-start.8 = (bf16[3,128,384]{2,1,0:T(8,128)(2,1)S(1)}, bf16[3,128,384]{2,1,0:T(8,128)(2,1)S(1)}, u32[]{:S(2)}, u32[]{:S(2)}) collective-permute-start(bf16[3,128,384]{2,1,0:T(8,128)(2,1)S(1)} %pad_maximum_fusion.refs_2_), channel_id=1, source_target_pairs={{0,16},{1,17},{2,18},{3,19},{4,20},{5,21},{6,22},{7,23},{8,24},{9,... | collective-permute-start | bytes 884744 | tf_op jit(solution)/shard_map/ppermute | solution.py:34
  14.7 14.3 %collective-permute-start.6 = (bf16[3,128,384]{2,1,0:T(8,128)(2,1)S(1)}, bf16[3,128,384]{2,1,0:T(8,128)(2,1)S(1)}, u32[]{:S(2)}, u32[]{:S(2)}) collective-permute-start(bf16[3,128,384]{2,1,0:T(8,128)(2,1)S(1)} %pad_maximum_fusion.refs_2_), channel_id=1, source_target_pairs={{0,8},{1,9},{2,10},{3,11},{4,12},{5,13},{6,14},{7,15},{8,0},{9,1},... | collective-permute-start | bytes 884744 | tf_op jit(solution)/shard_map/ppermute | solution.py:34
  14.9 15.6 %collective-permute-start.1 = (bf16[4,128,384]{2,1,0:T(8,128)(2,1)S(1)}, bf16[4,128,384]{2,1,0:T(8,128)(2,1)S(1)}, u32[]{:S(2)}, u32[]{:S(2)}) collective-permute-start(bf16[4,128,384]{2,1,0:T(8,128)(2,1)S(1)} %collective-permute-done.refs_1_), channel_id=1, source_target_pairs={{0,1},{1,0},{2,3},{3,2},{4,5},{5,4},{6,7},{7,6},{8,9},{9,8},{10,11... | collective-permute-start | bytes 1179656 | tf_op jit(solution)/shard_map/ppermute | solution.py:34
  17.1 11.8 %collective-permute-start.5 = (bf16[3,128,384]{2,1,0:T(8,128)(2,1)S(1)}, bf16[3,128,384]{2,1,0:T(8,128)(2,1)S(1)}, u32[]{:S(2)}, u32[]{:S(2)}) collective-permute-start(bf16[3,128,384]{2,1,0:T(8,128)(2,1)S(1)} %pad_maximum_fusion.refs_2_), channel_id=1, source_target_pairs={{0,1},{1,0},{2,3},{3,2},{4,5},{5,4},{6,7},{7,6},{8,9},{9,8},{10,11... | collective-permute-start | bytes 884744 | tf_op jit(solution)/shard_map/ppermute | solution.py:34
  20.4 8.6 %collective-permute-start.11 = (bf16[3,128,384]{2,1,0:T(8,128)(2,1)S(1)}, bf16[3,128,384]{2,1,0:T(8,128)(2,1)S(1)}, u32[]{:S(2)}, u32[]{:S(2)}) collective-permute-start(bf16[3,128,384]{2,1,0:T(8,128)(2,1)S(1)} %collective-permute-done.10.refs_8_), channel_id=1, source_target_pairs={{0,1},{1,0},{2,3},{3,2},{4,5},{5,4},{6,7},{7,6},{8,9},{9,8},{10,11... | collective-permute-start | bytes 884744 | tf_op jit(solution)/shard_map/ppermute | solution.py:34
  36.1 25.1 %collective-permute-start.17 = (bf16[4,128,768]{2,1,0:T(8,128)(2,1)S(1)}, bf16[4,128,768]{2,1,0:T(8,128)(2,1)S(1)}, u32[]{:S(2)}, u32[]{:S(2)}) collective-permute-start(bf16[4,128,768]{2,1,0:T(8,128)(2,1)S(1)} %get-tuple-element.20.refs_2_.refs_0_), channel_id=1, source_target_pairs={{0,8},{1,17},{2,10},{3,19},{4,12},{5,21},{6,14},{7,23},{8,0},{9,25... | collective-permute-start | bytes 2359304 | tf_op jit(solution)/shard_map/ppermute | solution.py:34
  36.2 6.6 %collective-permute-start.12 = (bf16[1,128,768]{2,1,0:T(8,128)(2,1)S(1)}, bf16[1,128,768]{2,1,0:T(8,128)(2,1)S(1)}, u32[]{:S(2)}, u32[]{:S(2)}) collective-permute-start(bf16[1,128,768]{2,1,0:T(8,128)(2,1)S(1)} %get-tuple-element.16), channel_id=1, source_target_pairs={{0,6},{1,7},{2,0},{3,1},{4,2},{5,3},{6,4},{7,5},{8,14},{9,15},{10,... | collective-permute-start | bytes 589832 | tf_op jit(solution)/shard_map/ppermute | solution.py:34
  38.1 9.5 %collective-permute-start.13 = (bf16[1,128,768]{2,1,0:T(8,128)(2,1)S(1)}, bf16[1,128,768]{2,1,0:T(8,128)(2,1)S(1)}, u32[]{:S(2)}, u32[]{:S(2)}) collective-permute-start(bf16[1,128,768]{2,1,0:T(8,128)(2,1)S(1)} %get-tuple-element.17), channel_id=1, source_target_pairs={{0,14},{1,15},{2,8},{3,9},{4,10},{5,11},{6,12},{7,13},{8,6},{9,7},... | collective-permute-start | bytes 589832 | tf_op jit(solution)/shard_map/ppermute | solution.py:34
  38.5 24.6 %collective-permute-start.18 = (bf16[4,128,768]{2,1,0:T(8,128)(2,1)S(1)}, bf16[4,128,768]{2,1,0:T(8,128)(2,1)S(1)}, u32[]{:S(2)}, u32[]{:S(2)}) collective-permute-start(bf16[4,128,768]{2,1,0:T(8,128)(2,1)S(1)} %get-tuple-element.20.refs_2_.refs_0_), channel_id=1, source_target_pairs={{0,16},{1,9},{2,18},{3,11},{4,20},{5,13},{6,22},{7,15},{8,24},{9,1... | collective-permute-start | bytes 2359304 | tf_op jit(solution)/shard_map/ppermute | solution.py:34
  39.3 13.4 %collective-permute-start.14 = (bf16[1,128,768]{2,1,0:T(8,128)(2,1)S(1)}, bf16[1,128,768]{2,1,0:T(8,128)(2,1)S(1)}, u32[]{:S(2)}, u32[]{:S(2)}) collective-permute-start(bf16[1,128,768]{2,1,0:T(8,128)(2,1)S(1)} %get-tuple-element.18), channel_id=1, source_target_pairs={{0,22},{1,23},{2,16},{3,17},{4,18},{5,19},{6,20},{7,21},{8,30},{9,... | collective-permute-start | bytes 589832 | tf_op jit(solution)/shard_map/ppermute | solution.py:34
  42.8 13.5 %collective-permute-start.15 = (bf16[1,128,768]{2,1,0:T(8,128)(2,1)S(1)}, bf16[1,128,768]{2,1,0:T(8,128)(2,1)S(1)}, u32[]{:S(2)}, u32[]{:S(2)}) collective-permute-start(bf16[1,128,768]{2,1,0:T(8,128)(2,1)S(1)} %get-tuple-element.19), channel_id=1, source_target_pairs={{0,30},{1,31},{2,24},{3,25},{4,26},{5,27},{6,28},{7,29},{8,22},{9,... | collective-permute-start | bytes 589832 | tf_op jit(solution)/shard_map/ppermute | solution.py:34
  56.4 19.3 %collective-permute-start.16 = (bf16[4,128,768]{2,1,0:T(8,128)(2,1)S(1)}, bf16[4,128,768]{2,1,0:T(8,128)(2,1)S(1)}, u32[]{:S(2)}, u32[]{:S(2)}) collective-permute-start(bf16[4,128,768]{2,1,0:T(8,128)(2,1)S(1)} %constant_dynamic-update-slice_fusion.refs_0_), channel_id=1, source_target_pairs={{0,6},{1,7},{2,0},{3,1},{4,2},{5,3},{6,4},{7,5},{8,14},{9,15},{10,... | collective-permute-start | bytes 2359304 | tf_op jit(solution)/shard_map/ppermute | solution.py:34
  61.2 14.5 %collective-permute-start.19 = (bf16[4,128,768]{2,1,0:T(8,128)(2,1)S(1)}, bf16[4,128,768]{2,1,0:T(8,128)(2,1)S(1)}, u32[]{:S(2)}, u32[]{:S(2)}) collective-permute-start(bf16[4,128,768]{2,1,0:T(8,128)(2,1)S(1)} %collective-permute-done.17.refs_3_.refs_1_), channel_id=1, source_target_pairs={{0,16},{1,9},{2,18},{3,11},{4,20},{5,13},{6,22},{7,15},{8,24},{9,1... | collective-permute-start | bytes 2359304 | tf_op jit(solution)/shard_map/ppermute | solution.py:34
  61.9 15.1 %collective-permute-start.20 = (bf16[4,128,768]{2,1,0:T(8,128)(2,1)S(1)}, bf16[4,128,768]{2,1,0:T(8,128)(2,1)S(1)}, u32[]{:S(2)}, u32[]{:S(2)}) collective-permute-start(bf16[4,128,768]{2,1,0:T(8,128)(2,1)S(1)} %get-tuple-element.20.refs_2_.refs_0_), channel_id=1, source_target_pairs={{0,1},{1,0},{2,3},{3,2},{4,5},{5,4},{6,7},{7,6},{8,9},{9,8},{10,11... | collective-permute-start | bytes 2359304 | tf_op jit(solution)/shard_map/ppermute | solution.py:34
  62.1 15.0 %collective-permute-start.21 = (bf16[4,128,768]{2,1,0:T(8,128)(2,1)S(1)}, bf16[4,128,768]{2,1,0:T(8,128)(2,1)S(1)}, u32[]{:S(2)}, u32[]{:S(2)}) collective-permute-start(bf16[4,128,768]{2,1,0:T(8,128)(2,1)S(1)} %collective-permute-done.17.refs_3_.refs_1_), channel_id=1, source_target_pairs={{0,1},{1,0},{2,3},{3,2},{4,5},{5,4},{6,7},{7,6},{8,9},{9,8},{10,11... | collective-permute-start | bytes 2359304 | tf_op jit(solution)/shard_map/ppermute | solution.py:34
  63.1 13.9 %collective-permute-start.22 = (bf16[4,128,768]{2,1,0:T(8,128)(2,1)S(1)}, bf16[4,128,768]{2,1,0:T(8,128)(2,1)S(1)}, u32[]{:S(2)}, u32[]{:S(2)}) collective-permute-start(bf16[4,128,768]{2,1,0:T(8,128)(2,1)S(1)} %collective-permute-done.18.refs_4_.refs_2_), channel_id=1, source_target_pairs={{0,1},{1,0},{2,3},{3,2},{4,5},{5,4},{6,7},{7,6},{8,9},{9,8},{10,11... | collective-permute-start | bytes 2359304 | tf_op jit(solution)/shard_map/ppermute | solution.py:34
  80.9 10.4 %collective-permute-start.24 = (bf16[1024,128]{1,0:T(8,128)(2,1)S(1)}, bf16[1024,128]{1,0:T(8,128)(2,1)S(1)}, u32[]{:S(2)}, u32[]{:S(2)}) collective-permute-start(bf16[1024,128]{1,0:T(8,128)(2,1)S(1)} %get-tuple-element.22), channel_id=1, source_target_pairs={{0,2},{1,3},{2,4},{3,5},{4,6},{5,7},{6,0},{7,1},{8,10},{9,11},{10,... | collective-permute-start | bytes 786440 | tf_op jit(solution)/shard_map/ppermute | solution.py:34
  91.6 9.7 %collective-permute-start.29 = (bf16[1024,128]{1,0:T(8,128)(2,1)S(1)}, bf16[1024,128]{1,0:T(8,128)(2,1)S(1)}, u32[]{:S(2)}, u32[]{:S(2)}) collective-permute-start(bf16[1024,128]{1,0:T(8,128)(2,1)S(1)} %get-tuple-element.25), channel_id=1, source_target_pairs={{0,24},{1,25},{2,26},{3,27},{4,28},{5,29},{8,16},{9,17},{10,18},{1... | collective-permute-start | bytes 786440 | tf_op jit(solution)/shard_map/ppermute | solution.py:34
  95.7 10.3 %collective-permute-start.28 = (bf16[1024,128]{1,0:T(8,128)(2,1)S(1)}, bf16[1024,128]{1,0:T(8,128)(2,1)S(1)}, u32[]{:S(2)}, u32[]{:S(2)}) collective-permute-start(bf16[1024,128]{1,0:T(8,128)(2,1)S(1)} %get-tuple-element.26), channel_id=1, source_target_pairs={{0,16},{1,9},{2,18},{5,13},{6,22},{7,15},{8,24},{10,26},{11,3},{12... | collective-permute-start | bytes 786440 | tf_op jit(solution)/shard_map/ppermute | solution.py:34
  97.6 10.6 %collective-permute-start.27 = (bf16[1024,128]{1,0:T(8,128)(2,1)S(1)}, bf16[1024,128]{1,0:T(8,128)(2,1)S(1)}, u32[]{:S(2)}, u32[]{:S(2)}) collective-permute-start(bf16[1024,128]{1,0:T(8,128)(2,1)S(1)} %get-tuple-element.27), channel_id=1, source_target_pairs={{0,8},{1,17},{3,19},{4,12},{6,14},{7,23},{9,25},{10,2},{11,27},{12... | collective-permute-start | bytes 786440 | tf_op jit(solution)/shard_map/ppermute | solution.py:34
  (16 other events, 143.8 us)
